TPU v7x, 32 devices: a whole 2x2x4 slice. The times are simulated.
32 devices in a mesh: groups: 2 (over y), ctx: 8 (over z, core), rows: 2 (over x).
Axes of the slice: x: 2, y: 2, z: 4, core: 2. Of those that a mesh axis runs over, the one named last changes fastest.
Arguments:
- queries: bfloat16 [64, 4, 8192], P(('groups', 'ctx'), None, 'rows'), parts along dimension 0, may hold values from -34 to 34
- selected: int32 [64, 4, 16], P(('groups', 'ctx')), parts along dimension 0, may hold values from 0 to 31, all different within a row; in each aligned block of 16 rows (0 to 15, 16 to 31, ..., all dimensions but the last counted through in order) at most 16 rows name the same one
- placement: int32 [64], P('groups'), parts along dimension 0, may hold values from 0 to 31, each once
- lengths: int32 [64], P(('groups', 'ctx')), parts along dimension 0, may hold values from 1 to 125, as said below
- cache_k: bfloat16 [64, 1024, 1024], P(('groups', 'ctx'), None, 'rows'), parts along dimension 0, may hold values from -10 to 10
- cache_v: bfloat16 [64, 1024, 1024], P(('groups', 'ctx'), None, 'rows'), parts along dimension 0, may hold values from -12 to 12
- suffix_k: bfloat16 [64, 128, 1024], P(('groups', 'ctx'), None, 'rows'), parts along dimension 0, may hold values from -12 to 12
- suffix_v: bfloat16 [64, 128, 1024], P(('groups', 'ctx'), None, 'rows'), parts along dimension 0, may hold values from -12 to 12
Outputs:
- attended: bfloat16 [64, 4, 8192], P(('groups', 'ctx'), None, 'rows'), parts along dimension 0
There are 2 independent parts, one for each index of `groups`. A program takes and returns all parts, laid end to end along the dimension named above; each array names one. Nothing has to cross between parts.
Inputs may be any that keep to these rules, and one draw needn't show every extreme that they name: `selected`: each row and step lists 16 different block ids. Over the 4 rows of one device and all 4 steps together no block id is listed more than 16 times, and some block id is listed exactly 16 times. A permutation: block id b is stored at cache index placement[b]. At step t the first lengths[r] + t suffix slots of row r are valid; some row has exactly 125.
All inputs are finite; a program needn't handle non-finite values.
Results may differ from a plain program's by a relative error of at most 0.0041.
Values may be sent and summed in bfloat16 or wider, within the bound.
No kernel may reach another device: no remote copies, remote signals or barrier semaphores. Data moves between devices by JAX's collectives and lax.ppermute only.
A program may use at most 64 MiB of HBM per device.

v0:
```python
import math

import jax
import jax.numpy as jnp
from jax import lax
from jax.sharding import PartitionSpec as P

HD = 128


def block_positions(chosen, placement):
    block_ids = jnp.arange(placement.shape[0], dtype=jnp.int32)
    matches = chosen[..., None] == block_ids
    return jnp.sum(jnp.where(matches, placement, 0), axis=-1)


def hits_ranks(positions, targets):
    present = jnp.sum((positions[:, :, None] == targets[None, None, :]).astype(jnp.int32), axis=1)
    before = jnp.cumsum(present, axis=0) - present
    return (present, before)


def dispatch_from(present, before, capacity):
    slot_ids = jnp.arange(capacity, dtype=jnp.int32)
    picked = (present[:, :, None] == 1) & (before[:, :, None] == slot_ids[None, None, :])
    return jnp.transpose(picked, (1, 2, 0)).astype(jnp.bfloat16)


def attend_block(block_queries, block_keys, block_values, kv_here):
    item_count = block_queries.shape[0]
    score_scale = 1.0 / math.sqrt(HD)
    grouped = block_queries.reshape(item_count, kv_here, -1, HD)
    outputs = []
    log_sums = []
    for head_group in range(kv_here):
        keys_now = block_keys[:, head_group * HD : (head_group + 1) * HD]
        values_now = block_values[:, head_group * HD : (head_group + 1) * HD]
        scores = (
            jnp.einsum(
                "nhd,td->nht", grouped[:, head_group], keys_now, preferred_element_type=jnp.float32
            )
            * score_scale
        )
        highest = jnp.max(scores, axis=-1, keepdims=True)
        exponent = jnp.exp(scores - highest)
        totals = jnp.sum(exponent, axis=-1, keepdims=True)
        weighted = (
            jnp.einsum(
                "nht,td->nhd",
                exponent.astype(jnp.bfloat16),
                values_now,
                preferred_element_type=jnp.float32,
            )
            / totals
        )
        outputs.append(weighted.astype(jnp.bfloat16))
        log_sums.append((highest + jnp.log(totals))[..., 0])
    return (
        jnp.stack(outputs, axis=1).reshape(item_count, -1),
        jnp.stack(log_sums, axis=1).reshape(item_count, -1),
    )


def local(queries, selected, placement, lengths, cache_k, cache_v, suffix_k, suffix_v):
    rows_here, steps, width = queries.shape
    listed = selected.shape[2]
    ctx_devices = lax.axis_size("ctx")
    blocks_here = cache_k.shape[0]
    kv_here = cache_k.shape[2] // HD
    heads_here = width // HD
    group_size = heads_here // kv_here
    total_blocks = placement.shape[0]
    items = rows_here * steps
    capacity = min(items, 2 * ((items * listed + total_blocks - 1) // total_blocks))
    every_position = jnp.arange(total_blocks, dtype=jnp.int32)
    all_queries = lax.all_gather(queries, "ctx", axis=0, tiled=True)
    all_selected = lax.all_gather(selected, "ctx", axis=0, tiled=True)
    all_positions = block_positions(all_selected.reshape(ctx_devices, items, listed), placement)
    own_index = lax.axis_index("ctx")
    positions = lax.dynamic_index_in_dim(all_positions, own_index, 0, keepdims=False)
    local_targets = own_index * blocks_here + jnp.arange(blocks_here, dtype=jnp.int32)

    def local_dispatch(source_positions):
        source_present, source_before = hits_ranks(source_positions, local_targets)
        return dispatch_from(source_present, source_before, capacity)

    dispatch = jax.vmap(local_dispatch)(all_positions)
    received = jnp.einsum(
        "sbcm,smw->sbcw",
        dispatch,
        all_queries.reshape(ctx_devices, items, width),
        preferred_element_type=jnp.float32,
    ).astype(jnp.bfloat16)
    present, before = hits_ranks(positions, every_position)
    block_outputs = []
    block_logs = []
    for slot_index in range(blocks_here):
        outputs, log_sums = attend_block(
            received[:, slot_index].reshape(ctx_devices * capacity, width),
            cache_k[slot_index],
            cache_v[slot_index],
            kv_here,
        )
        block_outputs.append(outputs.reshape(ctx_devices, capacity, width))
        block_logs.append(log_sums.reshape(ctx_devices, capacity, heads_here))
    partial_out = jnp.stack(block_outputs, axis=1).reshape(
        ctx_devices, blocks_here * capacity, width
    )
    partial_log = jnp.stack(block_logs, axis=1).reshape(
        ctx_devices, blocks_here * capacity, heads_here
    )
    returned_out, returned_log = (
        lax.all_to_all(
            partial_out.astype(jnp.float32), "ctx", split_axis=0, concat_axis=0, tiled=True
        ).astype(partial_out.dtype),
        lax.all_to_all(partial_log, "ctx", split_axis=0, concat_axis=0, tiled=True),
    )
    slot_of = jnp.sum(
        jnp.where(positions[:, :, None] == every_position[None, None, :], before[:, None, :], 0),
        axis=-1,
    )
    flat_target = (positions * capacity + slot_of).reshape(-1)
    collect = flat_target[:, None] == jnp.arange(total_blocks * capacity, dtype=jnp.int32)[None, :]
    picked_out = jnp.dot(
        collect.astype(jnp.bfloat16),
        returned_out.reshape(total_blocks * capacity, width),
        preferred_element_type=jnp.float32,
    )
    picked_log = jnp.dot(
        collect.astype(jnp.float32),
        returned_log.reshape(total_blocks * capacity, heads_here),
        precision=lax.Precision.HIGHEST,
    )
    score_scale = 1.0 / math.sqrt(HD)
    suffix_len = suffix_k.shape[1]
    query_heads = queries.reshape(rows_here, steps, kv_here, group_size, HD)
    key_heads = suffix_k.reshape(rows_here, suffix_len, kv_here, HD)
    value_heads = suffix_v.reshape(rows_here, suffix_len, kv_here, HD)
    scores = (
        jnp.einsum("rsghd,rtgd->rsght", query_heads, key_heads, preferred_element_type=jnp.float32)
        * score_scale
    )
    limits = lengths[:, None] + jnp.arange(steps, dtype=jnp.int32)[None, :]
    visible = jnp.arange(suffix_len, dtype=jnp.int32)[None, None, :] < limits[:, :, None]
    scores = jnp.where(visible[:, :, None, None, :], scores, -jnp.inf)
    highest = jnp.max(scores, axis=-1, keepdims=True)
    exponent = jnp.exp(scores - highest)
    totals = jnp.sum(exponent, axis=-1, keepdims=True)
    suffix_out = (
        jnp.einsum(
            "rsght,rtgd->rsghd",
            exponent.astype(jnp.bfloat16),
            value_heads,
            preferred_element_type=jnp.float32,
        )
        / totals
    )
    suffix_log = (highest + jnp.log(totals))[..., 0]
    parts_out = jnp.concatenate(
        [
            picked_out.reshape(items, listed, heads_here, HD),
            suffix_out.reshape(items, 1, heads_here, HD),
        ],
        axis=1,
    )
    parts_log = jnp.concatenate(
        [picked_log.reshape(items, listed, heads_here), suffix_log.reshape(items, 1, heads_here)],
        axis=1,
    )
    largest = jnp.max(parts_log, axis=1, keepdims=True)
    factors = jnp.exp(parts_log - largest)
    merged = jnp.sum(factors[..., None] * parts_out, axis=1) / jnp.sum(factors, axis=1)[..., None]
    return merged.reshape(rows_here, steps, width).astype(jnp.bfloat16)


def solution(mesh):
    in_specs = (
        P(("groups", "ctx"), None, "rows"),
        P(("groups", "ctx"), None, None),
        P("groups"),
        P(("groups", "ctx")),
        P(("groups", "ctx"), None, "rows"),
        P(("groups", "ctx"), None, "rows"),
        P(("groups", "ctx"), None, "rows"),
        P(("groups", "ctx"), None, "rows"),
    )
    out_specs = P(("groups", "ctx"), None, "rows")
    return jax.shard_map(local, mesh=mesh, in_specs=in_specs, out_specs=out_specs, check_vma=False)
```

profile of v0, /device:TPU:0, one launch (start us, length us, event | category | flops | bytes accessed | tf_op | source)
XLA Modules:
  0.0 230.9 jit_solution(889467690205915180)
XLA Ops:
  7.3 15.9 %all_gather.6 = s32[32,4,16]{2,1,0:T(4,128)S(1)} all-gather(s32[4,4,16]{2,1,0:T(4,128)} %param.9), channel_id=1, replica_groups=mesh['groups'=2,'ctx'=8,'rows'=2] {'ctx'}, dimensions={0}, use_global_device_ids=true | all-gather | bytes 9216 | tf_op jit(solution)/shard_map/all_gather | solution.py:77
  23.1 3.2 %select_reduce_fusion = s32[8,16,16]{2,1,0:T(8,128)S(1)} fusion(s32[32]{0:T(128)} %param.10, s32[8,16,16]{2,1,0:T(8,128)S(1)} %bitcast.391), kind=kLoop, calls=%fused_computation.184 | loop fusion | flops 194560 | bytes 16512 | tf_op jit(solution)/shard_map/reduce_sum | solution.py:14
  28.0 4.0 %slice_bitcast_fusion.7 = (bf16[1024,512]{1,0:T(8,128)(2,1)S(1)}, bf16[1024,512]{1,0:T(8,128)(2,1)S(1)}, bf16[1024,512]{1,0:T(8,128)(2,1)}, bf16[1024,512]{1,0:T(8,128)(2,1)}) fusion(bf16[4,1024,512]{2,1,0:T(8,128)(2,1)} %param.12), kind=kLoop, calls=%fused_computation.183 | loop fusion | bytes 8388608 | tf_op jit(solution)/shard_map/squeeze | solution.py:100
  32.0 2.1 slice_bitcast_fusion.3
  34.1 1.9 reshape.555
  54.2 1.6 fusion.196
  57.6 1.6 fusion.187
  60.9 1.6 fusion.178
  65.6 1.6 fusion.169
  68.2 1.6 fusion.160
  71.5 1.6 fusion.151
  74.8 1.6 fusion.142
  79.4 1.6 fusion.133
  82.3 1.6 fusion.124
  85.7 1.6 fusion.115
  101.4 4.9 %all-to-all-start = ((f32[8,1,2048]{2,1,0:T(1,128)}), f32[8,1,2048]{2,1,0:T(1,128)S(1)}, u32[]{:S(2)}, u32[]{:S(2)}) async-start(f32[8,1,2048]{2,1,0:T(1,128)} %reshape.595), calls=%async_computation | async-start | bytes 131072 | tf_op jit(solution)/shard_map/all_to_all | solution.py:116
  106.3 1.8 maximum_convert_fusion
  108.1 2.2 copy.166
  110.3 1.8 all-to-all-done
  112.1 4.7 %all-to-all-start.1 = ((bf16[8,64,4096]{2,1,0:T(8,128)(2,1)}), bf16[8,64,4096]{2,1,0:T(8,128)(2,1)}, u32[]{:S(2)}, u32[]{:S(2)}) async-start(bf16[8,64,4096]{2,1,0:T(8,128)(2,1)} %bitcast.375), calls=%async_computation.1 | async-start | bytes 8388608 | tf_op jit(solution)/shard_map/all_to_all | solution.py:113
  121.7 89.2 %all-to-all-done.1 = bf16[8,64,4096]{2,1,0:T(8,128)(2,1)} async-done(((bf16[8,64,4096]{2,1,0:T(8,128)(2,1)}), bf16[8,64,4096]{2,1,0:T(8,128)(2,1)}, u32[]{:S(2)}, u32[]{:S(2)}) %all-to-all-start.1) | async-done | bytes 4194336 | tf_op jit(solution)/shard_map/all_to_all | solution.py:113
  210.8 6.5 %copy.167 = bf16[4096,512]{1,0:T(8,128)(2,1)} copy(bf16[4096,512]{0,1:T(8,128)(2,1)} %bitcast.101) | data formatting | bytes 8388608 | tf_op jit(solution)/shard_map/dot_general | solution.py:124
  217.4 3.5 %fusion.252 = f32[16,16,32,128]{3,1,2,0:T(8,128)S(1)} fusion(bf16[32,128,512,1]{2,1,0,3:T(8,128)(2,1)} %bitcast.376, s32[16,16]{1,0:T(8,128)S(1)} %multiply_add_fusion), kind=kOutput, calls=%fused_computation.193 | convolution fusion | flops 1073872896 | bytes 8389632 | tf_op jit(solution)/shard_map/dot_general | solution.py:124
  220.9 2.2 fusion
  (149 shorter events, 56.8 us)
Async XLA Ops:
  6.5 27.5 %all-gather.2.cloned.1.call-start = ((), (), s32[]{:S(2)}) async-start(), calls=%async_computation.2 | async-start | bytes 1179648 | tf_op jit(solution)/shard_map/all_gather | solution.py:76
  28.0 4.0 %copy-start = (bf16[4,1024,512]{2,1,0:T(8,128)(2,1)S(1)}, bf16[4,1024,512]{2,1,0:T(8,128)(2,1)}, u32[]{:S(2)}) copy-start(bf16[4,1024,512]{2,1,0:T(8,128)(2,1)} %param.13) | copy-start | bytes 12582916
  37.7 1.2 copy-start.2
  39.7 1.7 copy-start.6
  48.4 1.4 copy-start.1
  50.7 1.7 copy-start.5
  63.7 1.9 copy-start.4
  77.7 1.7 copy-start.3
  90.5 1.3 copy-start.10
  90.5 1.4 copy-start.11
  90.5 1.4 copy-start.12
  92.7 3.8 %copy-start.13 = (bf16[128,1,8,128]{3,0,2,1:T(8,128)(2,1)S(1)}, bf16[128,1,8,128]{3,0,2,1:T(8,128)(2,1)}, u32[]{:S(2)}) copy-start(bf16[128,1,8,128]{3,0,2,1:T(8,128)(2,1)} %fusion.133) | copy-start | bytes 786436
  101.4 10.7 %all-to-all-start = ((f32[8,1,2048]{2,1,0:T(1,128)}), f32[8,1,2048]{2,1,0:T(1,128)S(1)}, u32[]{:S(2)}, u32[]{:S(2)}) async-start(f32[8,1,2048]{2,1,0:T(1,128)} %reshape.595), calls=%async_computation | async-start | bytes 131072 | tf_op jit(solution)/shard_map/all_to_all | solution.py:116
  112.1 4.7 %copy-start.9 = (bf16[4,4,4096]{2,1,0:T(4,128)(2,1)S(1)}, bf16[4,4,4096]{2,1,0:T(4,128)(2,1)}, u32[]{:S(2)}) copy-start(bf16[4,4,4096]{2,1,0:T(4,128)(2,1)} %param.8) | copy-start | bytes 393220
  112.1 4.9 %copy-start.7 = (bf16[4,128,512]{2,1,0:T(8,128)(2,1)S(1)}, bf16[4,128,512]{2,1,0:T(8,128)(2,1)}, u32[]{:S(2)}) copy-start(bf16[4,128,512]{2,1,0:T(8,128)(2,1)} %param.14) | copy-start | bytes 1572868
  112.1 5.0 %copy-start.14 = (s32[4]{0:T(128)S(1)}, s32[4]{0:T(128)}, u32[]{:S(2)}) copy-start(s32[4]{0:T(128)} %param.11) | copy-start | bytes 52
  112.1 6.2 %copy-start.8 = (bf16[4,128,512]{2,1,0:T(8,128)(2,1)S(1)}, bf16[4,128,512]{2,1,0:T(8,128)(2,1)}, u32[]{:S(2)}) copy-start(bf16[4,128,512]{2,1,0:T(8,128)(2,1)} %param.15) | copy-start | bytes 1572868
  112.1 98.7 %all-to-all-start.1 = ((bf16[8,64,4096]{2,1,0:T(8,128)(2,1)}), bf16[8,64,4096]{2,1,0:T(8,128)(2,1)}, u32[]{:S(2)}, u32[]{:S(2)}) async-start(bf16[8,64,4096]{2,1,0:T(8,128)(2,1)} %bitcast.375), calls=%async_computation.1 | async-start | bytes 8388608 | tf_op jit(solution)/shard_map/all_to_all | solution.py:113
Sparse Core Ops, SparseCore 0:
  9.0 24.7 all-gather.1
where the time goes:
time: 235 us; the launch traced here: 231 us
  waiting for transfers between devices  91.7 us (39%)
  matrix products  40.7 us (17%)
  local copies, waits for them, and re-layouts  30 us (13%)
  other arithmetic  28.8 us (12%)
  blocking collectives  15.9 us (7%)
  between operations  14.3 us (6%)
  starting transfers between devices  9.56 us (4%)
    all_to_all x1, waiting for transfers between devices, local(): lax.all_to_all(partial_out.astype(jnp.float32), 'ctx', split_axis=0, conc...  89.2 us
    dot_general x16, matrix products, attend_block(): jnp.einsum('nht,td->nhd', exponent.astype(jnp.bfloat16), values_now, pref...  22 us
    all_gather x1, blocking collectives, local(): all_selected = lax.all_gather(selected, 'ctx', axis=0, tiled=True)  15.9 us
    reduce_sum x16, other arithmetic, attend_block(): totals = jnp.sum(exponent, axis=-1, keepdims=True)  15.3 us
    dot_general x16, matrix products, attend_block(): jnp.einsum('nhd,td->nht', grouped[:, head_group], keys_now, preferred_ele...  12.7 us
    dot_general x1, local copies, waits for them, and re-layouts, local(): jnp.dot(collect.astype(jnp.bfloat16), returned_out.reshape(total_blocks *...  6.54 us
    all_to_all x1, starting transfers between devices, local(): lax.all_to_all(partial_log, 'ctx', split_axis=0, concat_axis=0, tiled=True)  4.87 us
  transfers between devices with their start and end apart: 3, of which 2 were waited for; matrix products, arithmetic and copies ran while one was open for 9% of the time, Pallas kernels for 0%

commit v1 on v0

v1 whole, which is shorter than its diff:
```python
import functools
import math

import jax
import jax.numpy as jnp
from jax import lax
from jax.experimental import pallas as pl
from jax.experimental.pallas import tpu as pltpu
from jax.sharding import PartitionSpec as P

HD = 128
LANES = 128
SCALE = 1.0 / math.sqrt(HD)
LOG2E = math.log2(math.e)
NONE = -1e30
VMEM = 56 * 1024 * 1024


def split3(x):
    high = x.astype(jnp.bfloat16)
    rest = x - high.astype(jnp.float32)
    middle = rest.astype(jnp.bfloat16)
    low = (rest - middle.astype(jnp.float32)).astype(jnp.bfloat16)
    return high, middle, low


def dot_nt(a, b):
    return lax.dot_general(a, b, (((1,), (1,)), ((), ())), preferred_element_type=jnp.float32)


def block_kernel(heads_step, group_size, targets, q_ref, ids_ref, k_ref, v_ref, out_ref, logs_ref, s_ref):
    kv = pl.program_id(1)
    items = q_ref.shape[0]
    blocks = k_ref.shape[0]
    rows = heads_step * items
    lane = lax.broadcasted_iota(jnp.int32, (items, LANES), 1)
    ids = ids_ref[...].astype(jnp.float32)
    listed = []
    for b in range(blocks):
        target = targets[b].astype(jnp.float32)
        hit = jnp.max(jnp.where(ids == target, 1.0, 0.0), axis=1, keepdims=True)
        listed.append(jnp.concatenate([hit] * heads_step, axis=0))
    logs = jnp.where(kv == 0, jnp.zeros((items, LANES), jnp.float32), logs_ref[...])
    for first in range(0, group_size, heads_step):
        q = jnp.concatenate(
            [q_ref[:, h * HD : (h + 1) * HD] for h in range(first, first + heads_step)], axis=0
        )
        top = jnp.full((rows, LANES), NONE, jnp.float32)
        for b in range(blocks):
            s = dot_nt(q, k_ref[b])
            s_ref[b] = s
            here = s[:, :LANES]
            for t in range(1, s.shape[1] // LANES):
                here = jnp.maximum(here, s[:, t * LANES : (t + 1) * LANES])
            top = jnp.maximum(top, jnp.where(listed[b] > 0.0, here, NONE))
        highest = jnp.max(top, axis=1, keepdims=True)
        shift = highest * (SCALE * LOG2E)
        acc = jnp.zeros((rows, HD), jnp.float32)
        total = jnp.zeros((rows, LANES), jnp.float32)
        for b in range(blocks):
            off = jnp.where(listed[b] > 0.0, shift, -NONE)
            p = jnp.exp2(s_ref[b] * (SCALE * LOG2E) - off)
            for t in range(p.shape[1] // LANES):
                total += p[:, t * LANES : (t + 1) * LANES]
            acc += jnp.dot(p.astype(jnp.bfloat16), v_ref[b], preferred_element_type=jnp.float32)
        total = jnp.sum(total, axis=1, keepdims=True)
        some = total > 0.0
        out = jnp.where(some, acc / jnp.where(some, total, 1.0), 0.0).astype(jnp.bfloat16)
        log = jnp.where(some, highest * SCALE + jnp.log(jnp.where(some, total, 1.0)), NONE)
        for n in range(heads_step):
            head = kv * group_size + first + n
            start = pl.multiple_of(head * HD, HD)
            out_ref[:, pl.ds(start, HD)] = out[n * items : (n + 1) * items]
            logs = jnp.where(lane == head, log[n * items : (n + 1) * items], logs)
    logs_ref[...] = logs

    @pl.when(kv == pl.num_programs(1) - 1)
    def _():
        heads = (out_ref.shape[1] - LANES) // HD
        high, middle, low = split3(logs)
        parts = jnp.concatenate([high[:, :heads], middle[:, :heads], low[:, :heads]], axis=1)
        pad = jnp.zeros((items, LANES - 3 * heads), jnp.bfloat16)
        out_ref[:, heads * HD :] = jnp.concatenate([parts, pad], axis=1)


def attend_blocks(targets, payload, cache_k, cache_v, width):
    items_all = payload.shape[0]
    blocks, tokens, kv_width = cache_k.shape
    kv_here = kv_width // HD
    group_size = width // kv_width
    items = min(items_all, 128)
    heads_step = 2
    return pl.pallas_call(
        functools.partial(block_kernel, heads_step, group_size),
        grid_spec=pltpu.PrefetchScalarGridSpec(
            num_scalar_prefetch=1,
            grid=(items_all // items, kv_here),
            in_specs=[
                pl.BlockSpec((items, group_size * HD), lambda i, g, t: (i, g)),
                pl.BlockSpec((items, LANES), lambda i, g, t: (i, width // LANES)),
                pl.BlockSpec((blocks, tokens, HD), lambda i, g, t: (0, 0, g)),
                pl.BlockSpec((blocks, tokens, HD), lambda i, g, t: (0, 0, g)),
            ],
            out_specs=pl.BlockSpec((items, width + LANES), lambda i, g, t: (i, 0)),
            scratch_shapes=[
                pltpu.VMEM((items, LANES), jnp.float32),
                pltpu.VMEM((blocks, heads_step * items, tokens), jnp.float32),
            ],
        ),
        out_shape=jax.ShapeDtypeStruct((items_all, width + LANES), jnp.bfloat16),
        compiler_params=pltpu.CompilerParams(vmem_limit_bytes=VMEM),
        cost_estimate=pl.CostEstimate(
            flops=4 * items_all * blocks * tokens * width,
            bytes_accessed=4 * blocks * tokens * kv_width + 4 * items_all * width,
            transcendentals=items_all * blocks * tokens * width // HD,
        ),
    )(targets, payload, payload, cache_k, cache_v)


def suffix_kernel(kv_here, group_size, steps, q_ref, limit_ref, k_ref, v_ref, out_ref, log_ref):
    items = q_ref.shape[0]
    rows_here, tokens, _ = k_ref.shape
    span = rows_here * tokens
    row = group_size * items
    lane = lax.broadcasted_iota(jnp.int32, (items, LANES), 1)
    token = lax.broadcasted_iota(jnp.int32, (items, span), 1)
    item = lax.broadcasted_iota(jnp.int32, (items, span), 0)
    offset = token - (item // steps) * tokens
    seen = jnp.where((offset >= 0) & (offset < limit_ref[...]), 1.0, 0.0)
    seen = jnp.concatenate([seen] * group_size, axis=0)
    logs = jnp.zeros((items, LANES), jnp.float32)
    for g in range(kv_here):
        first = g * group_size
        q = jnp.concatenate(
            [q_ref[:, h * HD : (h + 1) * HD] for h in range(first, first + group_size)], axis=0
        )
        keys = k_ref[:, :, g * HD : (g + 1) * HD].reshape(span, HD)
        values = v_ref[:, :, g * HD : (g + 1) * HD].reshape(span, HD)
        s = jnp.where(seen > 0.0, dot_nt(q, keys), NONE)
        highest = jnp.max(s, axis=1, keepdims=True)
        p = jnp.exp2((s - highest) * (SCALE * LOG2E))
        p = jnp.where(seen > 0.0, p, 0.0)
        total = jnp.sum(p, axis=1, keepdims=True)
        out = jnp.dot(p.astype(jnp.bfloat16), values, preferred_element_type=jnp.float32) / total
        log = highest * SCALE + jnp.log(total)
        for n in range(group_size):
            h = first + n
            out_ref[:, h * HD : (h + 1) * HD] = out[n * items : (n + 1) * items]
            logs = jnp.where(lane == h, log[n * items : (n + 1) * items], logs)
    log_ref[...] = logs


def attend_suffix(queries, limits, suffix_k, suffix_v, steps):
    items, width = queries.shape
    kv_width = suffix_k.shape[2]
    return pl.pallas_call(
        functools.partial(suffix_kernel, kv_width // HD, width // kv_width, steps),
        out_shape=(
            jax.ShapeDtypeStruct((items, width), jnp.float32),
            jax.ShapeDtypeStruct((items, LANES), jnp.float32),
        ),
        compiler_params=pltpu.CompilerParams(vmem_limit_bytes=VMEM),
    )(queries, limits, suffix_k, suffix_v)


def merge_kernel(parts, items, back_ref, out_s_ref, log_s_ref, out_ref):
    heads = out_s_ref.shape[1] // HD
    width = heads * HD

    def log_of(part):
        return back_ref[pl.ds(pl.multiple_of(part * items, items), items), width:].astype(jnp.float32)

    def whole(x):
        x = x[:, : 3 * heads]
        return x[:, :heads] + x[:, heads : 2 * heads] + x[:, 2 * heads :]

    logs = [whole(log_of(part)) for part in range(parts)]
    log_s = log_s_ref[:, :heads]
    top = log_s
    for log in logs:
        top = jnp.maximum(top, log)
    factor_s = jnp.exp(log_s - top)
    factors = [jnp.exp(log - top) for log in logs]
    total = factor_s
    for factor in factors:
        total += factor
    inverse = 1.0 / total
    factor_s = factor_s * inverse
    factors = [factor * inverse for factor in factors]
    for h in range(heads):
        columns = slice(h * HD, (h + 1) * HD)
        acc = factor_s[:, h : h + 1] * out_s_ref[:, columns]
        for part in range(parts):
            value = back_ref[part * items : (part + 1) * items, columns].astype(jnp.float32)
            acc += factors[part][:, h : h + 1] * value
        out_ref[:, columns] = acc.astype(jnp.bfloat16)


def merge(back, out_s, log_s, parts):
    items, width = out_s.shape
    return pl.pallas_call(
        functools.partial(merge_kernel, parts, items),
        out_shape=jax.ShapeDtypeStruct((items, width), jnp.bfloat16),
        compiler_params=pltpu.CompilerParams(vmem_limit_bytes=VMEM),
    )(back, out_s, log_s)


def local(queries, selected, placement, lengths, cache_k, cache_v, suffix_k, suffix_v):
    rows_here, steps, width = queries.shape
    listed = selected.shape[2]
    parts = lax.axis_size("ctx")
    blocks_here = cache_k.shape[0]
    items = rows_here * steps
    own = lax.axis_index("ctx")
    flat_queries = queries.reshape(items, width)
    ids = jnp.pad(
        selected.reshape(items, listed).astype(jnp.bfloat16),
        ((0, 0), (0, LANES - listed)),
        constant_values=-1,
    )
    payload = lax.all_gather(
        jnp.concatenate([flat_queries, ids], axis=1), "ctx", axis=0, tiled=True
    )
    cache_index = own * blocks_here + jnp.arange(blocks_here, dtype=jnp.int32)
    block_ids = jnp.arange(placement.shape[0], dtype=jnp.int32)
    targets = jnp.sum(
        jnp.where(placement[None, :] == cache_index[:, None], block_ids[None, :], 0), axis=1
    )
    limits = (lengths[:, None] + jnp.arange(steps, dtype=jnp.int32)[None, :]).reshape(items, 1)
    out_s, log_s = attend_suffix(flat_queries, limits, suffix_k, suffix_v, steps)
    partial = attend_blocks(targets, payload, cache_k, cache_v, width)
    back = lax.all_to_all(partial, "ctx", split_axis=0, concat_axis=0, tiled=True)
    merged = merge(back, out_s, log_s, parts)
    return merged.reshape(rows_here, steps, width)


def solution(mesh):
    rows = P(("groups", "ctx"), None, "rows")
    in_specs = (
        rows,
        P(("groups", "ctx"), None, None),
        P("groups"),
        P(("groups", "ctx")),
        rows,
        rows,
        rows,
        rows,
    )
    return jax.shard_map(local, mesh=mesh, in_specs=in_specs, out_specs=rows, check_vma=False)
```

time: 235 us -> 110 us (0.47); the launches traced: 231 us -> 110 us
  waiting for transfers between devices: 91.7 us -> 47 us
  matrix products: 40.7 us -> 0 us
  Pallas kernels: 0 us -> 38.6 us
  other arithmetic: 28.8 us -> 2.87 us
  local copies, waits for them, and re-layouts: 30 us -> 4.22 us
  blocking collectives: 15.9 us -> 0 us
  starting transfers between devices: 9.56 us -> 3.69 us
    all_to_all x2 -> x1, waiting for transfers between devices: 91 us -> 23.3 us  [local(): lax.all_to_all(partial, 'ctx', split_axis=0, concat_axis=0, tiled=True)]
    dot_general x37 -> x0, matrix products: 40.7 us -> none  [the longest x16 22 us: attend_block(): jnp.einsum('nht,td->nhd', exponent.astype(jnp.bfloat16), values_now, pref...]
    pallas_call x0 -> x3, Pallas kernels: none -> 38.6 us  [the longest x1 32.6 us: attend_blocks(): pl.pallas_call(functools.partial(block_kernel, heads_step, group_size), g...]
    all_gather x1, waiting for transfers between devices: 0.01 us -> 23.7 us  [local(): lax.all_gather(jnp.concatenate([flat_queries, ids], axis=1), 'ctx', axis=...]
    reduce_sum x23 -> x1, other arithmetic: 22.3 us -> 1.41 us  [local(): jnp.sum(jnp.where(placement[None, :] == cache_index[:, None], block_ids[N...]
    all_gather x1 -> x0, blocking collectives: 15.9 us -> none  [local(): all_selected = lax.all_gather(selected, 'ctx', axis=0, tiled=True)]
    another operation x13 -> x0, local copies, waits for them, and re-layouts: 6.88 us -> none  [the longest x4 3.57 us: local(): jnp.stack(block_outputs, axis=1)]
    dot_general x1 -> x0, local copies, waits for them, and re-layouts: 6.54 us -> none  [local(): jnp.dot(collect.astype(jnp.bfloat16), returned_out.reshape(total_blocks *...]
  transfers between devices with their start and end apart: 3 -> 2, of which waited for: 2 -> 2; matrix products, arithmetic and copies ran while one was open for 9% -> 2% of each run, Pallas kernels for 0% -> 3%
where the time goes in v1:
time: 110 us
  waiting for transfers between devices  47 us (43%)
  Pallas kernels  38.6 us (35%)
  between operations  13.4 us (12%)
  local copies, waits for them, and re-layouts  4.22 us (4%)
  starting transfers between devices  3.69 us (3%)
  other arithmetic  2.87 us (3%)
    pallas_call x1, Pallas kernels, attend_blocks(): pl.pallas_call(functools.partial(block_kernel, heads_step, group_size), g...  32.6 us
    all_gather x1, waiting for transfers between devices, local(): lax.all_gather(jnp.concatenate([flat_queries, ids], axis=1), 'ctx', axis=...  23.7 us
    all_to_all x1, waiting for transfers between devices, local(): lax.all_to_all(partial, 'ctx', split_axis=0, concat_axis=0, tiled=True)  23.3 us
    all_to_all x1, starting transfers between devices, local(): lax.all_to_all(partial, 'ctx', split_axis=0, concat_axis=0, tiled=True)  3.69 us
    pallas_call x1, Pallas kernels, attend_suffix(): pl.pallas_call(functools.partial(suffix_kernel, kv_width // HD, width //...  3.21 us
    pallas_call x1, Pallas kernels, merge(): pl.pallas_call(functools.partial(merge_kernel, parts, items), out_shape=j...  2.83 us
  transfers between devices with their start and end apart: 2, of which 2 were waited for; matrix products, arithmetic and copies ran while one was open for 2% of the time, Pallas kernels for 3%

profile of v1, /device:TPU:0, one launch (start us, length us, event | category | flops | bytes accessed | tf_op | source)
XLA Modules:
  0.0 109.8 jit_solution(7564790625148289848)
XLA Ops:
  6.5 0.0 all-gather.2.cloned.1.call-start
  6.5 0.7 convert_element_type.8
  7.2 0.9 reshape.39.q_ref
  8.2 0.0 copy-start.1
  8.2 0.7 fusion.1
  8.9 0.0 all-gather.2.cloned.1.call-update
  8.9 1.4 %select_reduce_fusion.targets = s32[4]{0:T(128)} fusion(s32[32]{0:T(128)} %param.10, s32[4]{0:T(128)S(1)} %iota_add_fusion.1), kind=kLoop, calls=%fused_computation.4 | loop fusion | flops 380 | bytes 160 | tf_op jit(solution)/shard_map/reduce_sum | solution.py:226
  10.3 23.7 %all-gather.2.cloned.1.call-done.q_ref.ids_ref = bf16[128,4224]{1,0:T(8,128)(2,1)} async-done(((bf16[16,4224]{1,0:T(8,128)(2,1)}), bf16[128,4224]{1,0:T(8,128)(2,1)}) %all-gather.2.cloned.1.call-update) | async-done | bytes 1081360 | tf_op jit(solution)/shard_map/all_gather | solution.py:221
  34.0 32.6 %shard_map.82 = bf16[128,4224]{1,0:T(8,128)(2,1)} custom-call(s32[4]{0:T(128)} %select_reduce_fusion.targets, bf16[128,4224]{1,0:T(8,128)(2,1)} %all-gather.2.cloned.1.call-done.q_ref.ids_ref, bf16[128,4224]{1,0:T(8,128)(2,1)} %all-gather.2.cloned.1.call-done.q_ref.ids_ref, bf16[4,1024,512]{2,1,0:T(8,128)(2,1)} %k_ref.2, bf16[4,1024,512]{2,1,0:T(8,128)(2,1)} %v_ref.2), custom_call_target="tpu_custom_call" | custom-call | flops 8589934592 | bytes 10485760 | tf_op jit(solution)/shard_map/pallas_call | solution.py:93
  66.6 0.0 copy-done.1
  66.6 0.0 copy-start.2
  66.6 3.7 %all-to-all-start = ((bf16[8,16,4224]{2,1,0:T(8,128)(2,1)}), bf16[8,16,4224]{2,1,0:T(8,128)(2,1)S(1)}, u32[]{:S(2)}, u32[]{:S(2)}) async-start(bf16[8,16,4224]{2,1,0:T(8,128)(2,1)} %bitcast.4), calls=%async_computation | async-start | bytes 2162688 | tf_op jit(solution)/shard_map/all_to_all | solution.py:232
  70.3 0.0 copy-done.2
  70.3 0.1 iota_add_fusion
  70.4 0.7 add.41.limit_ref
  71.1 3.2 %shard_map.83 = (f32[16,4096]{1,0:T(8,128)}, f32[16,128]{1,0:T(8,128)}) custom-call(bf16[16,4096]{1,0:T(8,128)(2,1)} %copy-done.1, s32[16,1]{1,0:T(8,128)} %add.41.limit_ref, bf16[4,128,512]{2,1,0:T(8,128)(2,1)} %k_ref.3, bf16[4,128,512]{2,1,0:T(8,128)(2,1)} %v_ref.3), custom_call_target="tpu_custom_call" | custom-call | tf_op jit(solution)/shard_map/pallas_call | solution.py:156
  74.3 23.3 %all-to-all-done = bf16[8,16,4224]{2,1,0:T(8,128)(2,1)S(1)} async-done(((bf16[8,16,4224]{2,1,0:T(8,128)(2,1)}), bf16[8,16,4224]{2,1,0:T(8,128)(2,1)S(1)}, u32[]{:S(2)}, u32[]{:S(2)}) %all-to-all-start) | async-done | bytes 1081376 | tf_op jit(solution)/shard_map/all_to_all | solution.py:232
  97.5 0.0 copy-start
  97.5 1.0 copy-done
  98.5 2.8 %shard_map.84 = bf16[16,4096]{1,0:T(8,128)(2,1)} custom-call(bf16[128,4224]{1,0:T(8,128)(2,1)} %bitcast.3, f32[16,4096]{1,0:T(8,128)} %get-tuple-element.7.out_s_ref, f32[16,128]{1,0:T(8,128)} %get-tuple-element.8.log_s_ref), custom_call_target="tpu_custom_call" | custom-call | tf_op jit(solution)/shard_map/pallas_call | solution.py:201
  101.3 1.6 %reshape.40 = bf16[4,4,4096]{2,1,0:T(4,128)(2,1)} reshape(bf16[16,4096]{1,0:T(8,128)(2,1)} %shard_map.84) | data formatting | bytes 262144 | tf_op jit(solution)/shard_map/reshape | solution.py:234
  (1 shorter events, 0.0 us)
Async XLA Ops:
  6.5 27.5 %all-gather.2.cloned.1.call-start = ((), (), s32[]{:S(2)}) async-start(), calls=%async_computation.1 | async-start | bytes 1216512 | tf_op jit(solution)/shard_map/all_gather | solution.py:221
  8.2 58.4 %copy-start.1 = (bf16[16,4096]{1,0:T(8,128)(2,1)}, bf16[16,4096]{1,0:T(8,128)(2,1)S(1)}, u32[]{:S(2)}) copy-start(bf16[16,4096]{1,0:T(8,128)(2,1)S(1)} %reshape.39.q_ref) | copy-start | bytes 393220
  66.6 3.7 %copy-start.2 = (s32[4]{0:T(128)S(1)}, s32[4]{0:T(128)}, u32[]{:S(2)}) copy-start(s32[4]{0:T(128)} %param.11) | copy-start | bytes 52
  66.6 30.9 %all-to-all-start = ((bf16[8,16,4224]{2,1,0:T(8,128)(2,1)}), bf16[8,16,4224]{2,1,0:T(8,128)(2,1)S(1)}, u32[]{:S(2)}, u32[]{:S(2)}) async-start(bf16[8,16,4224]{2,1,0:T(8,128)(2,1)} %bitcast.4), calls=%async_computation | async-start | bytes 2162688 | tf_op jit(solution)/shard_map/all_to_all | solution.py:232
  97.5 1.0 copy-start
Sparse Core Ops, SparseCore 0:
  9.0 24.9 all-gather.1

commit v2 on v1

v2 whole, which is shorter than its diff:
```python
import functools
import math

import jax
import jax.numpy as jnp
from jax import lax
from jax.experimental import pallas as pl
from jax.experimental.pallas import tpu as pltpu
from jax.sharding import PartitionSpec as P

HD = 128
LANES = 128
SCALE = 1.0 / math.sqrt(HD)
LOG2E = math.log2(math.e)
NONE = -1e30
LOW, HIGH = 2.0**-80, 2.0**100
VMEM = 56 * 1024 * 1024


def split3(x):
    high = x.astype(jnp.bfloat16)
    rest = x - high.astype(jnp.float32)
    middle = rest.astype(jnp.bfloat16)
    low = (rest - middle.astype(jnp.float32)).astype(jnp.bfloat16)
    return high, middle, low


def dot_nt(a, b):
    return lax.dot_general(a, b, (((1,), (1,)), ((), ())), preferred_element_type=jnp.float32)


def stack(arrays):
    return arrays[0] if len(arrays) == 1 else jnp.concatenate(arrays, axis=0)


def params():
    return pltpu.CompilerParams(vmem_limit_bytes=VMEM)


def pack_kernel(chunks, q_ref, selected_ref, *out_refs):
    rows, steps, width = q_ref.shape
    items = rows * steps
    columns = width // chunks
    for c in range(chunks):
        part = q_ref[:, :, c * columns : (c + 1) * columns].astype(jnp.float32)
        out_refs[c][:, :columns] = part.reshape(items, columns).astype(jnp.bfloat16)
    ids = selected_ref[...].astype(jnp.float32).reshape(items, -1)
    pad = jnp.full((items, LANES - ids.shape[1]), -1.0, jnp.float32)
    out_refs[0][:, columns:] = jnp.concatenate([ids, pad], axis=1).astype(jnp.bfloat16)


def pack(queries, selected, chunks):
    rows, steps, width = queries.shape
    columns = width // chunks
    return pl.pallas_call(
        functools.partial(pack_kernel, chunks),
        out_shape=[
            jax.ShapeDtypeStruct((rows * steps, columns + (LANES if c == 0 else 0)), jnp.bfloat16)
            for c in range(chunks)
        ],
        compiler_params=params(),
    )(queries, selected)


def block_kernel(pieces, group_size, base_ref, place_ref, *refs):
    q_refs = refs[:pieces]
    id_refs = refs[pieces : 2 * pieces]
    k_ref, v_ref = refs[2 * pieces : 2 * pieces + 2]
    out_refs = refs[2 * pieces + 2 : 3 * pieces + 2]
    logs_ref, s_ref = refs[3 * pieces + 2 :]
    kv = pl.program_id(1)
    share = q_refs[0].shape[0]
    items = share * pieces
    blocks = k_ref.shape[0]
    tokens = k_ref.shape[1]
    lane = lax.broadcasted_iota(jnp.int32, (items, LANES), 1)
    first_head = kv * group_size
    mine = (lane >= first_head) & (lane < first_head + group_size)
    ids = stack([ref[...].astype(jnp.float32) for ref in id_refs])
    place = place_ref[...]
    block_ids = lax.broadcasted_iota(jnp.int32, place.shape, 1)
    hits = []
    for b in range(blocks):
        target = jnp.sum(
            jnp.where(place == base_ref[0] + b, block_ids, 0).astype(jnp.float32), axis=1, keepdims=True
        )
        hits.append(jnp.max(jnp.where(ids == target, 1.0, 0.0), axis=1, keepdims=True))
    some = hits[0]
    for hit in hits[1:]:
        some = jnp.maximum(some, hit)

    def write(head, out):
        start = pl.multiple_of((first_head + head) * HD, HD)
        out = out.astype(jnp.bfloat16)
        for n, ref in enumerate(out_refs):
            ref[:, pl.ds(start, HD)] = out[n * share : (n + 1) * share]

    step = 2
    ones = jnp.ones((tokens, LANES), jnp.bfloat16)
    totals = jnp.ones((items, LANES), jnp.float32)
    for first in range(0, group_size, step):
        q = stack(
            [ref[:, h * HD : (h + 1) * HD] for h in range(first, first + step) for ref in q_refs]
        )
        acc = jnp.zeros((step * items, HD + LANES), jnp.float32)
        for b in range(blocks):
            p = jnp.exp2(dot_nt(q, k_ref[b]) * (SCALE * LOG2E)).astype(jnp.bfloat16)
            values = jnp.concatenate([v_ref[b], ones], axis=1)
            here = jnp.dot(p, values, preferred_element_type=jnp.float32)
            hit = stack([hits[b]] * step)
            acc = jnp.where(hit > 0.0, acc + here, acc)
        for n in range(step):
            total = acc[n * items : (n + 1) * items, HD:]
            out = acc[n * items : (n + 1) * items, :HD]
            write(first + n, jnp.where(some > 0.0, out / jnp.where(some > 0.0, total, 1.0), 0.0))
            totals = jnp.where(lane == first_head + first + n, total, totals)
    good = (totals > LOW) & (totals < HIGH)
    bad = jnp.max(jnp.where(good | (some == 0.0), 0.0, 1.0))
    logs = jnp.where((some > 0.0) & good, jnp.log(jnp.where(good, totals, 1.0)), NONE)
    logs_ref[...] = jnp.where(mine, logs, logs_ref[...])

    @pl.when(bad > 0.0)
    def _():
        @pl.loop(0, group_size)
        def _(head):
            start = pl.multiple_of(head * HD, HD)
            q = stack([ref[:, pl.ds(start, HD)] for ref in q_refs])
            top = jnp.full((items, 1), NONE, jnp.float32)
            for b in range(blocks):
                s = dot_nt(q, k_ref[b])
                s_ref[b] = s
                here = jnp.max(s, axis=1, keepdims=True)
                top = jnp.where(hits[b] > 0.0, jnp.maximum(top, here), top)
            acc = jnp.zeros((items, HD), jnp.float32)
            total = jnp.zeros((items, 1), jnp.float32)
            for b in range(blocks):
                p = jnp.exp2((s_ref[b] - top) * (SCALE * LOG2E))
                p = jnp.where(hits[b] > 0.0, p, 0.0)
                total += jnp.sum(p, axis=1, keepdims=True)
                acc += jnp.dot(p.astype(jnp.bfloat16), v_ref[b], preferred_element_type=jnp.float32)
            safe = jnp.where(some > 0.0, total, 1.0)
            write(head, jnp.where(some > 0.0, acc / safe, 0.0))
            log = jnp.where(some > 0.0, top * SCALE + jnp.log(safe), NONE)
            logs_ref[...] = jnp.where(lane == first_head + head, log, logs_ref[...])

    @pl.when(kv == pl.num_programs(1) - 1)
    def _():
        heads = (out_refs[0].shape[1] - LANES) // HD
        parts = jnp.concatenate([x[:, :heads] for x in split3(logs_ref[...])], axis=1)
        pad = jnp.zeros((items, LANES - 3 * heads), jnp.bfloat16)
        both = jnp.concatenate([parts, pad], axis=1)
        for n, ref in enumerate(out_refs):
            ref[:, heads * HD :] = both[n * share : (n + 1) * share]


def attend_blocks(chunk, base, place, queries, ids, cache_k, cache_v, group_size, kv_chunk):
    pieces = len(queries)
    rows = queries[0].shape[0]
    blocks, tokens, _ = cache_k.shape
    columns = kv_chunk * group_size * HD
    id_block = ids[0].shape[1] // LANES - 1
    share = min(rows, 128)
    items = share * pieces
    out_columns = columns + LANES
    return pl.pallas_call(
        functools.partial(block_kernel, pieces, group_size),
        grid_spec=pltpu.PrefetchScalarGridSpec(
            num_scalar_prefetch=1,
            grid=(rows // share, kv_chunk),
            in_specs=[pl.BlockSpec(place.shape, lambda i, g, t: (0, 0))]
            + [pl.BlockSpec((share, group_size * HD), lambda i, g, t: (i, g))] * pieces
            + [pl.BlockSpec((share, LANES), lambda i, g, t: (i, id_block))] * pieces
            + [pl.BlockSpec((blocks, tokens, HD), lambda i, g, t: (0, 0, chunk * kv_chunk + g))] * 2,
            out_specs=[pl.BlockSpec((share, out_columns), lambda i, g, t: (i, 0))] * pieces,
            scratch_shapes=[
                pltpu.VMEM((items, LANES), jnp.float32),
                pltpu.VMEM((blocks, items, tokens), jnp.float32),
            ],
        ),
        out_shape=[jax.ShapeDtypeStruct((rows, out_columns), jnp.bfloat16)] * pieces,
        compiler_params=params(),
        cost_estimate=pl.CostEstimate(
            flops=8 * rows * pieces * blocks * tokens * columns,
            bytes_accessed=4 * blocks * tokens * kv_chunk * HD + 4 * rows * pieces * columns,
            transcendentals=rows * pieces * blocks * tokens * columns // HD,
        ),
    )(base, place, *queries, *ids, cache_k, cache_v)


def suffix_kernel(kv_here, group_size, steps, *refs):
    chunks = len(refs) - 5
    q_refs = refs[:chunks]
    limit_ref, k_ref, v_ref, out_ref, log_ref = refs[chunks:]
    items = limit_ref.shape[0]
    rows_here, tokens, _ = k_ref.shape
    span = rows_here * tokens
    lane = lax.broadcasted_iota(jnp.int32, (items, LANES), 1)
    token = lax.broadcasted_iota(jnp.int32, (items, span), 1)
    item = lax.broadcasted_iota(jnp.int32, (items, span), 0)
    offset = token - (item // steps) * tokens
    seen = jnp.where((offset >= 0) & (offset < limit_ref[...]), 1.0, 0.0)
    seen = jnp.concatenate([seen] * group_size, axis=0)
    logs = jnp.zeros((items, LANES), jnp.float32)
    kv_chunk = kv_here // chunks
    for g in range(kv_here):
        q_ref = q_refs[g // kv_chunk]
        first = (g % kv_chunk) * group_size
        q = stack([q_ref[:, h * HD : (h + 1) * HD] for h in range(first, first + group_size)])
        keys = k_ref[:, :, g * HD : (g + 1) * HD].reshape(span, HD)
        values = v_ref[:, :, g * HD : (g + 1) * HD].reshape(span, HD)
        s = jnp.where(seen > 0.0, dot_nt(q, keys), NONE)
        highest = jnp.max(s, axis=1, keepdims=True)
        p = jnp.exp2((s - highest) * (SCALE * LOG2E))
        p = jnp.where(seen > 0.0, p, 0.0)
        total = jnp.sum(p, axis=1, keepdims=True)
        out = jnp.dot(p.astype(jnp.bfloat16), values, preferred_element_type=jnp.float32) / total
        log = highest * SCALE + jnp.log(total)
        for n in range(group_size):
            h = g * group_size + n
            out_ref[:, h * HD : (h + 1) * HD] = out[n * items : (n + 1) * items]
            logs = jnp.where(lane == h, log[n * items : (n + 1) * items], logs)
    log_ref[...] = logs


def attend_suffix(queries, limits, suffix_k, suffix_v, steps, group_size):
    items = queries[0].shape[0]
    rows, tokens, kv_width = suffix_k.shape
    width = kv_width * group_size
    return pl.pallas_call(
        functools.partial(suffix_kernel, kv_width // HD, group_size, steps),
        out_shape=(
            jax.ShapeDtypeStruct((items, width), jnp.float32),
            jax.ShapeDtypeStruct((items, LANES), jnp.float32),
        ),
        compiler_params=params(),
        cost_estimate=pl.CostEstimate(
            flops=16 * items * rows * tokens * width,
            bytes_accessed=4 * suffix_k.size + 6 * items * width,
            transcendentals=items * rows * tokens * width // HD,
        ),
    )(*queries, limits, suffix_k, suffix_v)


def merge_kernel(steps, chunk, arrays, *refs):
    back_refs = refs[:arrays]
    out_s_ref, log_s_ref = refs[arrays : arrays + 2]
    out_ref = refs[-1]
    items, columns = out_s_ref.shape
    heads = columns // HD
    first = chunk * heads
    parts = [(ref, start) for ref in back_refs for start in range(0, ref.shape[0], items)]
    logs = []
    for ref, start in parts:
        x = ref[start : start + items, columns:].astype(jnp.float32)
        logs.append(x[:, :heads] + x[:, heads : 2 * heads] + x[:, 2 * heads : 3 * heads])
    log_s = log_s_ref[:, first : first + heads]
    top = log_s
    for log in logs:
        top = jnp.maximum(top, log)
    factor_s = jnp.exp(log_s - top)
    factors = [jnp.exp(log - top) for log in logs]
    total = factor_s
    for factor in factors:
        total += factor
    inverse = 1.0 / total
    factor_s = factor_s * inverse
    factors = [factor * inverse for factor in factors]
    for h in range(heads):
        span = slice(h * HD, (h + 1) * HD)
        acc = factor_s[:, h : h + 1] * out_s_ref[:, span]
        for factor, (ref, start) in zip(factors, parts):
            acc += factor[:, h : h + 1] * ref[start : start + items, span].astype(jnp.float32)
        for row in range(items // steps):
            out_ref[row, :, span] = acc[row * steps : (row + 1) * steps].astype(jnp.bfloat16)


def merge(chunk, steps, back, out_s, log_s, so_far):
    items, width = out_s.shape
    columns = back[0].shape[1] - LANES
    shape = (items // steps, steps, width)
    others = [] if so_far is None else [so_far]
    return pl.pallas_call(
        functools.partial(merge_kernel, steps, chunk, len(back)),
        grid=(1,),
        in_specs=[pl.BlockSpec(x.shape, lambda i: (0, 0)) for x in back]
        + [pl.BlockSpec((items, columns), lambda i: (0, chunk)), pl.BlockSpec(log_s.shape, lambda i: (0, 0))]
        + [pl.BlockSpec(memory_space=pl.ANY)] * len(others),
        out_specs=pl.BlockSpec((shape[0], steps, columns), lambda i: (0, 0, chunk)),
        out_shape=jax.ShapeDtypeStruct(shape, jnp.bfloat16),
        input_output_aliases={len(back) + 2: 0} if others else {},
        compiler_params=params(),
    )(*back, out_s, log_s, *others)


def swap(x, bits, size):
    return lax.ppermute(x, "ctx", [(i, i ^ bits) for i in range(size)])


def gather(x, size, few):
    if not few:
        return [lax.all_gather(x, "ctx", axis=0, tiled=True)]
    same = {0: x}
    for n in range(2, size, 2):
        same[n] = swap(x, n, size)
    every = dict(same)
    for n in range(0, size, 2):
        every[n ^ 1] = swap(same[n], 1, size)
    return [every[n] for n in range(size)]


def give_back(arrays, size, few):
    if not few:
        return [lax.all_to_all(arrays[0], "ctx", split_axis=0, concat_axis=0, tiled=True)]
    return [x if n == 0 else swap(x, n, size) for n, x in enumerate(arrays)]


def local(queries, selected, placement, lengths, cache_k, cache_v, suffix_k, suffix_v):
    rows_here, steps, width = queries.shape
    size = lax.axis_size("ctx")
    blocks_here, _, kv_width = cache_k.shape
    kv_here = kv_width // HD
    group_size = width // kv_width
    items = rows_here * steps
    few = size <= 8
    chunks = 2
    kv_chunk = kv_here // chunks
    base = (lax.axis_index("ctx") * blocks_here).astype(jnp.int32).reshape(1)
    place = placement.reshape(1, -1)
    limits = (lengths[:, None] + jnp.arange(steps, dtype=jnp.int32)[None, :]).reshape(items, 1)
    packed = pack(queries, selected, chunks)
    gathered = [gather(x, size, few) for x in packed]
    out_s, log_s = attend_suffix(packed, limits, suffix_k, suffix_v, steps, group_size)
    merged = None
    returned = []
    for c in range(chunks):
        partial = attend_blocks(
            c, base, place, gathered[c], gathered[0], cache_k, cache_v, group_size, kv_chunk
        )
        returned.append(give_back(partial, size, few))
    for c in range(chunks):
        merged = merge(c, steps, returned[c], out_s, log_s, merged)
    return merged


def solution(mesh):
    rows = P(("groups", "ctx"), None, "rows")
    in_specs = (
        rows,
        P(("groups", "ctx"), None, None),
        P("groups"),
        P(("groups", "ctx")),
        rows,
        rows,
        rows,
        rows,
    )
    return jax.shard_map(local, mesh=mesh, in_specs=in_specs, out_specs=rows, check_vma=False)
```

time: 110 us -> 121 us (1.10)
  Pallas kernels: 38.6 us -> 76.7 us
  waiting for transfers between devices: 47 us -> 10.9 us
  starting transfers between devices: 3.69 us -> 29.9 us
  between operations: 13.4 us -> 0.31 us
  other arithmetic: 2.87 us -> 0.07 us
  local copies, waits for them, and re-layouts: 4.22 us -> 2.05 us
    pallas_call x3 -> x6, Pallas kernels: 38.6 us -> 76.7 us  [the longest x2 67 us: attend_blocks(): pl.pallas_call(functools.partial(block_kernel, pieces, group_size), grid_...]
    ppermute x0 -> x28, starting transfers between devices: none -> 29.9 us  [swap(): return lax.ppermute(x, 'ctx', [(i, i ^ bits) for i in range(size)])]
    all_gather x1 -> x0, waiting for transfers between devices: 23.7 us -> none  [local(): lax.all_gather(jnp.concatenate([flat_queries, ids], axis=1), 'ctx', axis=...]
    all_to_all x1 -> x0, waiting for transfers between devices: 23.3 us -> none  [local(): lax.all_to_all(partial, 'ctx', split_axis=0, concat_axis=0, tiled=True)]
    ppermute x0 -> x28, waiting for transfers between devices: none -> 10.9 us  [swap(): return lax.ppermute(x, 'ctx', [(i, i ^ bits) for i in range(size)])]
    all_to_all x1 -> x0, starting transfers between devices: 3.69 us -> none  [local(): lax.all_to_all(partial, 'ctx', split_axis=0, concat_axis=0, tiled=True)]
    reshape x2 -> x0, local copies, waits for them, and re-layouts: 2.55 us -> none  [the longest x1 1.61 us: local(): return merged.reshape(rows_here, steps, width)]
    reduce_sum x1 -> x0, other arithmetic: 1.41 us -> none  [local(): jnp.sum(jnp.where(placement[None, :] == cache_index[:, None], block_ids[N...]
  transfers between devices with their start and end apart: 2 -> 28, of which waited for: 2 -> 5; matrix products, arithmetic and copies ran while one was open for 2% -> 1% of each run, Pallas kernels for 3% -> 60%
where the time goes in v2:
time: 121 us; the launch traced here: 120 us
  Pallas kernels  76.7 us (63%)
  starting transfers between devices  29.9 us (25%)
  waiting for transfers between devices  10.9 us (9%)
  local copies, waits for them, and re-layouts  2.05 us (2%)
    pallas_call x2, Pallas kernels, attend_blocks(): pl.pallas_call(functools.partial(block_kernel, pieces, group_size), grid_...  67 us
    ppermute x28, starting transfers between devices, swap(): return lax.ppermute(x, 'ctx', [(i, i ^ bits) for i in range(size)])  29.9 us
    ppermute x28, waiting for transfers between devices, swap(): return lax.ppermute(x, 'ctx', [(i, i ^ bits) for i in range(size)])  10.9 us
    pallas_call x2, Pallas kernels, merge(): pl.pallas_call(functools.partial(merge_kernel, steps, chunk, len(back)),...  4.92 us
    pallas_call x1, Pallas kernels, attend_suffix(): pl.pallas_call(functools.partial(suffix_kernel, kv_width // HD, group_siz...  3.21 us
  transfers between devices with their start and end apart: 28, of which 5 were waited for; matrix products, arithmetic and copies ran while one was open for 1% of the time, Pallas kernels for 60%

profile of v2, /device:TPU:0, one launch (start us, length us, event | category | flops | bytes accessed | tf_op | source)
XLA Modules:
  0.0 120.0 jit_solution(1986868563804641772)
XLA Ops:
  0.0 1.6 %shard_map.82 = (bf16[16,2176]{1,0:T(8,128)(2,1)}, bf16[16,2048]{1,0:T(8,128)(2,1)}) custom-call(bf16[4,4,4096]{2,1,0:T(4,128)(2,1)} %q_ref.1, s32[4,4,16]{2,1,0:T(4,128)} %selected_ref.1), custom_call_target="tpu_custom_call" | custom-call | tf_op jit(solution)/shard_map/pallas_call | solution.py:55
  1.6 5.0 %collective-permute-start.12 = (bf16[16,2176]{1,0:T(8,128)(2,1)}, bf16[16,2176]{1,0:T(8,128)(2,1)S(1)}, u32[]{:S(2)}, u32[]{:S(2)}) collective-permute-start(bf16[16,2176]{1,0:T(8,128)(2,1)} %get-tuple-element.26.refs_8_.refs_0_), channel_id=1, source_target_pairs={{0,12},{2,14},{4,8},{6,10},{8,4},{10,6},{12,0},{14,2},{1,13},{3,15... | collective-permute-start | bytes 208904 | tf_op jit(solution)/shard_map/ppermute | solution.py:296
  7.2 3.8 %collective-permute-start.5 = (bf16[16,2048]{1,0:T(8,128)(2,1)}, bf16[16,2048]{1,0:T(8,128)(2,1)S(1)}, u32[]{:S(2)}, u32[]{:S(2)}) collective-permute-start(bf16[16,2048]{1,0:T(8,128)(2,1)} %get-tuple-element.25.refs_0_.refs_1_), channel_id=1, source_target_pairs={{0,12},{2,14},{4,8},{6,10},{8,4},{10,6},{12,0},{14,2},{1,13},{3,15... | collective-permute-start | bytes 196616 | tf_op jit(solution)/shard_map/ppermute | solution.py:296
  11.0 3.7 %collective-permute-done.5.refs_6_ = bf16[16,2048]{1,0:T(8,128)(2,1)S(1)} collective-permute-done((bf16[16,2048]{1,0:T(8,128)(2,1)}, bf16[16,2048]{1,0:T(8,128)(2,1)S(1)}, u32[]{:S(2)}, u32[]{:S(2)}) %collective-permute-start.5) | collective-permute-done | bytes 65568 | tf_op jit(solution)/shard_map/ppermute | solution.py:296
  15.2 0.9 collective-permute-done.10.refs_12_.refs_4_
  16.7 1.7 %collective-permute-done.3.refs_4_ = bf16[16,2048]{1,0:T(8,128)(2,1)S(1)} collective-permute-done((bf16[16,2048]{1,0:T(8,128)(2,1)}, bf16[16,2048]{1,0:T(8,128)(2,1)S(1)}, u32[]{:S(2)}, u32[]{:S(2)}) %collective-permute-start.3) | collective-permute-done | bytes 65568 | tf_op jit(solution)/shard_map/ppermute | solution.py:296
  18.4 0.8 collective-permute-start.1
  19.2 3.7 %collective-permute-done.1.refs_2_ = bf16[16,2048]{1,0:T(8,128)(2,1)S(1)} collective-permute-done((bf16[16,2048]{1,0:T(8,128)(2,1)}, bf16[16,2048]{1,0:T(8,128)(2,1)S(1)}, u32[]{:S(2)}, u32[]{:S(2)}) %collective-permute-start.1) | collective-permute-done | bytes 65568 | tf_op jit(solution)/shard_map/ppermute | solution.py:296
  24.5 33.4 %shard_map.85 = (bf16[16,2176]{1,0:T(8,128)(2,1)}, bf16[16,2176]{1,0:T(8,128)(2,1)}, bf16[16,2176]{1,0:T(8,128)(2,1)}, bf16[16,2176]{1,0:T(8,128)(2,1)}, bf16[16...) custom-call(s32[1]{0:T(128)} %bitcast.base_ref, ...), custom_call_target="tpu_custom_call" | custom-call | flops 8589934592 | bytes 5242880 | tf_op jit(solution)/shard_map/pallas_call | solution.py:165
  58.1 0.8 collective-permute-start.22
  59.0 1.0 collective-permute-start.23
  59.9 2.1 %collective-permute-start.24 = (bf16[16,2176]{1,0:T(8,128)(2,1)}, bf16[16,2176]{1,0:T(8,128)(2,1)S(1)}, u32[]{:S(2)}, u32[]{:S(2)}) collective-permute-start(bf16[16,2176]{1,0:T(8,128)(2,1)} %get-tuple-element.41), channel_id=1, source_target_pairs={{0,8},{2,10},{4,12},{6,14},{8,0},{10,2},{12,4},{14,6},{1,9},{3,11}... | collective-permute-start | bytes 208904 | tf_op jit(solution)/shard_map/ppermute | solution.py:296
  62.7 33.6 %shard_map.83 = (bf16[16,2176]{1,0:T(8,128)(2,1)}, bf16[16,2176]{1,0:T(8,128)(2,1)}, bf16[16,2176]{1,0:T(8,128)(2,1)}, bf16[16,2176]{1,0:T(8,128)(2,1)}, bf16[16...) custom-call(s32[1]{0:T(128)} %bitcast.base_ref, ...), custom_call_target="tpu_custom_call" | custom-call | flops 8589934592 | bytes 5242880 | tf_op jit(solution)/shard_map/pallas_call | solution.py:165
  96.3 2.7 %collective-permute-start.26 = (bf16[16,2176]{1,0:T(8,128)(2,1)S(1)}, bf16[16,2176]{1,0:T(8,128)(2,1)S(1)}, u32[]{:S(2)}, u32[]{:S(2)}) collective-permute-start(bf16[16,2176]{1,0:T(8,128)(2,1)S(1)} %copy-done.23), channel_id=1, source_target_pairs={{0,12},{2,14},{4,8},{6,10},{8,4},{10,6},{12,0},{14,2},{1,13},{3,15... | collective-permute-start | bytes 208904 | tf_op jit(solution)/shard_map/ppermute | solution.py:296
  99.0 1.0 collective-permute-start.27
  100.4 1.5 %collective-permute-start.16 = (bf16[16,2176]{1,0:T(8,128)(2,1)}, bf16[16,2176]{1,0:T(8,128)(2,1)S(1)}, u32[]{:S(2)}, u32[]{:S(2)}) collective-permute-start(bf16[16,2176]{1,0:T(8,128)(2,1)} %get-tuple-element.30), channel_id=1, source_target_pairs={{0,6},{2,4},{4,2},{6,0},{8,14},{10,12},{12,10},{14,8},{1,7},{3,5},... | collective-permute-start | bytes 208904 | tf_op jit(solution)/shard_map/ppermute | solution.py:296
  101.9 0.9 collective-permute-done.26.refs_6_
  102.8 3.6 %collective-permute-start.17 = (bf16[16,2176]{1,0:T(8,128)(2,1)}, bf16[16,2176]{1,0:T(8,128)(2,1)S(1)}, u32[]{:S(2)}, u32[]{:S(2)}) collective-permute-start(bf16[16,2176]{1,0:T(8,128)(2,1)} %get-tuple-element.31), channel_id=1, source_target_pairs={{0,8},{2,10},{4,12},{6,14},{8,0},{10,2},{12,4},{14,6},{1,9},{3,11}... | collective-permute-start | bytes 208904 | tf_op jit(solution)/shard_map/ppermute | solution.py:296
  106.4 0.8 collective-permute-start.18
  107.2 1.2 collective-permute-start.19
  108.4 1.9 %collective-permute-start.20 = (bf16[16,2176]{1,0:T(8,128)(2,1)}, bf16[16,2176]{1,0:T(8,128)(2,1)S(1)}, u32[]{:S(2)}, u32[]{:S(2)}) collective-permute-start(bf16[16,2176]{1,0:T(8,128)(2,1)} %get-tuple-element.34), channel_id=1, source_target_pairs={{0,14},{2,12},{4,10},{6,8},{8,6},{10,4},{12,2},{14,0},{1,15},{3,13... | collective-permute-start | bytes 208904 | tf_op jit(solution)/shard_map/ppermute | solution.py:296
  111.1 3.2 %shard_map.84 = (f32[16,4096]{1,0:T(8,128)}, f32[16,128]{1,0:T(8,128)}) custom-call(bf16[16,2176]{1,0:T(8,128)(2,1)} %get-tuple-element.26.refs_8_.refs_0_, bf16[16,2048]{1,0:T(8,128)(2,1)} %get-tuple-element.25.refs_0_.refs_1_, s32[16,1]{1,0:T(8,128)} %add.27.refs_2_, bf16[4,128,512]{2,1,0:T(8,128)(2,1)} %refs_3_.1, bf16[4,128,512]{2,1,0:T(8,128)(2,1)} %refs_4_.1), custom_call_target="tpu_custom_call" | custom-call | flops 536870912 | bytes 1441792 | tf_op jit(solution)/shard_map/pallas_call | solution.py:229
  114.4 2.3 %shard_map.86.refs_10_ = bf16[4,4,4096]{2,1,0:T(4,128)(2,1)} custom-call(bf16[16,2176]{1,0:T(8,128)(2,1)} %get-tuple-element.37.refs_0_, bf16[16,2176]{1,0:T(8,128)(2,1)} %copy-done.7, bf16[16,2176]{1,0:T(8,128)(2,1)} %copy-done.8, bf16[16,2176]{1,0:T(8,128)(2,1)} %copy-done.9, bf16[16,2176]{1,0:T(8,128)(2,1)} %copy-done.10, bf16[16,2176]{1,0:T(8,128)(2,1)} %copy-done.11, ...), custom_call_target="tpu_custom_call" | custom-call | tf_op jit(solution)/shard_map/pallas_call | solution.py:282
  117.5 2.6 %shard_map.87 = bf16[4,4,4096]{2,1,0:T(4,128)(2,1)} custom-call(bf16[16,2176]{1,0:T(8,128)(2,1)} %get-tuple-element.27.refs_0_, bf16[16,2176]{1,0:T(8,128)(2,1)} %copy-done, bf16[16,2176]{1,0:T(8,128)(2,1)} %copy-done.1, bf16[16,2176]{1,0:T(8,128)(2,1)} %copy-done.2, bf16[16,2176]{1,0:T(8,128)(2,1)} %copy-done.3, ...), custom_call_target="tpu_custom_call", output_to_operand_aliasing={{}: (10, {})} | custom-call | tf_op jit(solution)/shard_map/pallas_call | solution.py:282
  (102 shorter events, 5.8 us)
Async XLA Ops:
  1.6 13.1 %collective-permute-start.12 = (bf16[16,2176]{1,0:T(8,128)(2,1)}, bf16[16,2176]{1,0:T(8,128)(2,1)S(1)}, u32[]{:S(2)}, u32[]{:S(2)}) collective-permute-start(bf16[16,2176]{1,0:T(8,128)(2,1)} %get-tuple-element.26.refs_8_.refs_0_), channel_id=1, source_target_pairs={{0,12},{2,14},{4,8},{6,10},{8,4},{10,6},{12,0},{14,2},{1,13},{3,15... | collective-permute-start | bytes 208904 | tf_op jit(solution)/shard_map/ppermute | solution.py:296
  6.6 9.5 %collective-permute-start.10 = (bf16[16,2176]{1,0:T(8,128)(2,1)}, bf16[16,2176]{1,0:T(8,128)(2,1)S(1)}, u32[]{:S(2)}, u32[]{:S(2)}) collective-permute-start(bf16[16,2176]{1,0:T(8,128)(2,1)} %get-tuple-element.26.refs_8_.refs_0_), channel_id=1, source_target_pairs={{0,8},{2,10},{4,12},{6,14},{8,0},{10,2},{12,4},{14,6},{1,9},{3,11}... | collective-permute-start | bytes 208904 | tf_op jit(solution)/shard_map/ppermute | solution.py:296
  6.6 9.5 %collective-permute-start.8 = (bf16[16,2176]{1,0:T(8,128)(2,1)}, bf16[16,2176]{1,0:T(8,128)(2,1)S(1)}, u32[]{:S(2)}, u32[]{:S(2)}) collective-permute-start(bf16[16,2176]{1,0:T(8,128)(2,1)} %get-tuple-element.26.refs_8_.refs_0_), channel_id=1, source_target_pairs={{0,4},{2,6},{4,0},{6,2},{8,12},{10,14},{12,8},{14,10},{1,5},{3,7},... | collective-permute-start | bytes 208904 | tf_op jit(solution)/shard_map/ppermute | solution.py:296
  7.2 7.5 %collective-permute-start.5 = (bf16[16,2048]{1,0:T(8,128)(2,1)}, bf16[16,2048]{1,0:T(8,128)(2,1)S(1)}, u32[]{:S(2)}, u32[]{:S(2)}) collective-permute-start(bf16[16,2048]{1,0:T(8,128)(2,1)} %get-tuple-element.25.refs_0_.refs_1_), channel_id=1, source_target_pairs={{0,12},{2,14},{4,8},{6,10},{8,4},{10,6},{12,0},{14,2},{1,13},{3,15... | collective-permute-start | bytes 196616 | tf_op jit(solution)/shard_map/ppermute | solution.py:296
  11.0 7.3 %collective-permute-start.3 = (bf16[16,2048]{1,0:T(8,128)(2,1)}, bf16[16,2048]{1,0:T(8,128)(2,1)S(1)}, u32[]{:S(2)}, u32[]{:S(2)}) collective-permute-start(bf16[16,2048]{1,0:T(8,128)(2,1)} %get-tuple-element.25.refs_0_.refs_1_), channel_id=1, source_target_pairs={{0,8},{2,10},{4,12},{6,14},{8,0},{10,2},{12,4},{14,6},{1,9},{3,11}... | collective-permute-start | bytes 196616 | tf_op jit(solution)/shard_map/ppermute | solution.py:296
  14.7 8.1 %collective-permute-start.7 = (bf16[16,2176]{1,0:T(8,128)(2,1)}, bf16[16,2176]{1,0:T(8,128)(2,1)S(1)}, u32[]{:S(2)}, u32[]{:S(2)}) collective-permute-start(bf16[16,2176]{1,0:T(8,128)(2,1)} %get-tuple-element.26.refs_8_.refs_0_), channel_id=1, source_target_pairs={{0,2},{2,0},{4,6},{6,4},{8,10},{10,8},{12,14},{14,12},{1,3},{3,1},... | collective-permute-start | bytes 208904 | tf_op jit(solution)/shard_map/ppermute | solution.py:296
  14.7 8.6 %collective-permute-start.13 = (bf16[16,2176]{1,0:T(8,128)(2,1)S(1)}, bf16[16,2176]{1,0:T(8,128)(2,1)S(1)}, u32[]{:S(2)}, u32[]{:S(2)}) collective-permute-start(bf16[16,2176]{1,0:T(8,128)(2,1)S(1)} %collective-permute-done.12.refs_14_.refs_6_), channel_id=1, source_target_pairs={{0,2},{2,0},{4,6},{6,4},{8,10},{10,8},{12,14},{14,12},{1,3},{3,1},... | collective-permute-start | bytes 208904 | tf_op jit(solution)/shard_map/ppermute | solution.py:296
  16.2 7.7 %collective-permute-start.9 = (bf16[16,2176]{1,0:T(8,128)(2,1)S(1)}, bf16[16,2176]{1,0:T(8,128)(2,1)S(1)}, u32[]{:S(2)}, u32[]{:S(2)}) collective-permute-start(bf16[16,2176]{1,0:T(8,128)(2,1)S(1)} %collective-permute-done.8.refs_10_.refs_2_), channel_id=1, source_target_pairs={{0,2},{2,0},{4,6},{6,4},{8,10},{10,8},{12,14},{14,12},{1,3},{3,1},... | collective-permute-start | bytes 208904 | tf_op jit(solution)/shard_map/ppermute | solution.py:296
  22.9 35.3 %collective-permute-start = (bf16[16,2048]{1,0:T(8,128)(2,1)}, bf16[16,2048]{1,0:T(8,128)(2,1)S(1)}, u32[]{:S(2)}, u32[]{:S(2)}) collective-permute-start(bf16[16,2048]{1,0:T(8,128)(2,1)} %get-tuple-element.25.refs_0_.refs_1_), channel_id=1, source_target_pairs={{0,2},{2,0},{4,6},{6,4},{8,10},{10,8},{12,14},{14,12},{1,3},{3,1},... | collective-permute-start | bytes 196616 | tf_op jit(solution)/shard_map/ppermute | solution.py:296
  22.9 36.1 %collective-permute-start.6 = (bf16[16,2048]{1,0:T(8,128)(2,1)S(1)}, bf16[16,2048]{1,0:T(8,128)(2,1)S(1)}, u32[]{:S(2)}, u32[]{:S(2)}) collective-permute-start(bf16[16,2048]{1,0:T(8,128)(2,1)S(1)} %collective-permute-done.5.refs_6_), channel_id=1, source_target_pairs={{0,2},{2,0},{4,6},{6,4},{8,10},{10,8},{12,14},{14,12},{1,3},{3,1},... | collective-permute-start | bytes 196616 | tf_op jit(solution)/shard_map/ppermute | solution.py:296
  23.4 36.6 %collective-permute-start.4 = (bf16[16,2048]{1,0:T(8,128)(2,1)S(1)}, bf16[16,2048]{1,0:T(8,128)(2,1)S(1)}, u32[]{:S(2)}, u32[]{:S(2)}) collective-permute-start(bf16[16,2048]{1,0:T(8,128)(2,1)S(1)} %collective-permute-done.3.refs_4_), channel_id=1, source_target_pairs={{0,2},{2,0},{4,6},{6,4},{8,10},{10,8},{12,14},{14,12},{1,3},{3,1},... | collective-permute-start | bytes 196616 | tf_op jit(solution)/shard_map/ppermute | solution.py:296
  23.5 38.6 %collective-permute-start.2 = (bf16[16,2048]{1,0:T(8,128)(2,1)S(1)}, bf16[16,2048]{1,0:T(8,128)(2,1)S(1)}, u32[]{:S(2)}, u32[]{:S(2)}) collective-permute-start(bf16[16,2048]{1,0:T(8,128)(2,1)S(1)} %collective-permute-done.1.refs_2_), channel_id=1, source_target_pairs={{0,2},{2,0},{4,6},{6,4},{8,10},{10,8},{12,14},{14,12},{1,3},{3,1},... | collective-permute-start | bytes 196616 | tf_op jit(solution)/shard_map/ppermute | solution.py:296
  58.0 38.3 %collective-permute-start.21 = (bf16[16,2176]{1,0:T(8,128)(2,1)}, bf16[16,2176]{1,0:T(8,128)(2,1)S(1)}, u32[]{:S(2)}, u32[]{:S(2)}) collective-permute-start(bf16[16,2176]{1,0:T(8,128)(2,1)} %get-tuple-element.38), channel_id=1, source_target_pairs={{0,2},{2,0},{4,6},{6,4},{8,10},{10,8},{12,14},{14,12},{1,3},{3,1},... | collective-permute-start | bytes 208904 | tf_op jit(solution)/shard_map/ppermute | solution.py:296
  58.1 40.9 %collective-permute-start.22 = (bf16[16,2176]{1,0:T(8,128)(2,1)}, bf16[16,2176]{1,0:T(8,128)(2,1)S(1)}, u32[]{:S(2)}, u32[]{:S(2)}) collective-permute-start(bf16[16,2176]{1,0:T(8,128)(2,1)} %get-tuple-element.39), channel_id=1, source_target_pairs={{0,4},{2,6},{4,0},{6,2},{8,12},{10,14},{12,8},{14,10},{1,5},{3,7},... | collective-permute-start | bytes 208904 | tf_op jit(solution)/shard_map/ppermute | solution.py:296
  59.0 41.1 %collective-permute-start.23 = (bf16[16,2176]{1,0:T(8,128)(2,1)}, bf16[16,2176]{1,0:T(8,128)(2,1)S(1)}, u32[]{:S(2)}, u32[]{:S(2)}) collective-permute-start(bf16[16,2176]{1,0:T(8,128)(2,1)} %get-tuple-element.40), channel_id=1, source_target_pairs={{0,6},{2,4},{4,2},{6,0},{8,14},{10,12},{12,10},{14,8},{1,7},{3,5},... | collective-permute-start | bytes 208904 | tf_op jit(solution)/shard_map/ppermute | solution.py:296
  59.9 40.5 %collective-permute-start.24 = (bf16[16,2176]{1,0:T(8,128)(2,1)}, bf16[16,2176]{1,0:T(8,128)(2,1)S(1)}, u32[]{:S(2)}, u32[]{:S(2)}) collective-permute-start(bf16[16,2176]{1,0:T(8,128)(2,1)} %get-tuple-element.41), channel_id=1, source_target_pairs={{0,8},{2,10},{4,12},{6,14},{8,0},{10,2},{12,4},{14,6},{1,9},{3,11}... | collective-permute-start | bytes 208904 | tf_op jit(solution)/shard_map/ppermute | solution.py:296
  62.1 38.4 %collective-permute-start.25 = (bf16[16,2176]{1,0:T(8,128)(2,1)}, bf16[16,2176]{1,0:T(8,128)(2,1)S(1)}, u32[]{:S(2)}, u32[]{:S(2)}) collective-permute-start(bf16[16,2176]{1,0:T(8,128)(2,1)} %get-tuple-element.42), channel_id=1, source_target_pairs={{0,10},{2,8},{4,14},{6,12},{8,2},{10,0},{12,6},{14,4},{1,11},{3,9}... | collective-permute-start | bytes 208904 | tf_op jit(solution)/shard_map/ppermute | solution.py:296
  99.0 7.4 %collective-permute-start.27 = (bf16[16,2176]{1,0:T(8,128)(2,1)S(1)}, bf16[16,2176]{1,0:T(8,128)(2,1)S(1)}, u32[]{:S(2)}, u32[]{:S(2)}) collective-permute-start(bf16[16,2176]{1,0:T(8,128)(2,1)S(1)} %copy-done.22), channel_id=1, source_target_pairs={{0,14},{2,12},{4,10},{6,8},{8,6},{10,4},{12,2},{14,0},{1,15},{3,13... | collective-permute-start | bytes 208904 | tf_op jit(solution)/shard_map/ppermute | solution.py:296
  100.4 8.0 %collective-permute-start.15 = (bf16[16,2176]{1,0:T(8,128)(2,1)}, bf16[16,2176]{1,0:T(8,128)(2,1)S(1)}, u32[]{:S(2)}, u32[]{:S(2)}) collective-permute-start(bf16[16,2176]{1,0:T(8,128)(2,1)} %get-tuple-element.29), channel_id=1, source_target_pairs={{0,4},{2,6},{4,0},{6,2},{8,12},{10,14},{12,8},{14,10},{1,5},{3,7},... | collective-permute-start | bytes 208904 | tf_op jit(solution)/shard_map/ppermute | solution.py:296
  100.4 16.3 %collective-permute-start.16 = (bf16[16,2176]{1,0:T(8,128)(2,1)}, bf16[16,2176]{1,0:T(8,128)(2,1)S(1)}, u32[]{:S(2)}, u32[]{:S(2)}) collective-permute-start(bf16[16,2176]{1,0:T(8,128)(2,1)} %get-tuple-element.30), channel_id=1, source_target_pairs={{0,6},{2,4},{4,2},{6,0},{8,14},{10,12},{12,10},{14,8},{1,7},{3,5},... | collective-permute-start | bytes 208904 | tf_op jit(solution)/shard_map/ppermute | solution.py:296
  102.8 13.9 %collective-permute-start.17 = (bf16[16,2176]{1,0:T(8,128)(2,1)}, bf16[16,2176]{1,0:T(8,128)(2,1)S(1)}, u32[]{:S(2)}, u32[]{:S(2)}) collective-permute-start(bf16[16,2176]{1,0:T(8,128)(2,1)} %get-tuple-element.31), channel_id=1, source_target_pairs={{0,8},{2,10},{4,12},{6,14},{8,0},{10,2},{12,4},{14,6},{1,9},{3,11}... | collective-permute-start | bytes 208904 | tf_op jit(solution)/shard_map/ppermute | solution.py:296
  106.4 10.3 %collective-permute-start.18 = (bf16[16,2176]{1,0:T(8,128)(2,1)}, bf16[16,2176]{1,0:T(8,128)(2,1)S(1)}, u32[]{:S(2)}, u32[]{:S(2)}) collective-permute-start(bf16[16,2176]{1,0:T(8,128)(2,1)} %get-tuple-element.32), channel_id=1, source_target_pairs={{0,10},{2,8},{4,14},{6,12},{8,2},{10,0},{12,6},{14,4},{1,11},{3,9}... | collective-permute-start | bytes 208904 | tf_op jit(solution)/shard_map/ppermute | solution.py:296
  107.2 9.5 %collective-permute-start.19 = (bf16[16,2176]{1,0:T(8,128)(2,1)}, bf16[16,2176]{1,0:T(8,128)(2,1)S(1)}, u32[]{:S(2)}, u32[]{:S(2)}) collective-permute-start(bf16[16,2176]{1,0:T(8,128)(2,1)} %get-tuple-element.33), channel_id=1, source_target_pairs={{0,12},{2,14},{4,8},{6,10},{8,4},{10,6},{12,0},{14,2},{1,13},{3,15... | collective-permute-start | bytes 208904 | tf_op jit(solution)/shard_map/ppermute | solution.py:296
  108.4 8.4 %collective-permute-start.20 = (bf16[16,2176]{1,0:T(8,128)(2,1)}, bf16[16,2176]{1,0:T(8,128)(2,1)S(1)}, u32[]{:S(2)}, u32[]{:S(2)}) collective-permute-start(bf16[16,2176]{1,0:T(8,128)(2,1)} %get-tuple-element.34), channel_id=1, source_target_pairs={{0,14},{2,12},{4,10},{6,8},{8,6},{10,4},{12,2},{14,0},{1,15},{3,13... | collective-permute-start | bytes 208904 | tf_op jit(solution)/shard_map/ppermute | solution.py:296
  (35 other events, 418.1 us)

commit v3 on v2

v3 whole, which is shorter than its diff:
```python
import functools
import math

import jax
import jax.numpy as jnp
from jax import lax
from jax.experimental import pallas as pl
from jax.experimental.pallas import tpu as pltpu
from jax.sharding import PartitionSpec as P

HD = 128
LANES = 128
SCALE = 1.0 / math.sqrt(HD)
LOG2E = math.log2(math.e)
NONE = -1e30
LOW, HIGH = 2.0**-80, 2.0**100
VMEM = 56 * 1024 * 1024
ROWS_STEP = 256


def split3(x):
    high = x.astype(jnp.bfloat16)
    rest = x - high.astype(jnp.float32)
    middle = rest.astype(jnp.bfloat16)
    low = (rest - middle.astype(jnp.float32)).astype(jnp.bfloat16)
    return high, middle, low


def dot_nt(a, b):
    return lax.dot_general(a, b, (((1,), (1,)), ((), ())), preferred_element_type=jnp.float32)


def stack(arrays):
    return arrays[0] if len(arrays) == 1 else jnp.concatenate(arrays, axis=0)


def params():
    return pltpu.CompilerParams(vmem_limit_bytes=VMEM)


def flat(x):
    return x.astype(jnp.float32).reshape(x.shape[0] * x.shape[1], x.shape[2])


def pack_kernel(where_ref, q_ref, selected_ref, mine_ref, other_ref):
    half = q_ref.shape[2] // 2
    core = where_ref[2]
    ids = flat(selected_ref[...])
    pad = jnp.full((ids.shape[0], LANES - ids.shape[1]), -1.0, jnp.float32)
    ids = jnp.concatenate([ids, pad], axis=1).astype(jnp.bfloat16)
    for ref, which in ((mine_ref, core), (other_ref, 1 - core)):
        start = pl.multiple_of(which * half, LANES)
        ref[:, :half] = flat(q_ref[:, :, pl.ds(start, half)]).astype(jnp.bfloat16)
        ref[:, half:] = ids


def pack(where, queries, selected):
    rows, steps, width = queries.shape
    shape = jax.ShapeDtypeStruct((rows * steps, width // 2 + LANES), jnp.bfloat16)
    whole = lambda i, w: (0, 0, 0)
    return pl.pallas_call(
        pack_kernel,
        grid_spec=pltpu.PrefetchScalarGridSpec(
            num_scalar_prefetch=1,
            grid=(1,),
            in_specs=[pl.BlockSpec(queries.shape, whole), pl.BlockSpec(selected.shape, whole)],
            out_specs=[pl.BlockSpec(shape.shape, lambda i, w: (0, 0))] * 2,
        ),
        out_shape=[shape, shape],
        compiler_params=params(),
    )(where, queries, selected)


def halve_kernel(blocks, where_ref, k_ref, v_ref, out_ref):
    @pl.when(pl.program_id(0) < blocks)
    def _():
        out_ref[...] = k_ref[...]

    @pl.when(pl.program_id(0) >= blocks)
    def _():
        out_ref[...] = v_ref[...]


def halve(where, cache_k, cache_v):
    blocks, tokens, columns = cache_k.shape
    block = (1, tokens, columns // 2)
    return pl.pallas_call(
        functools.partial(halve_kernel, blocks),
        grid_spec=pltpu.PrefetchScalarGridSpec(
            num_scalar_prefetch=1,
            grid=(2 * blocks,),
            in_specs=[
                pl.BlockSpec(block, lambda i, w: (jnp.minimum(i, blocks - 1), 0, 1 - w[2])),
                pl.BlockSpec(block, lambda i, w: (jnp.maximum(i - blocks, 0), 0, 1 - w[2])),
            ],
            out_specs=pl.BlockSpec(block, lambda i, w: (i, 0, 0)),
        ),
        out_shape=jax.ShapeDtypeStruct((2 * blocks, tokens, columns // 2), jnp.bfloat16),
        compiler_params=params(),
    )(where, cache_k, cache_v)


def block_kernel(pieces, group_size, step, where_ref, place_ref, *refs):
    q_refs = refs[:pieces]
    id_refs = refs[pieces : 2 * pieces]
    own_k, own_v, next_k, next_v = refs[2 * pieces : 2 * pieces + 4]
    out_ref, logs_ref, s_ref = refs[-3:]
    kv = pl.program_id(1)
    share = q_refs[0].shape[0]
    items = share * pieces
    blocks, tokens, _ = own_k.shape
    lane = lax.broadcasted_iota(jnp.int32, (items, LANES), 1)
    first_head = kv * group_size
    mine = (lane >= first_head) & (lane < first_head + group_size)
    ids = stack([ref[...].astype(jnp.float32) for ref in id_refs])
    place = place_ref[...]
    block_ids = lax.broadcasted_iota(jnp.int32, place.shape, 1)
    keys = [ref.at[b] for ref in (own_k, next_k) for b in range(blocks)]
    values = [ref.at[b] for ref in (own_v, next_v) for b in range(blocks)]
    hits = []
    for base in (where_ref[0], where_ref[1]):
        for b in range(blocks):
            target = jnp.sum(
                jnp.where(place == base + b, block_ids, 0).astype(jnp.float32), axis=1, keepdims=True
            )
            hits.append(jnp.max(jnp.where(ids == target, 1.0, 0.0), axis=1, keepdims=True))
    some = hits[0]
    for hit in hits[1:]:
        some = jnp.maximum(some, hit)

    def write(head, out):
        start = pl.multiple_of((first_head + head) * HD, HD)
        out_ref[:, pl.ds(start, HD)] = out.astype(jnp.bfloat16)

    ones = jnp.ones((tokens, LANES), jnp.bfloat16)
    totals = jnp.ones((items, LANES), jnp.float32)
    for first in range(0, group_size, step):
        q = stack(
            [ref[:, h * HD : (h + 1) * HD] for h in range(first, first + step) for ref in q_refs]
        )
        acc = jnp.zeros((step * items, HD + LANES), jnp.float32)
        for hit, key, value in zip(hits, keys, values):
            p = jnp.exp2(dot_nt(q, key[...]) * (SCALE * LOG2E)).astype(jnp.bfloat16)
            both = jnp.concatenate([value[...], ones], axis=1)
            here = jnp.dot(p, both, preferred_element_type=jnp.float32)
            acc = jnp.where(stack([hit] * step) > 0.0, acc + here, acc)
        for n in range(step):
            total = acc[n * items : (n + 1) * items, HD:]
            out = acc[n * items : (n + 1) * items, :HD]
            write(first + n, jnp.where(some > 0.0, out / jnp.where(some > 0.0, total, 1.0), 0.0))
            totals = jnp.where(lane == first_head + first + n, total, totals)
    good = (totals > LOW) & (totals < HIGH)
    bad = jnp.max(jnp.where(good | (some == 0.0), 0.0, 1.0))
    logs = jnp.where((some > 0.0) & good, jnp.log(jnp.where(good, totals, 1.0)), NONE)
    logs_ref[...] = jnp.where(mine, logs, logs_ref[...])

    @pl.when(bad > 0.0)
    def _():
        @pl.loop(0, group_size)
        def _(head):
            start = pl.multiple_of(head * HD, HD)
            q = stack([ref[:, pl.ds(start, HD)] for ref in q_refs])
            top = jnp.full((items, 1), NONE, jnp.float32)
            for n, (hit, key) in enumerate(zip(hits, keys)):
                s = dot_nt(q, key[...])
                s_ref[n] = s
                here = jnp.max(s, axis=1, keepdims=True)
                top = jnp.where(hit > 0.0, jnp.maximum(top, here), top)
            acc = jnp.zeros((items, HD), jnp.float32)
            total = jnp.zeros((items, 1), jnp.float32)
            for n, (hit, value) in enumerate(zip(hits, values)):
                p = jnp.exp2((s_ref[n] - top) * (SCALE * LOG2E))
                p = jnp.where(hit > 0.0, p, 0.0)
                total += jnp.sum(p, axis=1, keepdims=True)
                acc += jnp.dot(p.astype(jnp.bfloat16), value[...], preferred_element_type=jnp.float32)
            safe = jnp.where(some > 0.0, total, 1.0)
            write(head, jnp.where(some > 0.0, acc / safe, 0.0))
            log = jnp.where(some > 0.0, top * SCALE + jnp.log(safe), NONE)
            logs_ref[...] = jnp.where(lane == first_head + head, log, logs_ref[...])

    @pl.when(kv == pl.num_programs(1) - 1)
    def _():
        heads = (out_ref.shape[1] - LANES) // HD
        parts = jnp.concatenate([x[:, :heads] for x in split3(logs_ref[...])], axis=1)
        pad = jnp.zeros((items, LANES - 3 * heads), jnp.bfloat16)
        out_ref[:, heads * HD :] = jnp.concatenate([parts, pad], axis=1)


def attend_blocks(where, place, queries, cache_k, cache_v, halves, group_size, after):
    pieces = len(queries)
    rows, columns = queries[0].shape
    blocks, tokens, kv_width = cache_k.shape
    kv_half = kv_width // HD // 2
    share = min(rows, 128)
    items = share * pieces
    own = pl.BlockSpec((blocks, tokens, HD), lambda i, g, w: (0, 0, w[2] * kv_half + g))
    queries_block = pl.BlockSpec((share, group_size * HD), lambda i, g, w: (i, g))
    ids_block = pl.BlockSpec((share, LANES), lambda i, g, w: (i, columns // LANES - 1))
    return pl.pallas_call(
        functools.partial(block_kernel, pieces, group_size, max(1, ROWS_STEP // items)),
        grid_spec=pltpu.PrefetchScalarGridSpec(
            num_scalar_prefetch=1,
            grid=(rows // share, kv_half),
            in_specs=[pl.BlockSpec(place.shape, lambda i, g, w: (0, 0))]
            + [queries_block] * pieces
            + [ids_block] * pieces
            + [own, own]
            + [
                pl.BlockSpec((blocks, tokens, HD), lambda i, g, w: (0, 0, g)),
                pl.BlockSpec((blocks, tokens, HD), lambda i, g, w: (1, 0, g)),
            ]
            + [pl.BlockSpec(memory_space=pl.ANY)] * len(after),
            out_specs=pl.BlockSpec((items, columns), lambda i, g, w: (i, 0)),
            scratch_shapes=[
                pltpu.VMEM((items, LANES), jnp.float32),
                pltpu.VMEM((2 * blocks, items, tokens), jnp.float32),
            ],
        ),
        out_shape=jax.ShapeDtypeStruct((rows * pieces, columns), jnp.bfloat16),
        compiler_params=params(),
        cost_estimate=pl.CostEstimate(
            flops=16 * rows * pieces * blocks * tokens * columns,
            bytes_accessed=8 * blocks * tokens * kv_half * HD + 4 * rows * pieces * columns,
            transcendentals=2 * rows * pieces * blocks * tokens * columns // HD,
        ),
    )(where, place, *queries, *queries, cache_k, cache_v, halves, halves, *after)


def suffix_kernel(group_size, lengths_ref, q_ref, k_ref, v_ref, out_ref, log_ref):
    rows_here, steps, width = q_ref.shape
    tokens = k_ref.shape[1]
    kv_here = k_ref.shape[2] // HD
    items = rows_here * steps
    span = rows_here * tokens
    half = width // HD // 2
    lane = lax.broadcasted_iota(jnp.int32, (items, LANES), 1)
    token = lax.broadcasted_iota(jnp.int32, (items, span), 1)
    item = lax.broadcasted_iota(jnp.int32, (items, span), 0)
    seen = jnp.zeros((items, span), jnp.float32)
    for r in range(rows_here):
        offset = token - r * tokens
        inside = (item // steps == r) & (offset >= 0) & (offset < lengths_ref[r] + item % steps)
        seen = jnp.where(inside, 1.0, seen)
    seen = jnp.concatenate([seen] * group_size, axis=0)
    logs = [jnp.zeros((items, LANES), jnp.float32)] * 2
    for g in range(kv_here):
        columns = slice(g * group_size * HD, (g + 1) * group_size * HD)
        q_all = flat(q_ref[:, :, columns]).astype(jnp.bfloat16)
        q = stack([q_all[:, n * HD : (n + 1) * HD] for n in range(group_size)])
        keys = k_ref[:, :, g * HD : (g + 1) * HD].reshape(span, HD)
        values = v_ref[:, :, g * HD : (g + 1) * HD].reshape(span, HD)
        s = jnp.where(seen > 0.0, dot_nt(q, keys), NONE)
        highest = jnp.max(s, axis=1, keepdims=True)
        p = jnp.exp2((s - highest) * (SCALE * LOG2E))
        p = jnp.where(seen > 0.0, p, 0.0)
        total = jnp.sum(p, axis=1, keepdims=True)
        out = jnp.dot(p.astype(jnp.bfloat16), values, preferred_element_type=jnp.float32) / total
        log = highest * SCALE + jnp.log(total)
        for n in range(group_size):
            h = g * group_size + n
            out_ref[:, h * HD : (h + 1) * HD] = out[n * items : (n + 1) * items]
            side = h // half
            logs[side] = jnp.where(lane == h % half, log[n * items : (n + 1) * items], logs[side])
    for side in range(2):
        log_ref[side] = logs[side]


def attend_suffix(lengths, queries, suffix_k, suffix_v):
    rows, steps, width = queries.shape
    _, tokens, kv_width = suffix_k.shape
    items = rows * steps
    whole = lambda i, n: (0, 0, 0)
    return pl.pallas_call(
        functools.partial(suffix_kernel, width // kv_width),
        grid_spec=pltpu.PrefetchScalarGridSpec(
            num_scalar_prefetch=1,
            grid=(1,),
            in_specs=[pl.BlockSpec(x.shape, whole) for x in (queries, suffix_k, suffix_v)],
            out_specs=[
                pl.BlockSpec((items, width), lambda i, n: (0, 0)),
                pl.BlockSpec((2, items, LANES), whole),
            ],
        ),
        out_shape=(
            jax.ShapeDtypeStruct((items, width), jnp.float32),
            jax.ShapeDtypeStruct((2, items, LANES), jnp.float32),
        ),
        compiler_params=params(),
        cost_estimate=pl.CostEstimate(
            flops=16 * items * rows * tokens * width,
            bytes_accessed=4 * suffix_k.size + 6 * items * width,
            transcendentals=items * rows * tokens * width // HD,
        ),
    )(lengths, queries, suffix_k, suffix_v)


def merge_kernel(arrays, *refs):
    back_refs = refs[:arrays]
    out_refs = refs[arrays:]
    items = out_refs[0].shape[0]
    columns = out_refs[0].shape[1] - LANES
    heads = columns // HD
    for side, out_ref in enumerate(out_refs):
        parts = [
            (ref, start + side * items)
            for ref in back_refs
            for start in range(0, ref.shape[0], 2 * items)
        ]
        logs = []
        for ref, start in parts:
            x = ref[start : start + items, columns:].astype(jnp.float32)
            logs.append(x[:, :heads] + x[:, heads : 2 * heads] + x[:, 2 * heads : 3 * heads])
        top = logs[0]
        for log in logs[1:]:
            top = jnp.maximum(top, log)
        factors = [jnp.exp(log - top) for log in logs]
        total = factors[0]
        for factor in factors[1:]:
            total += factor
        inverse = 1.0 / total
        factors = [factor * inverse for factor in factors]
        for h in range(heads):
            span = slice(h * HD, (h + 1) * HD)
            acc = jnp.zeros((items, HD), jnp.float32)
            for factor, (ref, start) in zip(factors, parts):
                acc += factor[:, h : h + 1] * ref[start : start + items, span].astype(jnp.float32)
            out_ref[:, span] = acc
        log = top + jnp.log(total)
        pad = jnp.zeros((items, LANES - heads), jnp.float32)
        out_ref[:, columns:] = jnp.concatenate([log, pad], axis=1)


def merge(back, items):
    shape = jax.ShapeDtypeStruct((items, back[0].shape[1]), jnp.float32)
    return pl.pallas_call(
        functools.partial(merge_kernel, len(back)),
        out_shape=[shape, shape],
        compiler_params=params(),
    )(*back)


def finish_kernel(where_ref, mine_ref, other_ref, out_s_ref, log_s_ref, out_ref):
    items = mine_ref.shape[0]
    columns = mine_ref.shape[1] - LANES
    heads = columns // HD
    rows, steps, _ = out_ref.shape
    core = where_ref[2]
    for ref, which in ((mine_ref, core), (other_ref, 1 - core)):
        log = ref[:, columns:]
        log_s = log_s_ref[which]
        top = jnp.maximum(log, log_s)
        factor = jnp.exp(log - top)
        factor_s = jnp.exp(log_s - top)
        inverse = 1.0 / (factor + factor_s)
        factor, factor_s = factor * inverse, factor_s * inverse
        for h in range(heads):
            start = pl.multiple_of(which * columns + h * HD, HD)
            out = factor[:, h : h + 1] * ref[:, h * HD : (h + 1) * HD]
            out += factor_s[:, h : h + 1] * out_s_ref[:, pl.ds(start, HD)]
            for row in range(rows):
                part = out[row * steps : (row + 1) * steps]
                out_ref[row, :, pl.ds(start, HD)] = part.astype(jnp.bfloat16)


def finish(where, mine, other, out_s, log_s, shape):
    flat_map = lambda i, w: (0, 0)
    return pl.pallas_call(
        finish_kernel,
        grid_spec=pltpu.PrefetchScalarGridSpec(
            num_scalar_prefetch=1,
            grid=(1,),
            in_specs=[pl.BlockSpec(x.shape, flat_map) for x in (mine, other, out_s)]
            + [pl.BlockSpec(log_s.shape, lambda i, w: (0, 0, 0))],
            out_specs=pl.BlockSpec(shape, lambda i, w: (0, 0, 0)),
        ),
        out_shape=jax.ShapeDtypeStruct(shape, jnp.bfloat16),
        compiler_params=params(),
    )(where, mine, other, out_s, log_s)


def local(queries, selected, placement, lengths, cache_k, cache_v, suffix_k, suffix_v):
    rows_here, steps, width = queries.shape
    size = lax.axis_size("ctx")
    blocks_here, _, kv_width = cache_k.shape
    group_size = width // kv_width
    items = rows_here * steps
    chips = size // 2

    def swap(x, bits):
        return lax.ppermute(x, "ctx", [(i, i ^ bits) for i in range(size)])

    own = lax.axis_index("ctx")
    where = jnp.stack([own * blocks_here, (own ^ 1) * blocks_here, own & 1]).astype(jnp.int32)
    place = placement.reshape(1, -1)
    halves = swap(halve(where, cache_k, cache_v), 1)
    mine, other = pack(where, queries, selected)
    out_s, log_s = attend_suffix(lengths, queries, suffix_k, suffix_v)
    attend = functools.partial(attend_blocks, where, place)
    if chips <= 4:
        order = [2, 3, 1, 0] if chips == 4 else list(range(chips - 1, -1, -1))
        arrived = {k: [swap(mine, 2 * k) if k else mine, swap(other, 2 * k + 1)] for k in order}
        back = []
        after = [log_s]
        for k in order:
            partial = attend(arrived[k], cache_k, cache_v, halves, group_size, after)
            after = [partial]
            back.append(swap(partial, 2 * k) if k else partial)
    else:
        same = [[2 * z + core for z in range(chips)] for core in range(2)]
        chip = jnp.concatenate([mine, swap(other, 1)], axis=0)
        every = lax.all_gather(chip, "ctx", axis=0, tiled=True, axis_index_groups=same)
        partial = attend([every], cache_k, cache_v, halves, group_size, [log_s])
        back = [
            lax.all_to_all(
                partial, "ctx", split_axis=0, concat_axis=0, tiled=True, axis_index_groups=same
            )
        ]
    keep, send = merge(back, items)
    return finish(where, keep, swap(send, 1), out_s, log_s, queries.shape)


def solution(mesh):
    rows = P(("groups", "ctx"), None, "rows")
    in_specs = (
        rows,
        P(("groups", "ctx"), None, None),
        P("groups"),
        P(("groups", "ctx")),
        rows,
        rows,
        rows,
        rows,
    )
    return jax.shard_map(local, mesh=mesh, in_specs=in_specs, out_specs=rows, check_vma=False)
```

time: 121 us -> 175 us (1.45)
  Pallas kernels: 76.7 us -> 151 us
  starting transfers between devices: 29.9 us -> 16.1 us
  waiting for transfers between devices: 10.9 us -> 1.6 us
  local copies, waits for them, and re-layouts: 2.05 us -> 5.92 us
    pallas_call x6 -> x9, Pallas kernels: 76.7 us -> 151 us  [the longest x4 132 us: attend_blocks(): pl.pallas_call(functools.partial(block_kernel, pieces, group_size, max(1,...]
    ppermute x28 -> x12, starting transfers between devices: 29.9 us -> 16.1 us  [swap(): return lax.ppermute(x, 'ctx', [(i, i ^ bits) for i in range(size)])]
    ppermute x28 -> x12, waiting for transfers between devices: 10.9 us -> 1.6 us  [swap(): return lax.ppermute(x, 'ctx', [(i, i ^ bits) for i in range(size)])]
    unnamed x62 -> x24, local copies, waits for them, and re-layouts: 1.38 us -> 5.92 us
  transfers between devices with their start and end apart: 28 -> 12, of which waited for: 5 -> 1; matrix products, arithmetic and copies ran while one was open for 1% -> 0% of each run, Pallas kernels for 60% -> 79%
where the time goes in v3:
time: 175 us
  Pallas kernels  151 us (86%)
  starting transfers between devices  16.1 us (9%)
  local copies, waits for them, and re-layouts  5.92 us (3%)
    pallas_call x4, Pallas kernels, attend_blocks(): pl.pallas_call(functools.partial(block_kernel, pieces, group_size, max(1,...  132 us
    ppermute x12, starting transfers between devices, swap(): return lax.ppermute(x, 'ctx', [(i, i ^ bits) for i in range(size)])  16.1 us
    pallas_call x1, Pallas kernels, halve(): pl.pallas_call(functools.partial(halve_kernel, blocks), grid_spec=pltpu.P...  7.79 us
    unnamed x24, local copies, waits for them, and re-layouts  5.92 us
    pallas_call x1, Pallas kernels, attend_suffix(): pl.pallas_call(functools.partial(suffix_kernel, width // kv_width), grid_...  3.81 us
  transfers between devices with their start and end apart: 12, of which 1 were waited for; matrix products, arithmetic and copies ran while one was open for 0% of the time, Pallas kernels for 79%

profile of v3, /device:TPU:0, one launch (start us, length us, event | category | flops | bytes accessed | tf_op | source)
XLA Modules:
  0.0 174.9 jit_solution(7965086638076818285)
XLA Ops:
  0.0 0.7 pad_add_fusion.where_ref
  0.7 7.8 %shard_map.83 = bf16[8,1024,256]{2,1,0:T(8,128)(2,1)} custom-call(s32[3]{0:T(128)} %pad_add_fusion.where_ref, bf16[4,1024,512]{2,1,0:T(8,128)(2,1)} %refs_4_.7, bf16[4,1024,512]{2,1,0:T(8,128)(2,1)} %refs_5_.7), custom_call_target="tpu_custom_call" | custom-call | tf_op jit(solution)/shard_map/pallas_call | solution.py:87
  8.9 2.2 %shard_map.82 = (bf16[16,2176]{1,0:T(8,128)(2,1)}, bf16[16,2176]{1,0:T(8,128)(2,1)}) custom-call(s32[3]{0:T(128)} %pad_add_fusion.where_ref, bf16[4,4,4096]{2,1,0:T(4,128)(2,1)} %q_ref.3, s32[4,4,16]{2,1,0:T(4,128)} %selected_ref.1), custom_call_target="tpu_custom_call" | custom-call | tf_op jit(solution)/shard_map/pallas_call | solution.py:61
  11.1 3.6 %collective-permute-start = (bf16[16,2176]{1,0:T(8,128)(2,1)}, bf16[16,2176]{1,0:T(8,128)(2,1)S(1)}, u32[]{:S(2)}, u32[]{:S(2)}) collective-permute-start(bf16[16,2176]{1,0:T(8,128)(2,1)} %get-tuple-element.11.refs_0_.refs_2_), channel_id=1, source_target_pairs={{0,8},{2,10},{4,12},{6,14},{8,0},{10,2},{12,4},{14,6},{1,9},{3,11}... | collective-permute-start | bytes 208904 | tf_op jit(solution)/shard_map/ppermute | solution.py:390
  14.9 3.6 %collective-permute-start.4 = (bf16[16,2176]{1,0:T(8,128)(2,1)}, bf16[16,2176]{1,0:T(8,128)(2,1)S(1)}, u32[]{:S(2)}, u32[]{:S(2)}) collective-permute-start(bf16[16,2176]{1,0:T(8,128)(2,1)} %get-tuple-element.11.refs_0_.refs_2_), channel_id=1, source_target_pairs={{0,12},{2,14},{4,8},{6,10},{8,4},{10,6},{12,0},{14,2},{1,13},{3,15... | collective-permute-start | bytes 208904 | tf_op jit(solution)/shard_map/ppermute | solution.py:390
  18.5 3.8 %shard_map.84 = (f32[16,4096]{1,0:T(8,128)}, f32[2,16,128]{2,1,0:T(8,128)}) custom-call(s32[4]{0:T(128)} %lengths_ref.1, bf16[4,4,4096]{2,1,0:T(4,128)(2,1)} %q_ref.3, bf16[4,128,512]{2,1,0:T(8,128)(2,1)} %k_ref.3, bf16[4,128,512]{2,1,0:T(8,128)(2,1)} %v_ref.3), custom_call_target="tpu_custom_call" | custom-call | flops 536870912 | bytes 1441792 | tf_op jit(solution)/shard_map/pallas_call | solution.py:273
  22.3 2.3 %collective-permute-start.7 = (bf16[16,2176]{1,0:T(8,128)(2,1)}, bf16[16,2176]{1,0:T(8,128)(2,1)S(1)}, u32[]{:S(2)}, u32[]{:S(2)}) collective-permute-start(bf16[16,2176]{1,0:T(8,128)(2,1)} %get-tuple-element.11.refs_0_.refs_2_), channel_id=1, source_target_pairs={{0,4},{2,6},{4,0},{6,2},{8,12},{10,14},{12,8},{14,10},{1,5},{3,7},... | collective-permute-start | bytes 208904 | tf_op jit(solution)/shard_map/ppermute | solution.py:390
  24.6 1.1 collective-permute-start.8
  26.2 1.5 copy-done
  27.7 32.8 %shard_map.85.refs_8_ = bf16[32,2176]{1,0:T(8,128)(2,1)} custom-call(s32[3]{0:T(128)} %pad_add_fusion.where_ref, s32[1,32]{1,0:T(1,128)} %bitcast.4, bf16[16,2176]{1,0:T(8,128)(2,1)} %copy-done.6, bf16[16,2176]{1,0:T(8,128)(2,1)} %copy-done.7, bf16[16,2176]{1,0:T(8,128)(2,1)} %copy-done.6, bf16[16,2176]{1,0:T(8,128)(2,1)} %copy-done.7, ...), custom_call_target="tpu_custom_call" | custom-call | flops 4563402752 | bytes 8667136 | tf_op jit(solution)/shard_map/pallas_call | solution.py:199
  60.6 3.3 %collective-permute-start.3 = (bf16[32,2176]{1,0:T(8,128)(2,1)}, bf16[32,2176]{1,0:T(8,128)(2,1)S(1)}, u32[]{:S(2)}, u32[]{:S(2)}) collective-permute-start(bf16[32,2176]{1,0:T(8,128)(2,1)} %shard_map.85.refs_8_), channel_id=1, source_target_pairs={{0,8},{2,10},{4,12},{6,14},{8,0},{10,2},{12,4},{14,6},{1,9},{3,11}... | collective-permute-start | bytes 417800 | tf_op jit(solution)/shard_map/ppermute | solution.py:390
  63.9 0.6 copy-done.3
  64.5 32.8 %shard_map.86.refs_8_ = bf16[32,2176]{1,0:T(8,128)(2,1)} custom-call(s32[3]{0:T(128)} %pad_add_fusion.where_ref, s32[1,32]{1,0:T(1,128)} %bitcast.5, bf16[16,2176]{1,0:T(8,128)(2,1)} %copy-done.1, bf16[16,2176]{1,0:T(8,128)(2,1)} %copy-done.3, bf16[16,2176]{1,0:T(8,128)(2,1)} %copy-done.1, bf16[16,2176]{1,0:T(8,128)(2,1)} %copy-done.3, ...), custom_call_target="tpu_custom_call" | custom-call | flops 4563402752 | bytes 8667136 | tf_op jit(solution)/shard_map/pallas_call | solution.py:199
  97.6 0.6 copy-done.2
  98.2 0.6 copy-done.5
  98.9 33.0 %shard_map.87.refs_8_ = bf16[32,2176]{1,0:T(8,128)(2,1)} custom-call(s32[3]{0:T(128)} %pad_add_fusion.where_ref, s32[1,32]{1,0:T(1,128)} %bitcast.6, bf16[16,2176]{1,0:T(8,128)(2,1)} %copy-done.2, bf16[16,2176]{1,0:T(8,128)(2,1)} %copy-done.5, bf16[16,2176]{1,0:T(8,128)(2,1)} %copy-done.2, bf16[16,2176]{1,0:T(8,128)(2,1)} %copy-done.5, ...), custom_call_target="tpu_custom_call" | custom-call | flops 4563402752 | bytes 8667136 | tf_op jit(solution)/shard_map/pallas_call | solution.py:199
  131.9 0.8 collective-permute-start.9
  132.7 0.6 copy-done.4
  133.4 32.9 %shard_map.88.refs_3_ = bf16[32,2176]{1,0:T(8,128)(2,1)} custom-call(s32[3]{0:T(128)} %pad_add_fusion.where_ref, s32[1,32]{1,0:T(1,128)} %bitcast.7, bf16[16,2176]{1,0:T(8,128)(2,1)} %get-tuple-element.11.refs_0_.refs_2_, bf16[16,2176]{1,0:T(8,128)(2,1)} %copy-done.4, bf16[16,2176]{1,0:T(8,128)(2,1)} %get-tuple-element.11.refs_0_.refs_2_, ...), custom_call_target="tpu_custom_call" | custom-call | flops 4563402752 | bytes 8667136 | tf_op jit(solution)/shard_map/pallas_call | solution.py:199
  166.9 0.6 copy-done.8
  167.6 2.4 %shard_map.89 = (f32[16,2176]{1,0:T(8,128)}, f32[16,2176]{1,0:T(8,128)}) custom-call(bf16[32,2176]{1,0:T(8,128)(2,1)} %copy-done.8, bf16[32,2176]{1,0:T(8,128)(2,1)} %copy-done.9, bf16[32,2176]{1,0:T(8,128)(2,1)} %copy-done.10, bf16[32,2176]{1,0:T(8,128)(2,1)} %shard_map.88.refs_3_), custom_call_target="tpu_custom_call" | custom-call | tf_op jit(solution)/shard_map/pallas_call | solution.py:335
  170.0 1.6 collective-permute-done.11.other_ref
  171.6 0.7 copy-done.11
  172.2 2.7 %shard_map.90 = bf16[4,4,4096]{2,1,0:T(4,128)(2,1)} custom-call(s32[3]{0:T(128)} %pad_add_fusion.where_ref, f32[16,2176]{1,0:T(8,128)} %get-tuple-element.14.mine_ref, f32[16,2176]{1,0:T(8,128)} %copy-done.11, f32[16,4096]{1,0:T(8,128)} %get-tuple-element.16.out_s_ref, f32[2,16,128]{2,1,0:T(8,128)} %get-tuple-element.13.refs_8_.log_s_ref), custom_call_target="tpu_custom_call" | custom-call | tf_op jit(solution)/shard_map/pallas_call | solution.py:367
  (34 shorter events, 2.1 us)
Async XLA Ops:
  8.5 17.3 %collective-permute-start.2 = (bf16[8,1024,256]{2,1,0:T(8,128)(2,1)}, bf16[8,1024,256]{2,1,0:T(8,128)(2,1)S(1)}, u32[]{:S(2)}, u32[]{:S(2)}) collective-permute-start(bf16[8,1024,256]{2,1,0:T(8,128)(2,1)} %shard_map.83), channel_id=1, source_target_pairs={{0,2},{2,0},{4,6},{6,4},{8,10},{10,8},{12,14},{14,12},{1,3},{3,1},... | collective-permute-start | bytes 12582920 | tf_op jit(solution)/shard_map/ppermute | solution.py:390
  11.1 11.2 %collective-permute-start = (bf16[16,2176]{1,0:T(8,128)(2,1)}, bf16[16,2176]{1,0:T(8,128)(2,1)S(1)}, u32[]{:S(2)}, u32[]{:S(2)}) collective-permute-start(bf16[16,2176]{1,0:T(8,128)(2,1)} %get-tuple-element.11.refs_0_.refs_2_), channel_id=1, source_target_pairs={{0,8},{2,10},{4,12},{6,14},{8,0},{10,2},{12,4},{14,6},{1,9},{3,11}... | collective-permute-start | bytes 208904 | tf_op jit(solution)/shard_map/ppermute | solution.py:390
  14.7 9.9 %collective-permute-start.1 = (bf16[16,2176]{1,0:T(8,128)(2,1)}, bf16[16,2176]{1,0:T(8,128)(2,1)S(1)}, u32[]{:S(2)}, u32[]{:S(2)}) collective-permute-start(bf16[16,2176]{1,0:T(8,128)(2,1)} %get-tuple-element.12), channel_id=1, source_target_pairs={{0,10},{2,8},{4,14},{6,12},{8,2},{10,0},{12,6},{14,4},{1,11},{3,9}... | collective-permute-start | bytes 208904 | tf_op jit(solution)/shard_map/ppermute | solution.py:390
  14.9 45.7 %collective-permute-start.4 = (bf16[16,2176]{1,0:T(8,128)(2,1)}, bf16[16,2176]{1,0:T(8,128)(2,1)S(1)}, u32[]{:S(2)}, u32[]{:S(2)}) collective-permute-start(bf16[16,2176]{1,0:T(8,128)(2,1)} %get-tuple-element.11.refs_0_.refs_2_), channel_id=1, source_target_pairs={{0,12},{2,14},{4,8},{6,10},{8,4},{10,6},{12,0},{14,2},{1,13},{3,15... | collective-permute-start | bytes 208904 | tf_op jit(solution)/shard_map/ppermute | solution.py:390
  18.5 45.4 %collective-permute-start.5 = (bf16[16,2176]{1,0:T(8,128)(2,1)}, bf16[16,2176]{1,0:T(8,128)(2,1)S(1)}, u32[]{:S(2)}, u32[]{:S(2)}) collective-permute-start(bf16[16,2176]{1,0:T(8,128)(2,1)} %get-tuple-element.12), channel_id=1, source_target_pairs={{0,14},{2,12},{4,10},{6,8},{8,6},{10,4},{12,2},{14,0},{1,15},{3,13... | collective-permute-start | bytes 208904 | tf_op jit(solution)/shard_map/ppermute | solution.py:390
  22.3 3.9 %copy-start.6 = (bf16[16,2176]{1,0:T(8,128)(2,1)}, bf16[16,2176]{1,0:T(8,128)(2,1)S(1)}, u32[]{:S(2)}) copy-start(bf16[16,2176]{1,0:T(8,128)(2,1)S(1)} %collective-permute-done.refs_0_.refs_2_) | copy-start | bytes 208900
  22.3 75.3 %collective-permute-start.7 = (bf16[16,2176]{1,0:T(8,128)(2,1)}, bf16[16,2176]{1,0:T(8,128)(2,1)S(1)}, u32[]{:S(2)}, u32[]{:S(2)}) collective-permute-start(bf16[16,2176]{1,0:T(8,128)(2,1)} %get-tuple-element.11.refs_0_.refs_2_), channel_id=1, source_target_pairs={{0,4},{2,6},{4,0},{6,2},{8,12},{10,14},{12,8},{14,10},{1,5},{3,7},... | collective-permute-start | bytes 208904 | tf_op jit(solution)/shard_map/ppermute | solution.py:390
  24.6 1.6 copy-start.7
  24.6 73.0 %collective-permute-start.8 = (bf16[16,2176]{1,0:T(8,128)(2,1)}, bf16[16,2176]{1,0:T(8,128)(2,1)S(1)}, u32[]{:S(2)}, u32[]{:S(2)}) collective-permute-start(bf16[16,2176]{1,0:T(8,128)(2,1)} %get-tuple-element.12), channel_id=1, source_target_pairs={{0,6},{2,4},{4,2},{6,0},{8,14},{10,12},{12,10},{14,8},{1,7},{3,5},... | collective-permute-start | bytes 208904 | tf_op jit(solution)/shard_map/ppermute | solution.py:390
  25.8 1.9 %copy-start = (bf16[8,1024,256]{2,1,0:T(8,128)(2,1)}, bf16[8,1024,256]{2,1,0:T(8,128)(2,1)S(1)}, u32[]{:S(2)}) copy-start(bf16[8,1024,256]{2,1,0:T(8,128)(2,1)S(1)} %collective-permute-done.2.refs_6_.refs_7_) | copy-start | bytes 12582916
  25.8 107.0 %collective-permute-start.10 = (bf16[16,2176]{1,0:T(8,128)(2,1)}, bf16[16,2176]{1,0:T(8,128)(2,1)S(1)}, u32[]{:S(2)}, u32[]{:S(2)}) collective-permute-start(bf16[16,2176]{1,0:T(8,128)(2,1)} %get-tuple-element.12), channel_id=1, source_target_pairs={{0,2},{2,0},{4,6},{6,4},{8,10},{10,8},{12,14},{14,12},{1,3},{3,1},... | collective-permute-start | bytes 208904 | tf_op jit(solution)/shard_map/ppermute | solution.py:390
  60.6 3.4 %copy-start.1 = (bf16[16,2176]{1,0:T(8,128)(2,1)}, bf16[16,2176]{1,0:T(8,128)(2,1)S(1)}, u32[]{:S(2)}) copy-start(bf16[16,2176]{1,0:T(8,128)(2,1)S(1)} %collective-permute-done.4.refs_0_.refs_2_) | copy-start | bytes 208900
  60.6 105.7 %collective-permute-start.3 = (bf16[32,2176]{1,0:T(8,128)(2,1)}, bf16[32,2176]{1,0:T(8,128)(2,1)S(1)}, u32[]{:S(2)}, u32[]{:S(2)}) collective-permute-start(bf16[32,2176]{1,0:T(8,128)(2,1)} %shard_map.85.refs_8_), channel_id=1, source_target_pairs={{0,8},{2,10},{4,12},{6,14},{8,0},{10,2},{12,4},{14,6},{1,9},{3,11}... | collective-permute-start | bytes 417800 | tf_op jit(solution)/shard_map/ppermute | solution.py:390
  63.9 0.6 copy-start.3
  97.4 68.9 %collective-permute-start.6 = (bf16[32,2176]{1,0:T(8,128)(2,1)}, bf16[32,2176]{1,0:T(8,128)(2,1)S(1)}, u32[]{:S(2)}, u32[]{:S(2)}) collective-permute-start(bf16[32,2176]{1,0:T(8,128)(2,1)} %shard_map.86.refs_8_), channel_id=1, source_target_pairs={{0,12},{2,14},{4,8},{6,10},{8,4},{10,6},{12,0},{14,2},{1,13},{3,15... | collective-permute-start | bytes 417800 | tf_op jit(solution)/shard_map/ppermute | solution.py:390
  97.6 0.6 copy-start.2
  98.2 0.6 copy-start.5
  131.9 34.3 %collective-permute-start.9 = (bf16[32,2176]{1,0:T(8,128)(2,1)}, bf16[32,2176]{1,0:T(8,128)(2,1)S(1)}, u32[]{:S(2)}, u32[]{:S(2)}) collective-permute-start(bf16[32,2176]{1,0:T(8,128)(2,1)} %shard_map.87.refs_8_), channel_id=1, source_target_pairs={{0,4},{2,6},{4,0},{6,2},{8,12},{10,14},{12,8},{14,10},{1,5},{3,7},... | collective-permute-start | bytes 417800 | tf_op jit(solution)/shard_map/ppermute | solution.py:390
  132.7 0.6 copy-start.4
  166.2 0.7 copy-start.10
  166.2 0.7 copy-start.9
  166.9 0.6 copy-start.8
  170.0 1.6 collective-permute-start.11
  171.6 0.7 copy-start.11

commit v4 on v3

v4 whole, which is shorter than its diff:
```python
import functools
import math

import jax
import jax.numpy as jnp
from jax import lax
from jax.experimental import pallas as pl
from jax.experimental.pallas import tpu as pltpu
from jax.sharding import PartitionSpec as P

HD = 128
LANES = 128
SCALE = 1.0 / math.sqrt(HD)
LOG2E = math.log2(math.e)
NONE = -1e30
LOW, HIGH = 2.0**-80, 2.0**100
VMEM = 60 * 1024 * 1024
ROWS_STEP = 512


def split3(x):
    high = x.astype(jnp.bfloat16)
    rest = x - high.astype(jnp.float32)
    middle = rest.astype(jnp.bfloat16)
    low = (rest - middle.astype(jnp.float32)).astype(jnp.bfloat16)
    return high, middle, low


def dot_nt(a, b):
    return lax.dot_general(a, b, (((1,), (1,)), ((), ())), preferred_element_type=jnp.float32)


def stack(arrays):
    return arrays[0] if len(arrays) == 1 else jnp.concatenate(arrays, axis=0)


def params():
    return pltpu.CompilerParams(vmem_limit_bytes=VMEM)


def flat(x):
    return x.astype(jnp.float32).reshape(x.shape[0] * x.shape[1], x.shape[2])


ANY = pl.BlockSpec(memory_space=pl.ANY)


def pack_kernel(q_ref, selected_ref, mine_ref, other_ref):
    half = q_ref.shape[2] // 2
    core = lax.axis_index("ctx") % 2
    ids = flat(selected_ref[...])
    pad = jnp.full((ids.shape[0], LANES - ids.shape[1]), -1.0, jnp.float32)
    ids = jnp.concatenate([ids, pad], axis=1).astype(jnp.bfloat16)
    for ref, which in ((mine_ref, core), (other_ref, 1 - core)):
        start = pl.multiple_of(which * half, LANES)
        ref[:, :half] = flat(q_ref[:, :, pl.ds(start, half)]).astype(jnp.bfloat16)
        ref[:, half:] = ids


def pack(queries, selected):
    rows, steps, width = queries.shape
    shape = jax.ShapeDtypeStruct((rows * steps, width // 2 + LANES), jnp.bfloat16)
    return pl.pallas_call(pack_kernel, out_shape=[shape, shape], compiler_params=params())(
        queries, selected
    )


def halve_kernel(k_ref, v_ref, out_ref, sems):
    blocks, _, columns = k_ref.shape
    half = columns // 2
    start = pl.multiple_of((1 - lax.axis_index("ctx") % 2) * half, LANES)
    copies = [
        pltpu.make_async_copy(
            ref.at[b, :, pl.ds(start, half)], out_ref.at[n * blocks + b], sems.at[n * blocks + b]
        )
        for n, ref in enumerate((k_ref, v_ref))
        for b in range(blocks)
    ]
    for copy in copies:
        copy.start()
    for copy in copies:
        copy.wait()


def halve(cache_k, cache_v):
    blocks, tokens, columns = cache_k.shape
    return pl.pallas_call(
        halve_kernel,
        in_specs=[ANY, ANY],
        out_specs=ANY,
        out_shape=jax.ShapeDtypeStruct((2 * blocks, tokens, columns // 2), jnp.bfloat16),
        scratch_shapes=[pltpu.SemaphoreType.DMA((2 * blocks,))],
        compiler_params=params(),
    )(cache_k, cache_v)


def block_kernel(pieces, group_size, step, tiles, place_ref, *refs):
    q_refs = refs[:pieces]
    own_k, own_v, next_kv = refs[pieces : pieces + 3]
    out_refs = refs[-pieces - 7 : -7]
    q_ref, k_ref, v_ref, logs_ref, s_ref, sems, q_sems = refs[-7:]
    share = out_refs[0].shape[0]
    items, width = q_ref.shape
    columns = width - LANES
    kv_half, both_blocks, tokens, _ = k_ref.shape
    blocks = both_blocks // 2
    own = lax.axis_index("ctx")
    core = own % 2
    tile = pl.program_id(0)

    copies = {}
    for g in range(kv_half):
        mine = pl.ds(pl.multiple_of((core * kv_half + g) * HD, HD), HD)
        other = slice(g * HD, (g + 1) * HD)
        for b in range(both_blocks):
            if b < blocks:
                sources = own_k.at[b, :, mine], own_v.at[b, :, mine]
            else:
                sources = next_kv.at[b - blocks, :, other], next_kv.at[b, :, other]
            for n, (source, held) in enumerate(zip(sources, (k_ref, v_ref))):
                copies[g, b, n] = pltpu.make_async_copy(source, held.at[g, b], sems.at[g, b, n])
    q_copies = [
        pltpu.make_async_copy(
            ref.at[pl.ds(pl.multiple_of(tile * share, share), share)],
            q_ref.at[n * share : (n + 1) * share],
            q_sems.at[n],
        )
        for n, ref in enumerate(q_refs)
    ]

    def first_time(action):
        if tiles == 1:
            action()
        else:
            pl.when(tile == 0)(action)

    for copy in q_copies:
        copy.start()

    def start_all():
        for g in range(kv_half):
            for b in range(both_blocks):
                for n in range(2):
                    copies[g, b, n].start()

    first_time(start_all)
    for copy in q_copies:
        copy.wait()

    lane = lax.broadcasted_iota(jnp.int32, (items, LANES), 1)
    ids = q_ref[:, columns:].astype(jnp.float32)
    place = place_ref[...]
    block_ids = lax.broadcasted_iota(jnp.int32, place.shape, 1)
    hits = []
    for owner in (own, own + 1 - 2 * core):
        for b in range(blocks):
            target = jnp.sum(
                jnp.where(place == owner * blocks + b, block_ids, 0).astype(jnp.float32),
                axis=1,
                keepdims=True,
            )
            hits.append(jnp.max(jnp.where(ids == target, 1.0, 0.0), axis=1, keepdims=True))
    some = hits[0]
    for hit in hits[1:]:
        some = jnp.maximum(some, hit)

    def write(head, out):
        start = pl.multiple_of(head * HD, HD) if not isinstance(head, int) else head * HD
        out = out.astype(jnp.bfloat16)
        for n, ref in enumerate(out_refs):
            ref[:, pl.ds(start, HD)] = out[n * share : (n + 1) * share]

    ones = jnp.ones((tokens, LANES), jnp.bfloat16)
    totals = jnp.ones((items, LANES), jnp.float32)
    units = [
        (g, first, b)
        for g in range(kv_half)
        for first in range(0, group_size, step)
        for b in range(both_blocks)
    ]

    def scores(g, first, b):
        if first == 0:

            def ready():
                copies[g, b, 0].wait()
                copies[g, b, 1].wait()

            first_time(ready)
        heads = range(g * group_size + first, g * group_size + first + step)
        q = stack([q_ref[:, h * HD : (h + 1) * HD] for h in heads])
        return dot_nt(q, k_ref[g, b])

    s = scores(*units[0])
    acc = None
    for n, (g, first, b) in enumerate(units):
        following = scores(*units[n + 1]) if n + 1 < len(units) else None
        p = jnp.exp2(s * (SCALE * LOG2E)).astype(jnp.bfloat16)
        values = jnp.concatenate([v_ref[g, b], ones], axis=1)
        here = jnp.dot(p, values, preferred_element_type=jnp.float32)
        hit = stack([hits[b]] * step) > 0.0
        acc = jnp.where(hit, here if b == 0 else acc + here, 0.0 if b == 0 else acc)
        s = following
        if b == both_blocks - 1:
            for m in range(step):
                head = g * group_size + first + m
                total = acc[m * items : (m + 1) * items, HD:]
                out = acc[m * items : (m + 1) * items, :HD]
                write(head, jnp.where(some > 0.0, out / jnp.where(some > 0.0, total, 1.0), 0.0))
                totals = jnp.where(lane == head, total, totals)
    good = (totals > LOW) & (totals < HIGH)
    bad = jnp.max(jnp.where(good | (some == 0.0), 0.0, 1.0))
    logs = jnp.where((some > 0.0) & good, jnp.log(jnp.where(good, totals, 1.0)), NONE)
    logs_ref[...] = logs

    @pl.when(bad > 0.0)
    def _():
        @pl.loop(0, kv_half * group_size)
        def _(head):
            g = head // group_size
            q = q_ref[:, pl.ds(pl.multiple_of(head * HD, HD), HD)]
            top = jnp.full((items, 1), NONE, jnp.float32)
            for n, hit in enumerate(hits):
                s = dot_nt(q, k_ref[g, n])
                s_ref[n] = s
                here = jnp.max(s, axis=1, keepdims=True)
                top = jnp.where(hit > 0.0, jnp.maximum(top, here), top)
            acc = jnp.zeros((items, HD), jnp.float32)
            total = jnp.zeros((items, 1), jnp.float32)
            for n, hit in enumerate(hits):
                p = jnp.exp2((s_ref[n] - top) * (SCALE * LOG2E))
                p = jnp.where(hit > 0.0, p, 0.0)
                total += jnp.sum(p, axis=1, keepdims=True)
                acc += jnp.dot(p.astype(jnp.bfloat16), v_ref[g, n], preferred_element_type=jnp.float32)
            safe = jnp.where(some > 0.0, total, 1.0)
            write(head, jnp.where(some > 0.0, acc / safe, 0.0))
            log = jnp.where(some > 0.0, top * SCALE + jnp.log(safe), NONE)
            logs_ref[...] = jnp.where(lane == head, log, logs_ref[...])

    heads = columns // HD
    parts = jnp.concatenate([x[:, :heads] for x in split3(logs_ref[...])], axis=1)
    pad = jnp.zeros((items, LANES - 3 * heads), jnp.bfloat16)
    parts = jnp.concatenate([parts, pad], axis=1)
    for n, ref in enumerate(out_refs):
        ref[:, columns:] = parts[n * share : (n + 1) * share]


def attend_blocks(place, queries, cache_k, cache_v, halves, group_size, after):
    pieces = len(queries)
    rows, columns = queries[0].shape
    blocks, tokens, kv_width = cache_k.shape
    kv_half = kv_width // HD // 2
    share = min(rows, 64)
    items = share * pieces
    tiles = rows // share
    step = min(group_size, max(1, ROWS_STEP // items))
    return pl.pallas_call(
        functools.partial(block_kernel, pieces, group_size, step, tiles),
        grid=(tiles,),
        in_specs=[pl.BlockSpec(place.shape, lambda i: (0, 0))] + [ANY] * (pieces + 3 + len(after)),
        out_specs=[pl.BlockSpec((share, columns), lambda i: (i, 0))] * pieces,
        out_shape=[jax.ShapeDtypeStruct((rows, columns), jnp.bfloat16)] * pieces,
        scratch_shapes=[
            pltpu.VMEM((items, columns), jnp.bfloat16),
            pltpu.VMEM((kv_half, 2 * blocks, tokens, HD), jnp.bfloat16),
            pltpu.VMEM((kv_half, 2 * blocks, tokens, HD), jnp.bfloat16),
            pltpu.VMEM((items, LANES), jnp.float32),
            pltpu.VMEM((2 * blocks, items, tokens), jnp.float32),
            pltpu.SemaphoreType.DMA((kv_half, 2 * blocks, 2)),
            pltpu.SemaphoreType.DMA((pieces,)),
        ],
        compiler_params=params(),
        cost_estimate=pl.CostEstimate(
            flops=16 * rows * pieces * blocks * tokens * columns,
            bytes_accessed=8 * blocks * tokens * kv_half * HD + 4 * rows * pieces * columns,
            transcendentals=2 * rows * pieces * blocks * tokens * columns // HD,
        ),
    )(place, *queries, cache_k, cache_v, halves, *after)


def suffix_kernel(group_size, lengths_ref, q_ref, k_ref, v_ref, out_ref, log_ref):
    rows_here, steps, width = q_ref.shape
    tokens = k_ref.shape[1]
    kv_here = k_ref.shape[2] // HD
    items = rows_here * steps
    span = rows_here * tokens
    half = width // HD // 2
    lane = lax.broadcasted_iota(jnp.int32, (items, LANES), 1)
    token = lax.broadcasted_iota(jnp.int32, (items, span), 1)
    item = lax.broadcasted_iota(jnp.int32, (items, span), 0)
    seen = jnp.zeros((items, span), jnp.float32)
    for r in range(rows_here):
        offset = token - r * tokens
        inside = (item // steps == r) & (offset >= 0) & (offset < lengths_ref[r] + item % steps)
        seen = jnp.where(inside, 1.0, seen)
    seen = jnp.concatenate([seen] * group_size, axis=0)
    logs = [jnp.zeros((items, LANES), jnp.float32)] * 2
    for g in range(kv_here):
        columns = slice(g * group_size * HD, (g + 1) * group_size * HD)
        q_all = flat(q_ref[:, :, columns]).astype(jnp.bfloat16)
        q = stack([q_all[:, n * HD : (n + 1) * HD] for n in range(group_size)])
        keys = k_ref[:, :, g * HD : (g + 1) * HD].reshape(span, HD)
        values = v_ref[:, :, g * HD : (g + 1) * HD].reshape(span, HD)
        s = jnp.where(seen > 0.0, dot_nt(q, keys), NONE)
        highest = jnp.max(s, axis=1, keepdims=True)
        p = jnp.exp2((s - highest) * (SCALE * LOG2E))
        p = jnp.where(seen > 0.0, p, 0.0)
        total = jnp.sum(p, axis=1, keepdims=True)
        out = jnp.dot(p.astype(jnp.bfloat16), values, preferred_element_type=jnp.float32) / total
        log = highest * SCALE + jnp.log(total)
        for n in range(group_size):
            h = g * group_size + n
            out_ref[:, h * HD : (h + 1) * HD] = out[n * items : (n + 1) * items]
            side = h // half
            logs[side] = jnp.where(lane == h % half, log[n * items : (n + 1) * items], logs[side])
    for side in range(2):
        log_ref[side] = logs[side]


def attend_suffix(lengths, queries, suffix_k, suffix_v):
    rows, steps, width = queries.shape
    _, tokens, kv_width = suffix_k.shape
    items = rows * steps
    whole = lambda i, n: (0, 0, 0)
    return pl.pallas_call(
        functools.partial(suffix_kernel, width // kv_width),
        grid_spec=pltpu.PrefetchScalarGridSpec(
            num_scalar_prefetch=1,
            grid=(1,),
            in_specs=[pl.BlockSpec(x.shape, whole) for x in (queries, suffix_k, suffix_v)],
            out_specs=[
                pl.BlockSpec((items, width), lambda i, n: (0, 0)),
                pl.BlockSpec((2, items, LANES), whole),
            ],
        ),
        out_shape=(
            jax.ShapeDtypeStruct((items, width), jnp.float32),
            jax.ShapeDtypeStruct((2, items, LANES), jnp.float32),
        ),
        compiler_params=params(),
        cost_estimate=pl.CostEstimate(
            flops=16 * items * rows * tokens * width,
            bytes_accessed=4 * suffix_k.size + 6 * items * width,
            transcendentals=items * rows * tokens * width // HD,
        ),
    )(lengths, queries, suffix_k, suffix_v)


def merge_kernel(even, odd, *refs):
    sides = refs[:even], refs[even : even + odd]
    out_s_ref, log_s_ref, out_ref = refs[even + odd :]
    items, width = out_s_ref.shape
    columns = width // 2
    heads = columns // HD
    rows, steps, _ = out_ref.shape
    core = lax.axis_index("ctx") % 2
    for which, back in ((core, sides[0]), (1 - core, sides[1])):
        parts = [(ref, start) for ref in back for start in range(0, ref.shape[0], items)]
        logs = [log_s_ref[which][:, :heads]]
        for ref, start in parts:
            x = ref[start : start + items, columns:].astype(jnp.float32)
            logs.append(x[:, :heads] + x[:, heads : 2 * heads] + x[:, 2 * heads : 3 * heads])
        top = logs[0]
        for log in logs[1:]:
            top = jnp.maximum(top, log)
        factors = [jnp.exp(log - top) for log in logs]
        total = factors[0]
        for factor in factors[1:]:
            total += factor
        inverse = 1.0 / total
        factors = [factor * inverse for factor in factors]
        for h in range(heads):
            span = pl.ds(pl.multiple_of(which * columns + h * HD, HD), HD)
            acc = factors[0][:, h : h + 1] * out_s_ref[:, span]
            for factor, (ref, start) in zip(factors[1:], parts):
                value = ref[start : start + items, h * HD : (h + 1) * HD]
                acc += factor[:, h : h + 1] * value.astype(jnp.float32)
            for row in range(rows):
                out_ref[row, :, span] = acc[row * steps : (row + 1) * steps].astype(jnp.bfloat16)


def merge(even, odd, out_s, log_s, shape):
    return pl.pallas_call(
        functools.partial(merge_kernel, len(even), len(odd)),
        out_shape=jax.ShapeDtypeStruct(shape, jnp.bfloat16),
        compiler_params=params(),
    )(*even, *odd, out_s, log_s)


def local(queries, selected, placement, lengths, cache_k, cache_v, suffix_k, suffix_v):
    rows_here, steps, width = queries.shape
    size = lax.axis_size("ctx")
    kv_width = cache_k.shape[2]
    group_size = width // kv_width
    items = rows_here * steps
    chips = size // 2

    def swap(x, bits):
        return lax.ppermute(x, "ctx", [(i, i ^ bits) for i in range(size)]) if bits else x

    place = placement.reshape(1, -1)
    halves = swap(halve(cache_k, cache_v), 1)
    packed = pack(queries, selected)
    out_s, log_s = attend_suffix(lengths, queries, suffix_k, suffix_v)
    if chips <= 4:
        far = list(range(chips, size)) if chips > 1 else []
        arrived = {n: swap(packed[n % 2], n) for n in far + list(range(chips))}
        back = {}
        after = [log_s]
        for call in (far, list(range(chips))) if far else (list(range(size)),):
            partial = attend_blocks(
                place, [arrived[n] for n in call], cache_k, cache_v, halves, group_size, after
            )
            after = [partial[0]]
            for n, piece in zip(call, partial):
                back[n] = swap(piece, n)
        even = [back[n] for n in range(0, size, 2)]
        odd = [back[n] for n in range(1, size, 2)]
    else:
        same = [[2 * z + core for z in range(chips)] for core in range(2)]
        chip = jnp.concatenate([packed[0], swap(packed[1], 1)], axis=0)
        every = lax.all_gather(chip, "ctx", axis=0, tiled=True, axis_index_groups=same)
        (partial,) = attend_blocks(place, [every], cache_k, cache_v, halves, group_size, [log_s])
        back = lax.all_to_all(
            partial, "ctx", split_axis=0, concat_axis=0, tiled=True, axis_index_groups=same
        ).reshape(chips, 2, items, -1)
        even = [back[:, 0].reshape(chips * items, -1)]
        odd = [swap(back[:, 1].reshape(chips * items, -1), 1)]
    return merge(even, odd, out_s, log_s, queries.shape)


def solution(mesh):
    rows = P(("groups", "ctx"), None, "rows")
    in_specs = (
        rows,
        P(("groups", "ctx"), None, None),
        P("groups"),
        P(("groups", "ctx")),
        rows,
        rows,
        rows,
        rows,
    )
    return jax.shard_map(local, mesh=mesh, in_specs=in_specs, out_specs=rows, check_vma=False)
```

time: 175 us -> 260 us (1.49)
  Pallas kernels: 151 us -> 229 us
  starting transfers between devices: 16.1 us -> 24.4 us
  local copies, waits for them, and re-layouts: 5.92 us -> 1.9 us
    pallas_call x8 -> x5, Pallas kernels: 147 us -> 225 us  [the longest x1 128 us: halve(): pl.pallas_call(halve_kernel, in_specs=[ANY, ANY], out_specs=ANY, out_shap...]
    ppermute x12 -> x15, starting transfers between devices: 16.1 us -> 24.4 us  [swap(): lax.ppermute(x, 'ctx', [(i, i ^ bits) for i in range(size)])]
    unnamed x24 -> x36, local copies, waits for them, and re-layouts: 5.92 us -> 1.9 us
  transfers between devices with their start and end apart: 12 -> 15, of which waited for: 1 -> 2; matrix products, arithmetic and copies ran while one was open for 0% -> 0% of each run, Pallas kernels for 79% -> 20%
where the time goes in v4:
time: 260 us; the launch traced here: 259 us
  Pallas kernels  229 us (88%)
  starting transfers between devices  24.4 us (9%)
  waiting for transfers between devices  3.91 us (2%)
    pallas_call x1, Pallas kernels, halve(): pl.pallas_call(halve_kernel, in_specs=[ANY, ANY], out_specs=ANY, out_shap...  128 us
    pallas_call x2, Pallas kernels, attend_blocks(): pl.pallas_call(functools.partial(block_kernel, pieces, group_size, step,...  92.5 us
    ppermute x15, starting transfers between devices, swap(): lax.ppermute(x, 'ctx', [(i, i ^ bits) for i in range(size)])  24.4 us
  transfers between devices with their start and end apart: 15, of which 2 were waited for; matrix products, arithmetic and copies ran while one was open for 0% of the time, Pallas kernels for 20%

profile of v4, /device:TPU:0, one launch (start us, length us, event | category | flops | bytes accessed | tf_op | source)
XLA Modules:
  0.0 259.1 jit_solution(11838545948685565027)
XLA Ops:
  0.0 128.2 %shard_map.83 = bf16[8,1024,256]{2,1,0:T(8,128)(2,1)} custom-call(bf16[4,1024,512]{2,1,0:T(8,128)(2,1)} %refs_4_.3, bf16[4,1024,512]{2,1,0:T(8,128)(2,1)} %refs_5_.3), custom_call_target="tpu_custom_call" | custom-call | tf_op jit(solution)/shard_map/pallas_call | solution.py:87
  128.2 0.5 collective-permute-start.3
  128.8 1.6 shard_map.82
  130.3 3.6 %collective-permute-start.4 = (bf16[16,2176]{1,0:T(8,128)(2,1)}, bf16[16,2176]{1,0:T(8,128)(2,1)S(1)}, u32[]{:S(2)}, u32[]{:S(2)}) collective-permute-start(bf16[16,2176]{1,0:T(8,128)(2,1)} %get-tuple-element.17.refs_0_), channel_id=1, source_target_pairs={{0,8},{2,10},{4,12},{6,14},{8,0},{10,2},{12,4},{14,6},{1,9},{3,11}... | collective-permute-start | bytes 208904 | tf_op jit(solution)/shard_map/ppermute | solution.py:399
  133.9 0.1 collective-permute-start.5
  134.1 3.6 %collective-permute-start.6 = (bf16[16,2176]{1,0:T(8,128)(2,1)}, bf16[16,2176]{1,0:T(8,128)(2,1)S(1)}, u32[]{:S(2)}, u32[]{:S(2)}) collective-permute-start(bf16[16,2176]{1,0:T(8,128)(2,1)} %get-tuple-element.17.refs_0_), channel_id=1, source_target_pairs={{0,12},{2,14},{4,8},{6,10},{8,4},{10,6},{12,0},{14,2},{1,13},{3,15... | collective-permute-start | bytes 208904 | tf_op jit(solution)/shard_map/ppermute | solution.py:399
  137.7 3.8 %shard_map.84 = (f32[16,4096]{1,0:T(8,128)}, f32[2,16,128]{2,1,0:T(8,128)}) custom-call(s32[4]{0:T(128)} %lengths_ref.1, bf16[4,4,4096]{2,1,0:T(4,128)(2,1)} %q_ref.3, bf16[4,128,512]{2,1,0:T(8,128)(2,1)} %k_ref.3, bf16[4,128,512]{2,1,0:T(8,128)(2,1)} %v_ref.3), custom_call_target="tpu_custom_call" | custom-call | flops 536870912 | bytes 1441792 | tf_op jit(solution)/shard_map/pallas_call | solution.py:325
  141.5 0.4 collective-permute-start
  141.9 0.9 collective-permute-done.5.refs_1_
  142.8 2.5 collective-permute-start.1
  145.3 1.1 collective-permute-start.2
  146.5 0.6 copy-done.16
  147.1 46.2 %shard_map.85 = (bf16[16,2176]{1,0:T(8,128)(2,1)}, bf16[16,2176]{1,0:T(8,128)(2,1)}, bf16[16,2176]{1,0:T(8,128)(2,1)}, bf16[16,2176]{1,0:T(8,128)(2,1)}) custom-call(s32[1,32]{1,0:T(1,128)} %bitcast.1, bf16[16,2176]{1,0:T(8,128)(2,1)} %copy-done.11, bf16[16,2176]{1,0:T(8,128)(2,1)} %copy-done.13, bf16[16,2176]{1,0:T(8,128)(2,1)} %copy-done.14, ...), custom_call_target="tpu_custom_call" | custom-call | flops 9126805504 | bytes 8945664 | tf_op jit(solution)/shard_map/pallas_call | solution.py:257
  193.3 0.6 copy-done.12
  194.0 46.3 %shard_map.86 = (bf16[16,2176]{1,0:T(8,128)(2,1)}, bf16[16,2176]{1,0:T(8,128)(2,1)}, bf16[16,2176]{1,0:T(8,128)(2,1)}, bf16[16,2176]{1,0:T(8,128)(2,1)}) custom-call(s32[1,32]{1,0:T(1,128)} %bitcast.2, bf16[16,2176]{1,0:T(8,128)(2,1)} %get-tuple-element.17.refs_0_, bf16[16,2176]{1,0:T(8,128)(2,1)} %copy-done.12, bf16[16,2176]{1,0:T(8,128)(2,1)} %copy-done.15, ...), custom_call_target="tpu_custom_call" | custom-call | flops 9126805504 | bytes 8945664 | tf_op jit(solution)/shard_map/pallas_call | solution.py:257
  240.3 1.9 collective-permute-start.8
  242.2 2.0 collective-permute-start.9
  244.2 1.3 collective-permute-start.10
  245.5 0.6 collective-permute-start.12
  246.1 2.3 collective-permute-start.13
  248.4 4.4 %collective-permute-start.14 = (bf16[16,2176]{1,0:T(8,128)(2,1)S(1)}, bf16[16,2176]{1,0:T(8,128)(2,1)S(1)}, u32[]{:S(2)}, u32[]{:S(2)}) collective-permute-start(bf16[16,2176]{1,0:T(8,128)(2,1)S(1)} %copy-done.7), channel_id=1, source_target_pairs={{0,14},{2,12},{4,10},{6,8},{8,6},{10,4},{12,2},{14,0},{1,15},{3,13... | collective-permute-start | bytes 208904 | tf_op jit(solution)/shard_map/ppermute | solution.py:399
  252.8 3.0 %collective-permute-done.13.refs_6_ = bf16[16,2176]{1,0:T(8,128)(2,1)S(1)} collective-permute-done((bf16[16,2176]{1,0:T(8,128)(2,1)S(1)}, bf16[16,2176]{1,0:T(8,128)(2,1)S(1)}, u32[]{:S(2)}, u32[]{:S(2)}) %collective-permute-start.13) | collective-permute-done | bytes 69664 | tf_op jit(solution)/shard_map/ppermute | solution.py:399
  255.9 0.6 copy-done.5
  256.5 2.6 %shard_map.87 = bf16[4,4,4096]{2,1,0:T(4,128)(2,1)} custom-call(bf16[16,2176]{1,0:T(8,128)(2,1)} %get-tuple-element.21.refs_0_, bf16[16,2176]{1,0:T(8,128)(2,1)} %copy-done, bf16[16,2176]{1,0:T(8,128)(2,1)} %copy-done.1, bf16[16,2176]{1,0:T(8,128)(2,1)} %copy-done.2, bf16[16,2176]{1,0:T(8,128)(2,1)} %copy-done.3, bf16[16,2176]{1,0:T(8,128)(2,1)} %copy-done.4, ...), custom_call_target="tpu_custom_call" | custom-call | tf_op jit(solution)/shard_map/pallas_call | solution.py:383
  (48 shorter events, 0.2 us)
Async XLA Ops:
  128.2 18.2 %collective-permute-start.3 = (bf16[8,1024,256]{2,1,0:T(8,128)(2,1)}, bf16[8,1024,256]{2,1,0:T(8,128)(2,1)}, u32[]{:S(2)}, u32[]{:S(2)}) collective-permute-start(bf16[8,1024,256]{2,1,0:T(8,128)(2,1)} %shard_map.83), channel_id=1, source_target_pairs={{0,2},{2,0},{4,6},{6,4},{8,10},{10,8},{12,14},{14,12},{1,3},{3,1},... | collective-permute-start | bytes 12582920 | tf_op jit(solution)/shard_map/ppermute | solution.py:399
  130.3 11.2 %collective-permute-start.4 = (bf16[16,2176]{1,0:T(8,128)(2,1)}, bf16[16,2176]{1,0:T(8,128)(2,1)S(1)}, u32[]{:S(2)}, u32[]{:S(2)}) collective-permute-start(bf16[16,2176]{1,0:T(8,128)(2,1)} %get-tuple-element.17.refs_0_), channel_id=1, source_target_pairs={{0,8},{2,10},{4,12},{6,14},{8,0},{10,2},{12,4},{14,6},{1,9},{3,11}... | collective-permute-start | bytes 208904 | tf_op jit(solution)/shard_map/ppermute | solution.py:399
  133.9 8.8 %collective-permute-start.5 = (bf16[16,2176]{1,0:T(8,128)(2,1)}, bf16[16,2176]{1,0:T(8,128)(2,1)S(1)}, u32[]{:S(2)}, u32[]{:S(2)}) collective-permute-start(bf16[16,2176]{1,0:T(8,128)(2,1)} %get-tuple-element.18), channel_id=1, source_target_pairs={{0,10},{2,8},{4,14},{6,12},{8,2},{10,0},{12,6},{14,4},{1,11},{3,9}... | collective-permute-start | bytes 208904 | tf_op jit(solution)/shard_map/ppermute | solution.py:399
  134.1 11.2 %collective-permute-start.6 = (bf16[16,2176]{1,0:T(8,128)(2,1)}, bf16[16,2176]{1,0:T(8,128)(2,1)S(1)}, u32[]{:S(2)}, u32[]{:S(2)}) collective-permute-start(bf16[16,2176]{1,0:T(8,128)(2,1)} %get-tuple-element.17.refs_0_), channel_id=1, source_target_pairs={{0,12},{2,14},{4,8},{6,10},{8,4},{10,6},{12,0},{14,2},{1,13},{3,15... | collective-permute-start | bytes 208904 | tf_op jit(solution)/shard_map/ppermute | solution.py:399
  137.7 8.8 %collective-permute-start.7 = (bf16[16,2176]{1,0:T(8,128)(2,1)}, bf16[16,2176]{1,0:T(8,128)(2,1)S(1)}, u32[]{:S(2)}, u32[]{:S(2)}) collective-permute-start(bf16[16,2176]{1,0:T(8,128)(2,1)} %get-tuple-element.18), channel_id=1, source_target_pairs={{0,14},{2,12},{4,10},{6,8},{8,6},{10,4},{12,2},{14,0},{1,15},{3,13... | collective-permute-start | bytes 208904 | tf_op jit(solution)/shard_map/ppermute | solution.py:399
  141.5 4.9 %copy-start.11 = (bf16[16,2176]{1,0:T(8,128)(2,1)}, bf16[16,2176]{1,0:T(8,128)(2,1)S(1)}, u32[]{:S(2)}) copy-start(bf16[16,2176]{1,0:T(8,128)(2,1)S(1)} %collective-permute-done.4.refs_0_) | copy-start | bytes 208900
  141.5 51.8 %collective-permute-start = (bf16[16,2176]{1,0:T(8,128)(2,1)}, bf16[16,2176]{1,0:T(8,128)(2,1)S(1)}, u32[]{:S(2)}, u32[]{:S(2)}) collective-permute-start(bf16[16,2176]{1,0:T(8,128)(2,1)} %get-tuple-element.18), channel_id=1, source_target_pairs={{0,2},{2,0},{4,6},{6,4},{8,10},{10,8},{12,14},{14,12},{1,3},{3,1},... | collective-permute-start | bytes 208904 | tf_op jit(solution)/shard_map/ppermute | solution.py:399
  142.8 3.7 %copy-start.13 = (bf16[16,2176]{1,0:T(8,128)(2,1)}, bf16[16,2176]{1,0:T(8,128)(2,1)S(1)}, u32[]{:S(2)}) copy-start(bf16[16,2176]{1,0:T(8,128)(2,1)S(1)} %collective-permute-done.5.refs_1_) | copy-start | bytes 208900
  142.8 50.5 %collective-permute-start.1 = (bf16[16,2176]{1,0:T(8,128)(2,1)}, bf16[16,2176]{1,0:T(8,128)(2,1)S(1)}, u32[]{:S(2)}, u32[]{:S(2)}) collective-permute-start(bf16[16,2176]{1,0:T(8,128)(2,1)} %get-tuple-element.17.refs_0_), channel_id=1, source_target_pairs={{0,4},{2,6},{4,0},{6,2},{8,12},{10,14},{12,8},{14,10},{1,5},{3,7},... | collective-permute-start | bytes 208904 | tf_op jit(solution)/shard_map/ppermute | solution.py:399
  145.3 48.0 %collective-permute-start.2 = (bf16[16,2176]{1,0:T(8,128)(2,1)}, bf16[16,2176]{1,0:T(8,128)(2,1)S(1)}, u32[]{:S(2)}, u32[]{:S(2)}) collective-permute-start(bf16[16,2176]{1,0:T(8,128)(2,1)} %get-tuple-element.18), channel_id=1, source_target_pairs={{0,6},{2,4},{4,2},{6,0},{8,14},{10,12},{12,10},{14,8},{1,7},{3,5},... | collective-permute-start | bytes 208904 | tf_op jit(solution)/shard_map/ppermute | solution.py:399
  194.0 48.2 %copy-start.10 = (bf16[16,2176]{1,0:T(8,128)(2,1)S(1)}, bf16[16,2176]{1,0:T(8,128)(2,1)}, u32[]{:S(2)}) copy-start(bf16[16,2176]{1,0:T(8,128)(2,1)} %get-tuple-element.20.refs_7_) | copy-start | bytes 208900
  194.0 50.2 %copy-start.9 = (bf16[16,2176]{1,0:T(8,128)(2,1)S(1)}, bf16[16,2176]{1,0:T(8,128)(2,1)}, u32[]{:S(2)}) copy-start(bf16[16,2176]{1,0:T(8,128)(2,1)} %get-tuple-element.23) | copy-start | bytes 208900
  194.0 52.1 %copy-start.8 = (bf16[16,2176]{1,0:T(8,128)(2,1)S(1)}, bf16[16,2176]{1,0:T(8,128)(2,1)}, u32[]{:S(2)}) copy-start(bf16[16,2176]{1,0:T(8,128)(2,1)} %get-tuple-element.26) | copy-start | bytes 208900
  194.0 54.4 %copy-start.7 = (bf16[16,2176]{1,0:T(8,128)(2,1)S(1)}, bf16[16,2176]{1,0:T(8,128)(2,1)}, u32[]{:S(2)}) copy-start(bf16[16,2176]{1,0:T(8,128)(2,1)} %get-tuple-element.27) | copy-start | bytes 208900
  240.3 5.8 %collective-permute-start.8 = (bf16[16,2176]{1,0:T(8,128)(2,1)}, bf16[16,2176]{1,0:T(8,128)(2,1)S(1)}, u32[]{:S(2)}, u32[]{:S(2)}) collective-permute-start(bf16[16,2176]{1,0:T(8,128)(2,1)} %get-tuple-element.22), channel_id=1, source_target_pairs={{0,4},{2,6},{4,0},{6,2},{8,12},{10,14},{12,8},{14,10},{1,5},{3,7},... | collective-permute-start | bytes 208904 | tf_op jit(solution)/shard_map/ppermute | solution.py:399
  242.2 6.2 %collective-permute-start.9 = (bf16[16,2176]{1,0:T(8,128)(2,1)S(1)}, bf16[16,2176]{1,0:T(8,128)(2,1)S(1)}, u32[]{:S(2)}, u32[]{:S(2)}) collective-permute-start(bf16[16,2176]{1,0:T(8,128)(2,1)S(1)} %copy-done.10), channel_id=1, source_target_pairs={{0,8},{2,10},{4,12},{6,14},{8,0},{10,2},{12,4},{14,6},{1,9},{3,11}... | collective-permute-start | bytes 208904 | tf_op jit(solution)/shard_map/ppermute | solution.py:399
  244.2 8.6 %collective-permute-start.10 = (bf16[16,2176]{1,0:T(8,128)(2,1)S(1)}, bf16[16,2176]{1,0:T(8,128)(2,1)S(1)}, u32[]{:S(2)}, u32[]{:S(2)}) collective-permute-start(bf16[16,2176]{1,0:T(8,128)(2,1)S(1)} %copy-done.9), channel_id=1, source_target_pairs={{0,12},{2,14},{4,8},{6,10},{8,4},{10,6},{12,0},{14,2},{1,13},{3,15... | collective-permute-start | bytes 208904 | tf_op jit(solution)/shard_map/ppermute | solution.py:399
  245.5 7.3 %collective-permute-start.11 = (bf16[16,2176]{1,0:T(8,128)(2,1)}, bf16[16,2176]{1,0:T(8,128)(2,1)S(1)}, u32[]{:S(2)}, u32[]{:S(2)}) collective-permute-start(bf16[16,2176]{1,0:T(8,128)(2,1)} %get-tuple-element.24), channel_id=1, source_target_pairs={{0,2},{2,0},{4,6},{6,4},{8,10},{10,8},{12,14},{14,12},{1,3},{3,1},... | collective-permute-start | bytes 208904 | tf_op jit(solution)/shard_map/ppermute | solution.py:399
  245.5 7.3 %collective-permute-start.12 = (bf16[16,2176]{1,0:T(8,128)(2,1)}, bf16[16,2176]{1,0:T(8,128)(2,1)S(1)}, u32[]{:S(2)}, u32[]{:S(2)}) collective-permute-start(bf16[16,2176]{1,0:T(8,128)(2,1)} %get-tuple-element.25), channel_id=1, source_target_pairs={{0,6},{2,4},{4,2},{6,0},{8,14},{10,12},{12,10},{14,8},{1,7},{3,5},... | collective-permute-start | bytes 208904 | tf_op jit(solution)/shard_map/ppermute | solution.py:399
  246.1 9.8 %copy-start = (bf16[16,2176]{1,0:T(8,128)(2,1)}, bf16[16,2176]{1,0:T(8,128)(2,1)S(1)}, u32[]{:S(2)}) copy-start(bf16[16,2176]{1,0:T(8,128)(2,1)S(1)} %collective-permute-done.8.refs_1_) | copy-start | bytes 208900
  246.1 9.7 %collective-permute-start.13 = (bf16[16,2176]{1,0:T(8,128)(2,1)S(1)}, bf16[16,2176]{1,0:T(8,128)(2,1)S(1)}, u32[]{:S(2)}, u32[]{:S(2)}) collective-permute-start(bf16[16,2176]{1,0:T(8,128)(2,1)S(1)} %copy-done.8), channel_id=1, source_target_pairs={{0,10},{2,8},{4,14},{6,12},{8,2},{10,0},{12,6},{14,4},{1,11},{3,9}... | collective-permute-start | bytes 208904 | tf_op jit(solution)/shard_map/ppermute | solution.py:399
  248.4 7.5 %copy-start.1 = (bf16[16,2176]{1,0:T(8,128)(2,1)}, bf16[16,2176]{1,0:T(8,128)(2,1)S(1)}, u32[]{:S(2)}) copy-start(bf16[16,2176]{1,0:T(8,128)(2,1)S(1)} %collective-permute-done.9.refs_2_) | copy-start | bytes 208900
  248.4 7.4 %collective-permute-start.14 = (bf16[16,2176]{1,0:T(8,128)(2,1)S(1)}, bf16[16,2176]{1,0:T(8,128)(2,1)S(1)}, u32[]{:S(2)}, u32[]{:S(2)}) collective-permute-start(bf16[16,2176]{1,0:T(8,128)(2,1)S(1)} %copy-done.7), channel_id=1, source_target_pairs={{0,14},{2,12},{4,10},{6,8},{8,6},{10,4},{12,2},{14,0},{1,15},{3,13... | collective-permute-start | bytes 208904 | tf_op jit(solution)/shard_map/ppermute | solution.py:399
  252.8 3.1 %copy-start.3 = (bf16[16,2176]{1,0:T(8,128)(2,1)}, bf16[16,2176]{1,0:T(8,128)(2,1)S(1)}, u32[]{:S(2)}) copy-start(bf16[16,2176]{1,0:T(8,128)(2,1)S(1)} %collective-permute-done.11.refs_4_) | copy-start | bytes 208900
  (9 other events, 11.1 us)

commit v5 on v3

--- a/solution.py
+++ b/solution.py
@@ -14,8 +14,8 @@
 LOG2E = math.log2(math.e)
 NONE = -1e30
 LOW, HIGH = 2.0**-80, 2.0**100
-VMEM = 56 * 1024 * 1024
-ROWS_STEP = 256
+VMEM = 60 * 1024 * 1024
+ROWS_STEP = 512
 
 
 def split3(x):
@@ -42,9 +42,24 @@
     return x.astype(jnp.float32).reshape(x.shape[0] * x.shape[1], x.shape[2])
 
 
-def pack_kernel(where_ref, q_ref, selected_ref, mine_ref, other_ref):
+ANY = pl.BlockSpec(memory_space=pl.ANY)
+
+
+def pack_kernel(q_ref, selected_ref, k_ref, v_ref, mine_ref, other_ref, out_ref, held, in_sems, out_sems):
+    blocks, _, kv_columns = k_ref.shape
+    kv_half = kv_columns // 2
     half = q_ref.shape[2] // 2
-    core = where_ref[2]
+    core = lax.axis_index("ctx") % 2
+    kv_start = pl.multiple_of((1 - core) * kv_half, LANES)
+    reads, writes = [], []
+    for n, ref in enumerate((k_ref, v_ref)):
+        for b in range(blocks):
+            m = n * blocks + b
+            source = ref.at[b, :, pl.ds(kv_start, kv_half)]
+            reads.append(pltpu.make_async_copy(source, held.at[m], in_sems.at[m]))
+            writes.append(pltpu.make_async_copy(held.at[m], out_ref.at[m], out_sems.at[m]))
+    for read in reads:
+        read.start()
     ids = flat(selected_ref[...])
     pad = jnp.full((ids.shape[0], LANES - ids.shape[1]), -1.0, jnp.float32)
     ids = jnp.concatenate([ids, pad], axis=1).astype(jnp.bfloat16)
@@ -52,62 +67,44 @@
         start = pl.multiple_of(which * half, LANES)
         ref[:, :half] = flat(q_ref[:, :, pl.ds(start, half)]).astype(jnp.bfloat16)
         ref[:, half:] = ids
-
-
-def pack(where, queries, selected):
+    for read, write in zip(reads, writes):
+        read.wait()
+        write.start()
+    for write in writes:
+        write.wait()
+
+
+def pack(queries, selected, cache_k, cache_v):
     rows, steps, width = queries.shape
+    blocks, tokens, columns = cache_k.shape
     shape = jax.ShapeDtypeStruct((rows * steps, width // 2 + LANES), jnp.bfloat16)
-    whole = lambda i, w: (0, 0, 0)
+    kv_shape = (2 * blocks, tokens, columns // 2)
+    whole = pl.BlockSpec(memory_space=pltpu.VMEM)
     return pl.pallas_call(
         pack_kernel,
-        grid_spec=pltpu.PrefetchScalarGridSpec(
-            num_scalar_prefetch=1,
-            grid=(1,),
-            in_specs=[pl.BlockSpec(queries.shape, whole), pl.BlockSpec(selected.shape, whole)],
-            out_specs=[pl.BlockSpec(shape.shape, lambda i, w: (0, 0))] * 2,
-        ),
-        out_shape=[shape, shape],
+        in_specs=[whole, whole, ANY, ANY],
+        out_specs=[whole, whole, ANY],
+        out_shape=[shape, shape, jax.ShapeDtypeStruct(kv_shape, jnp.bfloat16)],
+        scratch_shapes=[
+            pltpu.VMEM(kv_shape, jnp.bfloat16),
+            pltpu.SemaphoreType.DMA((2 * blocks,)),
+            pltpu.SemaphoreType.DMA((2 * blocks,)),
+        ],
         compiler_params=params(),
-    )(where, queries, selected)
-
-
-def halve_kernel(blocks, where_ref, k_ref, v_ref, out_ref):
-    @pl.when(pl.program_id(0) < blocks)
-    def _():
-        out_ref[...] = k_ref[...]
-
-    @pl.when(pl.program_id(0) >= blocks)
-    def _():
-        out_ref[...] = v_ref[...]
-
-
-def halve(where, cache_k, cache_v):
-    blocks, tokens, columns = cache_k.shape
-    block = (1, tokens, columns // 2)
-    return pl.pallas_call(
-        functools.partial(halve_kernel, blocks),
-        grid_spec=pltpu.PrefetchScalarGridSpec(
-            num_scalar_prefetch=1,
-            grid=(2 * blocks,),
-            in_specs=[
-                pl.BlockSpec(block, lambda i, w: (jnp.minimum(i, blocks - 1), 0, 1 - w[2])),
-                pl.BlockSpec(block, lambda i, w: (jnp.maximum(i - blocks, 0), 0, 1 - w[2])),
-            ],
-            out_specs=pl.BlockSpec(block, lambda i, w: (i, 0, 0)),
-        ),
-        out_shape=jax.ShapeDtypeStruct((2 * blocks, tokens, columns // 2), jnp.bfloat16),
-        compiler_params=params(),
-    )(where, cache_k, cache_v)
+    )(queries, selected, cache_k, cache_v)
 
 
 def block_kernel(pieces, group_size, step, where_ref, place_ref, *refs):
     q_refs = refs[:pieces]
     id_refs = refs[pieces : 2 * pieces]
     own_k, own_v, next_k, next_v = refs[2 * pieces : 2 * pieces + 4]
-    out_ref, logs_ref, s_ref = refs[-3:]
+    outs = max(1, pieces // 2)
+    out_refs = refs[-2 - outs : -2]
+    logs_ref, s_ref = refs[-2:]
     kv = pl.program_id(1)
     share = q_refs[0].shape[0]
     items = share * pieces
+    kept = items // outs
     blocks, tokens, _ = own_k.shape
     lane = lax.broadcasted_iota(jnp.int32, (items, LANES), 1)
     first_head = kv * group_size
@@ -130,7 +127,9 @@
 
     def write(head, out):
         start = pl.multiple_of((first_head + head) * HD, HD)
-        out_ref[:, pl.ds(start, HD)] = out.astype(jnp.bfloat16)
+        out = out.astype(jnp.bfloat16)
+        for n, ref in enumerate(out_refs):
+            ref[:, pl.ds(start, HD)] = out[n * kept : (n + 1) * kept]
 
     ones = jnp.ones((tokens, LANES), jnp.bfloat16)
     totals = jnp.ones((items, LANES), jnp.float32)
@@ -180,10 +179,12 @@
 
     @pl.when(kv == pl.num_programs(1) - 1)
     def _():
-        heads = (out_ref.shape[1] - LANES) // HD
+        heads = (out_refs[0].shape[1] - LANES) // HD
         parts = jnp.concatenate([x[:, :heads] for x in split3(logs_ref[...])], axis=1)
         pad = jnp.zeros((items, LANES - 3 * heads), jnp.bfloat16)
-        out_ref[:, heads * HD :] = jnp.concatenate([parts, pad], axis=1)
+        parts = jnp.concatenate([parts, pad], axis=1)
+        for n, ref in enumerate(out_refs):
+            ref[:, heads * HD :] = parts[n * kept : (n + 1) * kept]
 
 
 def attend_blocks(where, place, queries, cache_k, cache_v, halves, group_size, after):
@@ -191,13 +192,14 @@
     rows, columns = queries[0].shape
     blocks, tokens, kv_width = cache_k.shape
     kv_half = kv_width // HD // 2
-    share = min(rows, 128)
+    share = min(rows, 64)
     items = share * pieces
+    outs = max(1, pieces // 2)
     own = pl.BlockSpec((blocks, tokens, HD), lambda i, g, w: (0, 0, w[2] * kv_half + g))
     queries_block = pl.BlockSpec((share, group_size * HD), lambda i, g, w: (i, g))
     ids_block = pl.BlockSpec((share, LANES), lambda i, g, w: (i, columns // LANES - 1))
     return pl.pallas_call(
-        functools.partial(block_kernel, pieces, group_size, max(1, ROWS_STEP // items)),
+        functools.partial(block_kernel, pieces, group_size, min(group_size, max(1, ROWS_STEP // items))),
         grid_spec=pltpu.PrefetchScalarGridSpec(
             num_scalar_prefetch=1,
             grid=(rows // share, kv_half),
@@ -210,18 +212,18 @@
                 pl.BlockSpec((blocks, tokens, HD), lambda i, g, w: (1, 0, g)),
             ]
             + [pl.BlockSpec(memory_space=pl.ANY)] * len(after),
-            out_specs=pl.BlockSpec((items, columns), lambda i, g, w: (i, 0)),
+            out_specs=[pl.BlockSpec((items // outs, columns), lambda i, g, w: (i, 0))] * outs,
             scratch_shapes=[
                 pltpu.VMEM((items, LANES), jnp.float32),
                 pltpu.VMEM((2 * blocks, items, tokens), jnp.float32),
             ],
         ),
-        out_shape=jax.ShapeDtypeStruct((rows * pieces, columns), jnp.bfloat16),
+        out_shape=[jax.ShapeDtypeStruct((rows * pieces // outs, columns), jnp.bfloat16)] * outs,
         compiler_params=params(),
         cost_estimate=pl.CostEstimate(
-            flops=16 * rows * pieces * blocks * tokens * columns,
-            bytes_accessed=8 * blocks * tokens * kv_half * HD + 4 * rows * pieces * columns,
-            transcendentals=2 * rows * pieces * blocks * tokens * columns // HD,
+            flops=rows * pieces * tokens * columns,
+            bytes_accessed=4 * rows * pieces * columns,
+            transcendentals=rows * pieces * columns,
         ),
     )(where, place, *queries, *queries, cache_k, cache_v, halves, halves, *after)
 
@@ -294,88 +296,106 @@
     )(lengths, queries, suffix_k, suffix_v)
 
 
-def merge_kernel(arrays, *refs):
-    back_refs = refs[:arrays]
-    out_refs = refs[arrays:]
-    items = out_refs[0].shape[0]
-    columns = out_refs[0].shape[1] - LANES
+def weigh(parts, items, heads):
+    columns = heads * HD
+    logs = []
+    for ref, start in parts:
+        x = ref[start : start + items, columns:].astype(jnp.float32)
+        logs.append(x[:, :heads] + x[:, heads : 2 * heads] + x[:, 2 * heads : 3 * heads])
+    return logs
+
+
+def shares(logs):
+    top = logs[0]
+    for log in logs[1:]:
+        top = jnp.maximum(top, log)
+    factors = [jnp.exp(log - top) for log in logs]
+    total = factors[0]
+    for factor in factors[1:]:
+        total += factor
+    inverse = 1.0 / total
+    return [factor * inverse for factor in factors], top + jnp.log(total)
+
+
+def parts_of(refs, items, side):
+    return [(ref, start + side * items) for ref in refs for start in range(0, ref.shape[0], 2 * items)]
+
+
+def other_kernel(*refs):
+    out_ref = refs[-1]
+    items = out_ref.shape[0]
+    columns = out_ref.shape[1] - LANES
     heads = columns // HD
-    for side, out_ref in enumerate(out_refs):
-        parts = [
-            (ref, start + side * items)
-            for ref in back_refs
-            for start in range(0, ref.shape[0], 2 * items)
-        ]
-        logs = []
-        for ref, start in parts:
-            x = ref[start : start + items, columns:].astype(jnp.float32)
-            logs.append(x[:, :heads] + x[:, heads : 2 * heads] + x[:, 2 * heads : 3 * heads])
-        top = logs[0]
-        for log in logs[1:]:
-            top = jnp.maximum(top, log)
-        factors = [jnp.exp(log - top) for log in logs]
-        total = factors[0]
-        for factor in factors[1:]:
-            total += factor
-        inverse = 1.0 / total
-        factors = [factor * inverse for factor in factors]
-        for h in range(heads):
-            span = slice(h * HD, (h + 1) * HD)
-            acc = jnp.zeros((items, HD), jnp.float32)
-            for factor, (ref, start) in zip(factors, parts):
-                acc += factor[:, h : h + 1] * ref[start : start + items, span].astype(jnp.float32)
-            out_ref[:, span] = acc
-        log = top + jnp.log(total)
-        pad = jnp.zeros((items, LANES - heads), jnp.float32)
-        out_ref[:, columns:] = jnp.concatenate([log, pad], axis=1)
-
-
-def merge(back, items):
-    shape = jax.ShapeDtypeStruct((items, back[0].shape[1]), jnp.float32)
+    parts = parts_of(refs[:-1], items, 1)
+    factors, log = shares(weigh(parts, items, heads))
+    for h in range(heads):
+        span = slice(h * HD, (h + 1) * HD)
+        acc = jnp.zeros((items, HD), jnp.float32)
+        for factor, (ref, start) in zip(factors, parts):
+            acc += factor[:, h : h + 1] * ref[start : start + items, span].astype(jnp.float32)
+        out_ref[:, span] = acc
+    pad = jnp.zeros((items, LANES - heads), jnp.float32)
+    out_ref[:, columns:] = jnp.concatenate([log, pad], axis=1)
+
+
+def merge_other(back, items):
     return pl.pallas_call(
-        functools.partial(merge_kernel, len(back)),
-        out_shape=[shape, shape],
+        other_kernel,
+        out_shape=jax.ShapeDtypeStruct((items, back[0].shape[1]), jnp.float32),
         compiler_params=params(),
     )(*back)
 
 
-def finish_kernel(where_ref, mine_ref, other_ref, out_s_ref, log_s_ref, out_ref):
-    items = mine_ref.shape[0]
-    columns = mine_ref.shape[1] - LANES
+def finish_kernel(arrays, own, where_ref, *refs):
+    back_refs = refs[:arrays]
+    out_s_ref, log_s_ref = refs[arrays : arrays + 2]
+    out_ref = refs[-1]
+    rows, steps, columns = out_ref.shape
+    items = rows * steps
     heads = columns // HD
-    rows, steps, _ = out_ref.shape
-    core = where_ref[2]
-    for ref, which in ((mine_ref, core), (other_ref, 1 - core)):
-        log = ref[:, columns:]
-        log_s = log_s_ref[which]
-        top = jnp.maximum(log, log_s)
-        factor = jnp.exp(log - top)
-        factor_s = jnp.exp(log_s - top)
-        inverse = 1.0 / (factor + factor_s)
-        factor, factor_s = factor * inverse, factor_s * inverse
-        for h in range(heads):
-            start = pl.multiple_of(which * columns + h * HD, HD)
-            out = factor[:, h : h + 1] * ref[:, h * HD : (h + 1) * HD]
-            out += factor_s[:, h : h + 1] * out_s_ref[:, pl.ds(start, HD)]
-            for row in range(rows):
-                part = out[row * steps : (row + 1) * steps]
-                out_ref[row, :, pl.ds(start, HD)] = part.astype(jnp.bfloat16)
-
-
-def finish(where, mine, other, out_s, log_s, shape):
-    flat_map = lambda i, w: (0, 0)
+    log_s = log_s_ref[0][:, :heads]
+    if own:
+        parts = parts_of(back_refs, items, 0)
+        logs = weigh(parts, items, heads)
+    else:
+        parts = [(back_refs[0], 0)]
+        logs = [back_refs[0][:, columns : columns + heads]]
+    factors, _ = shares([log_s] + logs)
+    for h in range(heads):
+        span = slice(h * HD, (h + 1) * HD)
+        acc = factors[0][:, h : h + 1] * out_s_ref[:, span]
+        for factor, (ref, start) in zip(factors[1:], parts):
+            acc += factor[:, h : h + 1] * ref[start : start + items, span].astype(jnp.float32)
+        for row in range(rows):
+            out_ref[row, :, span] = acc[row * steps : (row + 1) * steps].astype(jnp.bfloat16)
+
+
+def finish(where, back, out_s, log_s, shape, so_far):
+    rows, steps, width = shape
+    items = rows * steps
+    own = so_far is None
+    others = [] if own else [so_far]
+
+    def side(w):
+        return w[2] if own else 1 - w[2]
+
     return pl.pallas_call(
-        finish_kernel,
+        functools.partial(finish_kernel, len(back), own),
         grid_spec=pltpu.PrefetchScalarGridSpec(
             num_scalar_prefetch=1,
             grid=(1,),
-            in_specs=[pl.BlockSpec(x.shape, flat_map) for x in (mine, other, out_s)]
-            + [pl.BlockSpec(log_s.shape, lambda i, w: (0, 0, 0))],
-            out_specs=pl.BlockSpec(shape, lambda i, w: (0, 0, 0)),
+            in_specs=[pl.BlockSpec(x.shape, lambda i, w: (0, 0)) for x in back]
+            + [
+                pl.BlockSpec((items, width // 2), lambda i, w: (0, side(w))),
+                pl.BlockSpec((1,) + log_s.shape[1:], lambda i, w: (side(w), 0, 0)),
+            ]
+            + [ANY] * len(others),
+            out_specs=pl.BlockSpec((rows, steps, width // 2), lambda i, w: (0, 0, side(w))),
         ),
         out_shape=jax.ShapeDtypeStruct(shape, jnp.bfloat16),
+        input_output_aliases={} if own else {len(back) + 3: 0},
         compiler_params=params(),
-    )(where, mine, other, out_s, log_s)
+    )(where, *back, out_s, log_s, *others)
 
 
 def local(queries, selected, placement, lengths, cache_k, cache_v, suffix_k, suffix_v):
@@ -387,36 +407,40 @@
     chips = size // 2
 
     def swap(x, bits):
-        return lax.ppermute(x, "ctx", [(i, i ^ bits) for i in range(size)])
+        return lax.ppermute(x, "ctx", [(i, i ^ bits) for i in range(size)]) if bits else x
 
     own = lax.axis_index("ctx")
     where = jnp.stack([own * blocks_here, (own ^ 1) * blocks_here, own & 1]).astype(jnp.int32)
     place = placement.reshape(1, -1)
-    halves = swap(halve(where, cache_k, cache_v), 1)
-    mine, other = pack(where, queries, selected)
+    *packed, halves = pack(queries, selected, cache_k, cache_v)
+    halves = swap(halves, 1)
     out_s, log_s = attend_suffix(lengths, queries, suffix_k, suffix_v)
     attend = functools.partial(attend_blocks, where, place)
     if chips <= 4:
-        order = [2, 3, 1, 0] if chips == 4 else list(range(chips - 1, -1, -1))
-        arrived = {k: [swap(mine, 2 * k) if k else mine, swap(other, 2 * k + 1)] for k in order}
+        calls = [[2, 3], [1], [0]] if chips == 4 else [[k] for k in range(chips - 1, -1, -1)]
+        arrived = {
+            k: [swap(packed[0], 2 * k), swap(packed[1], 2 * k + 1)] for call in calls for k in call
+        }
         back = []
         after = [log_s]
-        for k in order:
-            partial = attend(arrived[k], cache_k, cache_v, halves, group_size, after)
-            after = [partial]
-            back.append(swap(partial, 2 * k) if k else partial)
+        for call in calls:
+            pieces = [piece for k in call for piece in arrived[k]]
+            partial = attend(pieces, cache_k, cache_v, halves, group_size, after)
+            after = [partial[0], arrived[0][1]]
+            back += [swap(x, 2 * k) for k, x in zip(call, partial)]
     else:
         same = [[2 * z + core for z in range(chips)] for core in range(2)]
-        chip = jnp.concatenate([mine, swap(other, 1)], axis=0)
+        chip = jnp.concatenate([packed[0], swap(packed[1], 1)], axis=0)
         every = lax.all_gather(chip, "ctx", axis=0, tiled=True, axis_index_groups=same)
-        partial = attend([every], cache_k, cache_v, halves, group_size, [log_s])
+        (partial,) = attend([every], cache_k, cache_v, halves, group_size, [log_s])
         back = [
             lax.all_to_all(
                 partial, "ctx", split_axis=0, concat_axis=0, tiled=True, axis_index_groups=same
             )
         ]
-    keep, send = merge(back, items)
-    return finish(where, keep, swap(send, 1), out_s, log_s, queries.shape)
+    other = swap(merge_other(back, items), 1)
+    half = finish(where, back, out_s, log_s, queries.shape, None)
+    return finish(where, [other], out_s, log_s, queries.shape, half)
 
 
 def solution(mesh):

time: 175 us -> 150 us (0.86)
  Pallas kernels: 151 us -> 124 us
  waiting for transfers between devices: 1.6 us -> 4.98 us
  local copies, waits for them, and re-layouts: 5.92 us -> 3.87 us
    pallas_call x8 -> x7, Pallas kernels: 147 us -> 120 us  [the longest x3 108 us: attend_blocks(): pl.pallas_call(functools.partial(block_kernel, pieces, group_size, min(gr...]
    ppermute x12, waiting for transfers between devices: 1.6 us -> 4.98 us  [swap(): lax.ppermute(x, 'ctx', [(i, i ^ bits) for i in range(size)])]
    unnamed x24, local copies, waits for them, and re-layouts: 5.92 us -> 3.87 us
  transfers between devices with their start and end apart: 12 -> 12, of which waited for: 1 -> 2; matrix products, arithmetic and copies ran while one was open for 0% -> 0% of each run, Pallas kernels for 79% -> 76%
where the time goes in v5:
time: 150 us
  Pallas kernels  124 us (83%)
  starting transfers between devices  16.1 us (11%)
  waiting for transfers between devices  4.98 us (3%)
  local copies, waits for them, and re-layouts  3.87 us (3%)
    pallas_call x3, Pallas kernels, attend_blocks(): pl.pallas_call(functools.partial(block_kernel, pieces, group_size, min(gr...  108 us
    ppermute x12, starting transfers between devices, swap(): lax.ppermute(x, 'ctx', [(i, i ^ bits) for i in range(size)])  16.1 us
    pallas_call x2, Pallas kernels, finish(): pl.pallas_call(functools.partial(finish_kernel, len(back), own), grid_spe...  5.29 us
    pallas_call x1, Pallas kernels, pack(): pl.pallas_call(pack_kernel, in_specs=[whole, whole, ANY, ANY], out_specs=...  5.21 us
    ppermute x12, waiting for transfers between devices, swap(): lax.ppermute(x, 'ctx', [(i, i ^ bits) for i in range(size)])  4.98 us
    unnamed x24, local copies, waits for them, and re-layouts  3.87 us
    pallas_call x1, Pallas kernels, attend_suffix(): pl.pallas_call(functools.partial(suffix_kernel, width // kv_width), grid_...  3.8 us
  transfers between devices with their start and end apart: 12, of which 2 were waited for; matrix products, arithmetic and copies ran while one was open for 0% of the time, Pallas kernels for 76%

profile of v5, /device:TPU:0, one launch (start us, length us, event | category | flops | bytes accessed | tf_op | source)
XLA Modules:
  0.0 149.7 jit_solution(13586970854295346169)
XLA Ops:
  0.0 5.2 %shard_map.82 = (bf16[16,2176]{1,0:T(8,128)(2,1)}, bf16[16,2176]{1,0:T(8,128)(2,1)}, bf16[8,1024,256]{2,1,0:T(8,128)(2,1)}) custom-call(bf16[4,4,4096]{2,1,0:T(4,128)(2,1)} %q_ref.3, s32[4,4,16]{2,1,0:T(4,128)} %selected_ref.1, bf16[4,1024,512]{2,1,0:T(8,128)(2,1)} %refs_4_.3, bf16[4,1024,512]{2,1,0:T(8,128)(2,1)} %refs_5_.3), custom_call_target="tpu_custom_call" | custom-call | tf_op jit(solution)/shard_map/pallas_call | solution.py:83
  5.7 3.7 %collective-permute-start = (bf16[16,2176]{1,0:T(8,128)(2,1)}, bf16[16,2176]{1,0:T(8,128)(2,1)S(1)}, u32[]{:S(2)}, u32[]{:S(2)}) collective-permute-start(bf16[16,2176]{1,0:T(8,128)(2,1)} %get-tuple-element.12.refs_0_.refs_2_), channel_id=1, source_target_pairs={{0,8},{2,10},{4,12},{6,14},{8,0},{10,2},{12,4},{14,6},{1,9},{3,11}... | collective-permute-start | bytes 208904 | tf_op jit(solution)/shard_map/ppermute | solution.py:410
  9.5 3.7 %collective-permute-start.2 = (bf16[16,2176]{1,0:T(8,128)(2,1)}, bf16[16,2176]{1,0:T(8,128)(2,1)S(1)}, u32[]{:S(2)}, u32[]{:S(2)}) collective-permute-start(bf16[16,2176]{1,0:T(8,128)(2,1)} %get-tuple-element.12.refs_0_.refs_2_), channel_id=1, source_target_pairs={{0,12},{2,14},{4,8},{6,10},{8,4},{10,6},{12,0},{14,2},{1,13},{3,15... | collective-permute-start | bytes 208904 | tf_op jit(solution)/shard_map/ppermute | solution.py:410
  13.1 1.0 collective-permute-done.refs_0_.refs_4_
  14.1 3.9 %collective-permute-done.1.refs_1_.refs_5_ = bf16[16,2176]{1,0:T(8,128)(2,1)S(1)} collective-permute-done((bf16[16,2176]{1,0:T(8,128)(2,1)}, bf16[16,2176]{1,0:T(8,128)(2,1)S(1)}, u32[]{:S(2)}, u32[]{:S(2)}) %collective-permute-start.1) | collective-permute-done | bytes 69664 | tf_op jit(solution)/shard_map/ppermute | solution.py:410
  18.1 2.6 %collective-permute-start.7 = (bf16[16,2176]{1,0:T(8,128)(2,1)}, bf16[16,2176]{1,0:T(8,128)(2,1)S(1)}, u32[]{:S(2)}, u32[]{:S(2)}) collective-permute-start(bf16[16,2176]{1,0:T(8,128)(2,1)} %get-tuple-element.12.refs_0_.refs_2_), channel_id=1, source_target_pairs={{0,4},{2,6},{4,0},{6,2},{8,12},{10,14},{12,8},{14,10},{1,5},{3,7},... | collective-permute-start | bytes 208904 | tf_op jit(solution)/shard_map/ppermute | solution.py:410
  20.7 1.1 collective-permute-start.8
  21.9 0.6 pad_add_fusion.where_ref
  22.5 3.8 %shard_map.83 = (f32[16,4096]{1,0:T(8,128)}, f32[2,16,128]{2,1,0:T(8,128)}) custom-call(s32[4]{0:T(128)} %lengths_ref.1, bf16[4,4,4096]{2,1,0:T(4,128)(2,1)} %q_ref.3, bf16[4,128,512]{2,1,0:T(8,128)(2,1)} %k_ref.3, bf16[4,128,512]{2,1,0:T(8,128)(2,1)} %v_ref.3), custom_call_target="tpu_custom_call" | custom-call | flops 536870912 | bytes 1441792 | tf_op jit(solution)/shard_map/pallas_call | solution.py:275
  26.3 0.6 copy-done.7
  26.9 41.7 %shard_map.84 = (bf16[32,2176]{1,0:T(8,128)(2,1)}, bf16[32,2176]{1,0:T(8,128)(2,1)}) custom-call(s32[3]{0:T(128)} %pad_add_fusion.where_ref, s32[1,32]{1,0:T(1,128)} %bitcast.4, bf16[16,2176]{1,0:T(8,128)(2,1)} %copy-done.4, bf16[16,2176]{1,0:T(8,128)(2,1)} %copy-done.5, bf16[16,2176]{1,0:T(8,128)(2,1)} %copy-done.6, bf16[16,2176]{1,0:T(8,128)(2,1)} %copy-done.7, ...), custom_call_target="tpu_custom_call" | custom-call | flops 142606336 | bytes 557056 | tf_op jit(solution)/shard_map/pallas_call | solution.py:201
  68.6 2.3 %collective-permute-start.5 = (bf16[32,2176]{1,0:T(8,128)(2,1)}, bf16[32,2176]{1,0:T(8,128)(2,1)S(1)}, u32[]{:S(2)}, u32[]{:S(2)}) collective-permute-start(bf16[32,2176]{1,0:T(8,128)(2,1)} %get-tuple-element.16.refs_8_), channel_id=1, source_target_pairs={{0,8},{2,10},{4,12},{6,14},{8,0},{10,2},{12,4},{14,6},{1,9},{3,11}... | collective-permute-start | bytes 417800 | tf_op jit(solution)/shard_map/ppermute | solution.py:410
  70.9 0.6 copy-done
  71.5 0.6 copy-done.9
  72.2 32.8 %shard_map.85.refs_8_ = bf16[32,2176]{1,0:T(8,128)(2,1)} custom-call(s32[3]{0:T(128)} %pad_add_fusion.where_ref, s32[1,32]{1,0:T(1,128)} %bitcast.5, bf16[16,2176]{1,0:T(8,128)(2,1)} %copy-done.8, bf16[16,2176]{1,0:T(8,128)(2,1)} %copy-done.9, bf16[16,2176]{1,0:T(8,128)(2,1)} %copy-done.8, bf16[16,2176]{1,0:T(8,128)(2,1)} %copy-done.9, ...), custom_call_target="tpu_custom_call" | custom-call | flops 71303168 | bytes 278528 | tf_op jit(solution)/shard_map/pallas_call | solution.py:201
  105.0 1.7 %collective-permute-start.10 = (bf16[32,2176]{1,0:T(8,128)(2,1)}, bf16[32,2176]{1,0:T(8,128)(2,1)S(1)}, u32[]{:S(2)}, u32[]{:S(2)}) collective-permute-start(bf16[32,2176]{1,0:T(8,128)(2,1)} %shard_map.85.refs_8_), channel_id=1, source_target_pairs={{0,4},{2,6},{4,0},{6,2},{8,12},{10,14},{12,8},{14,10},{1,5},{3,7},... | collective-permute-start | bytes 417800 | tf_op jit(solution)/shard_map/ppermute | solution.py:410
  106.7 0.5 collective-permute-start.6
  107.2 33.0 %shard_map.86.refs_3_ = bf16[32,2176]{1,0:T(8,128)(2,1)} custom-call(s32[3]{0:T(128)} %pad_add_fusion.where_ref, s32[1,32]{1,0:T(1,128)} %bitcast.6, bf16[16,2176]{1,0:T(8,128)(2,1)} %get-tuple-element.12.refs_0_.refs_2_, bf16[16,2176]{1,0:T(8,128)(2,1)} %copy-done, bf16[16,2176]{1,0:T(8,128)(2,1)} %get-tuple-element.12.refs_0_.refs_2_, ...), custom_call_target="tpu_custom_call" | custom-call | flops 71303168 | bytes 278528 | tf_op jit(solution)/shard_map/pallas_call | solution.py:201
  140.2 0.6 copy-done.2
  140.9 0.7 copy-done.3
  141.6 2.1 %shard_map.87 = f32[16,2176]{1,0:T(8,128)} custom-call(bf16[32,2176]{1,0:T(8,128)(2,1)} %copy-done.1, bf16[32,2176]{1,0:T(8,128)(2,1)} %copy-done.3, bf16[32,2176]{1,0:T(8,128)(2,1)} %copy-done.2, bf16[32,2176]{1,0:T(8,128)(2,1)} %shard_map.86.refs_3_), custom_call_target="tpu_custom_call" | custom-call | tf_op jit(solution)/shard_map/pallas_call | solution.py:342
  143.7 2.8 %shard_map.88.refs_3_ = bf16[4,4,4096]{2,1,0:T(4,128)(2,1)} custom-call(s32[3]{0:T(128)} %pad_add_fusion.where_ref, bf16[32,2176]{1,0:T(8,128)(2,1)} %copy-done.1, bf16[32,2176]{1,0:T(8,128)(2,1)} %copy-done.3, bf16[32,2176]{1,0:T(8,128)(2,1)} %copy-done.2, bf16[32,2176]{1,0:T(8,128)(2,1)} %shard_map.86.refs_3_, ...), custom_call_target="tpu_custom_call" | custom-call | tf_op jit(solution)/shard_map/pallas_call | solution.py:382
  146.6 0.7 copy-done.10
  147.2 2.4 %shard_map.89 = bf16[4,4,4096]{2,1,0:T(4,128)(2,1)} custom-call(s32[3]{0:T(128)} %pad_add_fusion.where_ref, f32[16,2176]{1,0:T(8,128)} %copy-done.10, f32[16,4096]{1,0:T(8,128)} %get-tuple-element.18.refs_4_.refs_1_, f32[2,16,128]{2,1,0:T(8,128)} %get-tuple-element.15.refs_12_.refs_5_.refs_2_, ...), custom_call_target="tpu_custom_call", output_to_operand_aliasing={{}: (4, {})} | custom-call | tf_op jit(solution)/shard_map/pallas_call | solution.py:382
  (33 shorter events, 0.8 us)
Async XLA Ops:
  5.2 21.0 %collective-permute-start.4 = (bf16[8,1024,256]{2,1,0:T(8,128)(2,1)}, bf16[8,1024,256]{2,1,0:T(8,128)(2,1)}, u32[]{:S(2)}, u32[]{:S(2)}) collective-permute-start(bf16[8,1024,256]{2,1,0:T(8,128)(2,1)} %get-tuple-element.14), channel_id=1, source_target_pairs={{0,2},{2,0},{4,6},{6,4},{8,10},{10,8},{12,14},{14,12},{1,3},{3,1},... | collective-permute-start | bytes 12582920 | tf_op jit(solution)/shard_map/ppermute | solution.py:410
  5.7 8.4 %collective-permute-start = (bf16[16,2176]{1,0:T(8,128)(2,1)}, bf16[16,2176]{1,0:T(8,128)(2,1)S(1)}, u32[]{:S(2)}, u32[]{:S(2)}) collective-permute-start(bf16[16,2176]{1,0:T(8,128)(2,1)} %get-tuple-element.12.refs_0_.refs_2_), channel_id=1, source_target_pairs={{0,8},{2,10},{4,12},{6,14},{8,0},{10,2},{12,4},{14,6},{1,9},{3,11}... | collective-permute-start | bytes 208904 | tf_op jit(solution)/shard_map/ppermute | solution.py:410
  9.4 8.7 %collective-permute-start.1 = (bf16[16,2176]{1,0:T(8,128)(2,1)}, bf16[16,2176]{1,0:T(8,128)(2,1)S(1)}, u32[]{:S(2)}, u32[]{:S(2)}) collective-permute-start(bf16[16,2176]{1,0:T(8,128)(2,1)} %get-tuple-element.13), channel_id=1, source_target_pairs={{0,10},{2,8},{4,14},{6,12},{8,2},{10,0},{12,6},{14,4},{1,11},{3,9}... | collective-permute-start | bytes 208904 | tf_op jit(solution)/shard_map/ppermute | solution.py:410
  9.5 11.3 %collective-permute-start.2 = (bf16[16,2176]{1,0:T(8,128)(2,1)}, bf16[16,2176]{1,0:T(8,128)(2,1)S(1)}, u32[]{:S(2)}, u32[]{:S(2)}) collective-permute-start(bf16[16,2176]{1,0:T(8,128)(2,1)} %get-tuple-element.12.refs_0_.refs_2_), channel_id=1, source_target_pairs={{0,12},{2,14},{4,8},{6,10},{8,4},{10,6},{12,0},{14,2},{1,13},{3,15... | collective-permute-start | bytes 208904 | tf_op jit(solution)/shard_map/ppermute | solution.py:410
  13.1 13.1 %collective-permute-start.3 = (bf16[16,2176]{1,0:T(8,128)(2,1)}, bf16[16,2176]{1,0:T(8,128)(2,1)S(1)}, u32[]{:S(2)}, u32[]{:S(2)}) collective-permute-start(bf16[16,2176]{1,0:T(8,128)(2,1)} %get-tuple-element.13), channel_id=1, source_target_pairs={{0,14},{2,12},{4,10},{6,8},{8,6},{10,4},{12,2},{14,0},{1,15},{3,13... | collective-permute-start | bytes 208904 | tf_op jit(solution)/shard_map/ppermute | solution.py:410
  14.1 12.1 %copy-start.4 = (bf16[16,2176]{1,0:T(8,128)(2,1)}, bf16[16,2176]{1,0:T(8,128)(2,1)S(1)}, u32[]{:S(2)}) copy-start(bf16[16,2176]{1,0:T(8,128)(2,1)S(1)} %collective-permute-done.refs_0_.refs_4_) | copy-start | bytes 208900
  14.1 56.7 %collective-permute-start.9 = (bf16[16,2176]{1,0:T(8,128)(2,1)}, bf16[16,2176]{1,0:T(8,128)(2,1)S(1)}, u32[]{:S(2)}, u32[]{:S(2)}) collective-permute-start(bf16[16,2176]{1,0:T(8,128)(2,1)} %get-tuple-element.13), channel_id=1, source_target_pairs={{0,2},{2,0},{4,6},{6,4},{8,10},{10,8},{12,14},{14,12},{1,3},{3,1},... | collective-permute-start | bytes 208904 | tf_op jit(solution)/shard_map/ppermute | solution.py:410
  18.1 8.2 %copy-start.5 = (bf16[16,2176]{1,0:T(8,128)(2,1)}, bf16[16,2176]{1,0:T(8,128)(2,1)S(1)}, u32[]{:S(2)}) copy-start(bf16[16,2176]{1,0:T(8,128)(2,1)S(1)} %collective-permute-done.1.refs_1_.refs_5_) | copy-start | bytes 208900
  18.1 52.8 %collective-permute-start.7 = (bf16[16,2176]{1,0:T(8,128)(2,1)}, bf16[16,2176]{1,0:T(8,128)(2,1)S(1)}, u32[]{:S(2)}, u32[]{:S(2)}) collective-permute-start(bf16[16,2176]{1,0:T(8,128)(2,1)} %get-tuple-element.12.refs_0_.refs_2_), channel_id=1, source_target_pairs={{0,4},{2,6},{4,0},{6,2},{8,12},{10,14},{12,8},{14,10},{1,5},{3,7},... | collective-permute-start | bytes 208904 | tf_op jit(solution)/shard_map/ppermute | solution.py:410
  20.7 5.5 %copy-start.6 = (bf16[16,2176]{1,0:T(8,128)(2,1)}, bf16[16,2176]{1,0:T(8,128)(2,1)S(1)}, u32[]{:S(2)}) copy-start(bf16[16,2176]{1,0:T(8,128)(2,1)S(1)} %collective-permute-done.2.refs_2_.refs_6_) | copy-start | bytes 208900
  20.7 50.2 %collective-permute-start.8 = (bf16[16,2176]{1,0:T(8,128)(2,1)}, bf16[16,2176]{1,0:T(8,128)(2,1)S(1)}, u32[]{:S(2)}, u32[]{:S(2)}) collective-permute-start(bf16[16,2176]{1,0:T(8,128)(2,1)} %get-tuple-element.13), channel_id=1, source_target_pairs={{0,6},{2,4},{4,2},{6,0},{8,14},{10,12},{12,10},{14,8},{1,7},{3,5},... | collective-permute-start | bytes 208904 | tf_op jit(solution)/shard_map/ppermute | solution.py:410
  26.3 0.6 copy-start.7
  68.6 38.1 %copy-start.11 = (bf16[32,2176]{1,0:T(8,128)(2,1)S(1)}, bf16[32,2176]{1,0:T(8,128)(2,1)}, u32[]{:S(2)}) copy-start(bf16[32,2176]{1,0:T(8,128)(2,1)} %get-tuple-element.17) | copy-start | bytes 417796
  68.6 71.6 %collective-permute-start.5 = (bf16[32,2176]{1,0:T(8,128)(2,1)}, bf16[32,2176]{1,0:T(8,128)(2,1)S(1)}, u32[]{:S(2)}, u32[]{:S(2)}) collective-permute-start(bf16[32,2176]{1,0:T(8,128)(2,1)} %get-tuple-element.16.refs_8_), channel_id=1, source_target_pairs={{0,8},{2,10},{4,12},{6,14},{8,0},{10,2},{12,4},{14,6},{1,9},{3,11}... | collective-permute-start | bytes 417800 | tf_op jit(solution)/shard_map/ppermute | solution.py:410
  70.9 0.6 copy-start
  70.9 0.7 copy-start.8
  71.5 0.6 copy-start.9
  105.0 35.2 %collective-permute-start.10 = (bf16[32,2176]{1,0:T(8,128)(2,1)}, bf16[32,2176]{1,0:T(8,128)(2,1)S(1)}, u32[]{:S(2)}, u32[]{:S(2)}) collective-permute-start(bf16[32,2176]{1,0:T(8,128)(2,1)} %shard_map.85.refs_8_), channel_id=1, source_target_pairs={{0,4},{2,6},{4,0},{6,2},{8,12},{10,14},{12,8},{14,10},{1,5},{3,7},... | collective-permute-start | bytes 417800 | tf_op jit(solution)/shard_map/ppermute | solution.py:410
  106.7 33.6 %collective-permute-start.6 = (bf16[32,2176]{1,0:T(8,128)(2,1)S(1)}, bf16[32,2176]{1,0:T(8,128)(2,1)S(1)}, u32[]{:S(2)}, u32[]{:S(2)}) collective-permute-start(bf16[32,2176]{1,0:T(8,128)(2,1)S(1)} %copy-done.11), channel_id=1, source_target_pairs={{0,12},{2,14},{4,8},{6,10},{8,4},{10,6},{12,0},{14,2},{1,13},{3,15... | collective-permute-start | bytes 417800 | tf_op jit(solution)/shard_map/ppermute | solution.py:410
  140.2 0.7 copy-start.2
  140.2 0.7 copy-start.1
  140.9 0.7 copy-start.3
  143.7 2.8 %collective-permute-start.11 = (f32[16,2176]{1,0:T(8,128)}, f32[16,2176]{1,0:T(8,128)S(1)}, u32[]{:S(2)}, u32[]{:S(2)}) collective-permute-start(f32[16,2176]{1,0:T(8,128)} %shard_map.87), channel_id=1, source_target_pairs={{0,2},{2,0},{4,6},{6,4},{8,10},{10,8},{12,14},{14,12},{1,3},{3,1},... | collective-permute-start | bytes 417800 | tf_op jit(solution)/shard_map/ppermute | solution.py:410
  146.6 0.7 copy-start.10

commit v6 on v5

--- a/solution.py
+++ b/solution.py
@@ -14,7 +14,7 @@
 LOG2E = math.log2(math.e)
 NONE = -1e30
 LOW, HIGH = 2.0**-80, 2.0**100
-VMEM = 60 * 1024 * 1024
+VMEM = 36 * 1024 * 1024
 ROWS_STEP = 512
 
 
@@ -28,6 +28,10 @@
 
 def dot_nt(a, b):
     return lax.dot_general(a, b, (((1,), (1,)), ((), ())), preferred_element_type=jnp.float32)
+
+
+def dot_tn(a, b):
+    return lax.dot_general(a, b, (((0,), (0,)), ((), ())), preferred_element_type=jnp.float32)
 
 
 def stack(arrays):
@@ -131,23 +135,32 @@
         for n, ref in enumerate(out_refs):
             ref[:, pl.ds(start, HD)] = out[n * kept : (n + 1) * kept]
 
-    ones = jnp.ones((tokens, LANES), jnp.bfloat16)
+    listed = jnp.zeros((items, LANES), jnp.float32)
+    for n, hit in enumerate(hits):
+        listed = jnp.where(lane == n, hit, listed)
+    wide = (items, step * items)
+    column = lax.broadcasted_iota(jnp.int32, wide, 1) % items
+    spread = jnp.where(column == lax.broadcasted_iota(jnp.int32, wide, 0), 1.0, 0.0)
+    listed = dot_tn(listed, spread)
     totals = jnp.ones((items, LANES), jnp.float32)
     for first in range(0, group_size, step):
         q = stack(
             [ref[:, h * HD : (h + 1) * HD] for h in range(first, first + step) for ref in q_refs]
         )
-        acc = jnp.zeros((step * items, HD + LANES), jnp.float32)
-        for hit, key, value in zip(hits, keys, values):
-            p = jnp.exp2(dot_nt(q, key[...]) * (SCALE * LOG2E)).astype(jnp.bfloat16)
-            both = jnp.concatenate([value[...], ones], axis=1)
-            here = jnp.dot(p, both, preferred_element_type=jnp.float32)
-            acc = jnp.where(stack([hit] * step) > 0.0, acc + here, acc)
+        acc = jnp.zeros((HD, step * items), jnp.float32)
+        total = jnp.zeros((1, step * items), jnp.float32)
+        for n, (key, value) in enumerate(zip(keys, values)):
+            p = jnp.exp2(dot_nt(key[...], q) * (SCALE * LOG2E))
+            here = dot_tn(value[...], p.astype(jnp.bfloat16))
+            hit = listed[n : n + 1] > 0.0
+            acc = jnp.where(hit, acc + here, acc)
+            total = jnp.where(hit, total + jnp.sum(p, axis=0, keepdims=True), total)
+        out = (acc / jnp.where(total > 0.0, total, 1.0)).T
+        total = jnp.broadcast_to(total, (8, step * items)).T
         for n in range(step):
-            total = acc[n * items : (n + 1) * items, HD:]
-            out = acc[n * items : (n + 1) * items, :HD]
-            write(first + n, jnp.where(some > 0.0, out / jnp.where(some > 0.0, total, 1.0), 0.0))
-            totals = jnp.where(lane == first_head + first + n, total, totals)
+            rows = slice(n * items, (n + 1) * items)
+            write(first + n, out[rows])
+            totals = jnp.where(lane == first_head + first + n, total[rows, :1], totals)
     good = (totals > LOW) & (totals < HIGH)
     bad = jnp.max(jnp.where(good | (some == 0.0), 0.0, 1.0))
     logs = jnp.where((some > 0.0) & good, jnp.log(jnp.where(good, totals, 1.0)), NONE)
@@ -228,7 +241,8 @@
     )(where, place, *queries, *queries, cache_k, cache_v, halves, halves, *after)
 
 
-def suffix_kernel(group_size, lengths_ref, q_ref, k_ref, v_ref, out_ref, log_ref):
+def suffix_kernel(group_size, lengths_ref, q_ref, k_ref, v_ref, pass_ref, out_ref, log_ref, passed_ref):
+    passed_ref[...] = pass_ref[...]
     rows_here, steps, width = q_ref.shape
     tokens = k_ref.shape[1]
     kv_here = k_ref.shape[2] // HD
@@ -267,7 +281,7 @@
         log_ref[side] = logs[side]
 
 
-def attend_suffix(lengths, queries, suffix_k, suffix_v):
+def attend_suffix(lengths, queries, suffix_k, suffix_v, passing):
     rows, steps, width = queries.shape
     _, tokens, kv_width = suffix_k.shape
     items = rows * steps
@@ -277,15 +291,18 @@
         grid_spec=pltpu.PrefetchScalarGridSpec(
             num_scalar_prefetch=1,
             grid=(1,),
-            in_specs=[pl.BlockSpec(x.shape, whole) for x in (queries, suffix_k, suffix_v)],
+            in_specs=[pl.BlockSpec(x.shape, whole) for x in (queries, suffix_k, suffix_v)]
+            + [pl.BlockSpec(passing.shape, lambda i, n: (0, 0))],
             out_specs=[
                 pl.BlockSpec((items, width), lambda i, n: (0, 0)),
                 pl.BlockSpec((2, items, LANES), whole),
+                pl.BlockSpec(passing.shape, lambda i, n: (0, 0)),
             ],
         ),
         out_shape=(
             jax.ShapeDtypeStruct((items, width), jnp.float32),
             jax.ShapeDtypeStruct((2, items, LANES), jnp.float32),
+            jax.ShapeDtypeStruct(passing.shape, passing.dtype),
         ),
         compiler_params=params(),
         cost_estimate=pl.CostEstimate(
@@ -293,7 +310,7 @@
             bytes_accessed=4 * suffix_k.size + 6 * items * width,
             transcendentals=items * rows * tokens * width // HD,
         ),
-    )(lengths, queries, suffix_k, suffix_v)
+    )(lengths, queries, suffix_k, suffix_v, passing)
 
 
 def weigh(parts, items, heads):
@@ -414,13 +431,16 @@
     place = placement.reshape(1, -1)
     *packed, halves = pack(queries, selected, cache_k, cache_v)
     halves = swap(halves, 1)
-    out_s, log_s = attend_suffix(lengths, queries, suffix_k, suffix_v)
+    out_s, log_s, passed = attend_suffix(lengths, queries, suffix_k, suffix_v, packed[1])
     attend = functools.partial(attend_blocks, where, place)
     if chips <= 4:
-        calls = [[2, 3], [1], [0]] if chips == 4 else [[k] for k in range(chips - 1, -1, -1)]
-        arrived = {
-            k: [swap(packed[0], 2 * k), swap(packed[1], 2 * k + 1)] for call in calls for k in call
-        }
+        calls = [[2, 1], [3], [0]] if chips == 4 else [[k] for k in range(chips - 1, -1, -1)]
+        arrived = {0: [packed[0], swap(passed, 1)]}
+        for k in range(1, chips):
+            if k == 3:
+                arrived[k] = [swap(x, 2) for x in arrived[2]]
+            else:
+                arrived[k] = [swap(packed[0], 2 * k), swap(packed[1], 2 * k + 1)]
         back = []
         after = [log_s]
         for call in calls:
@@ -430,7 +450,7 @@
             back += [swap(x, 2 * k) for k, x in zip(call, partial)]
     else:
         same = [[2 * z + core for z in range(chips)] for core in range(2)]
-        chip = jnp.concatenate([packed[0], swap(packed[1], 1)], axis=0)
+        chip = jnp.concatenate([packed[0], swap(passed, 1)], axis=0)
         every = lax.all_gather(chip, "ctx", axis=0, tiled=True, axis_index_groups=same)
         (partial,) = attend([every], cache_k, cache_v, halves, group_size, [log_s])
         back = [

time: 150 us -> 142 us (0.947)
  Pallas kernels: 124 us -> 115 us
  local copies, waits for them, and re-layouts: 3.87 us -> 10.4 us
  starting transfers between devices: 16.1 us -> 12.7 us
    unnamed x24 -> x22, local copies, waits for them, and re-layouts: 3.87 us -> 10.4 us
    ppermute x12, starting transfers between devices: 16.1 us -> 12.7 us  [swap(): lax.ppermute(x, 'ctx', [(i, i ^ bits) for i in range(size)])]
    pallas_call x1, Pallas kernels: 5.21 us -> 2.41 us  [pack(): pl.pallas_call(pack_kernel, in_specs=[whole, whole, ANY, ANY], out_specs=...]
    pallas_call x2, Pallas kernels: 5.29 us -> 2.9 us  [finish(): pl.pallas_call(functools.partial(finish_kernel, len(back), own), grid_spe...]
    pallas_call x1, Pallas kernels: 3.8 us -> 1.74 us  [attend_suffix(): pl.pallas_call(functools.partial(suffix_kernel, width // kv_width), grid_...]
    pallas_call x1, Pallas kernels: 2.11 us -> 0.33 us  [merge_other(): pl.pallas_call(other_kernel, out_shape=jax.ShapeDtypeStruct((items, back[...]
  transfers between devices with their start and end apart: 12 -> 12, of which waited for: 2 -> 2; matrix products, arithmetic and copies ran while one was open for 0% -> 0% of each run, Pallas kernels for 76% -> 78%
where the time goes in v6:
time: 142 us
  Pallas kernels  115 us (81%)
  starting transfers between devices  12.7 us (9%)
  local copies, waits for them, and re-layouts  10.4 us (7%)
  waiting for transfers between devices  3.64 us (3%)
    pallas_call x3, Pallas kernels, attend_blocks(): pl.pallas_call(functools.partial(block_kernel, pieces, group_size, min(gr...  108 us
    ppermute x12, starting transfers between devices, swap(): lax.ppermute(x, 'ctx', [(i, i ^ bits) for i in range(size)])  12.7 us
    unnamed x22, local copies, waits for them, and re-layouts  10.4 us
    ppermute x12, waiting for transfers between devices, swap(): lax.ppermute(x, 'ctx', [(i, i ^ bits) for i in range(size)])  3.64 us
    pallas_call x2, Pallas kernels, finish(): pl.pallas_call(functools.partial(finish_kernel, len(back), own), grid_spe...  2.9 us
  transfers between devices with their start and end apart: 12, of which 2 were waited for; matrix products, arithmetic and copies ran while one was open for 0% of the time, Pallas kernels for 78%

profile of v6, /device:TPU:0, one launch (start us, length us, event | category | flops | bytes accessed | tf_op | source)
XLA Modules:
  0.0 142.0 jit_solution(14539938119674835912)
XLA Ops:
  0.0 2.2 %copy-done = bf16[4,1024,512]{2,1,0:T(8,128)(2,1)S(1)} copy-done((bf16[4,1024,512]{2,1,0:T(8,128)(2,1)S(1)}, bf16[4,1024,512]{2,1,0:T(8,128)(2,1)}, u32[]{:S(2)}) %copy-start) | copy-done | bytes 4194328
  2.2 2.2 %copy-done.2 = bf16[4,1024,512]{2,1,0:T(8,128)(2,1)S(1)} copy-done((bf16[4,1024,512]{2,1,0:T(8,128)(2,1)S(1)}, bf16[4,1024,512]{2,1,0:T(8,128)(2,1)}, u32[]{:S(2)}) %copy-start.2) | copy-done | bytes 4194328
  4.4 0.9 copy-done.4
  5.3 0.7 copy-done.6
  6.0 2.4 %shard_map.82 = (bf16[16,2176]{1,0:T(8,128)(2,1)S(1)}, bf16[16,2176]{1,0:T(8,128)(2,1)S(1)}, bf16[8,1024,256]{2,1,0:T(8,128)(2,1)}) custom-call(bf16[4,4,4096]{2,1,0:T(4,128)(2,1)S(1)} %copy-done.4, s32[4,4,16]{2,1,0:T(4,128)S(1)} %copy-done.6, bf16[4,1024,512]{2,1,0:T(8,128)(2,1)S(1)} %copy-done, bf16[4,1024,512]{2,1,0:T(8,128)(2,1)S(1)} %copy-done.2), custom_call_target="tpu_custom_call" | custom-call | tf_op jit(solution)/shard_map/pallas_call | solution.py:87
  8.4 0.5 collective-permute-start.4
  8.9 3.7 %collective-permute-start = (bf16[16,2176]{1,0:T(8,128)(2,1)S(1)}, bf16[16,2176]{1,0:T(8,128)(2,1)S(1)}, u32[]{:S(2)}, u32[]{:S(2)}) collective-permute-start(bf16[16,2176]{1,0:T(8,128)(2,1)S(1)} %get-tuple-element.13.refs_0_.refs_2_), channel_id=1, source_target_pairs={{0,8},{2,10},{4,12},{6,14},{8,0},{10,2},{12,4},{14,6},{1,9},{3,11}... | collective-permute-start | bytes 208904 | tf_op jit(solution)/shard_map/ppermute | solution.py:427
  12.7 1.6 %collective-permute-start.2 = (bf16[16,2176]{1,0:T(8,128)(2,1)S(1)}, bf16[16,2176]{1,0:T(8,128)(2,1)S(1)}, u32[]{:S(2)}, u32[]{:S(2)}) collective-permute-start(bf16[16,2176]{1,0:T(8,128)(2,1)S(1)} %get-tuple-element.13.refs_0_.refs_2_), channel_id=1, source_target_pairs={{0,4},{2,6},{4,0},{6,2},{8,12},{10,14},{12,8},{14,10},{1,5},{3,7},... | collective-permute-start | bytes 208904 | tf_op jit(solution)/shard_map/ppermute | solution.py:427
  14.3 1.7 %shard_map.83 = (f32[16,4096]{1,0:T(8,128)S(1)}, f32[2,16,128]{2,1,0:T(8,128)S(1)}, bf16[16,2176]{1,0:T(8,128)(2,1)S(1)}) custom-call(s32[4]{0:T(128)S(1)} %copy-done.10, bf16[4,4,4096]{2,1,0:T(4,128)(2,1)S(1)} %copy-done.5, bf16[4,128,512]{2,1,0:T(8,128)(2,1)S(1)} %copy-done.8, bf16[4,128,512]{2,1,0:T(8,128)(2,1)S(1)} %copy-done.9, ...), custom_call_target="tpu_custom_call" | custom-call | flops 536870912 | bytes 1441792 | tf_op jit(solution)/shard_map/pallas_call | solution.py:289
  16.1 1.2 collective-permute-done.refs_0_.refs_4_
  17.2 2.5 %collective-permute-done.1.refs_1_.refs_5_ = bf16[16,2176]{1,0:T(8,128)(2,1)S(1)} collective-permute-done((bf16[16,2176]{1,0:T(8,128)(2,1)S(1)}, bf16[16,2176]{1,0:T(8,128)(2,1)S(1)}, u32[]{:S(2)}, u32[]{:S(2)}) %collective-permute-start.1) | collective-permute-done | bytes 69664 | tf_op jit(solution)/shard_map/ppermute | solution.py:427
  19.7 1.0 collective-permute-start.7
  20.7 1.1 collective-permute-start.8
  21.8 2.2 %copy-done.1 = bf16[4,1024,512]{2,1,0:T(8,128)(2,1)S(1)} copy-done((bf16[4,1024,512]{2,1,0:T(8,128)(2,1)S(1)}, bf16[4,1024,512]{2,1,0:T(8,128)(2,1)}, u32[]{:S(2)}) %copy-start.1) | copy-done | bytes 4194328
  24.0 2.2 %copy-done.3 = bf16[4,1024,512]{2,1,0:T(8,128)(2,1)S(1)} copy-done((bf16[4,1024,512]{2,1,0:T(8,128)(2,1)S(1)}, bf16[4,1024,512]{2,1,0:T(8,128)(2,1)}, u32[]{:S(2)}) %copy-start.3) | copy-done | bytes 4194328
  26.2 39.4 %shard_map.84 = (bf16[32,2176]{1,0:T(8,128)(2,1)S(1)}, bf16[32,2176]{1,0:T(8,128)(2,1)S(1)}) custom-call(s32[3]{0:T(128)S(1)} %pad_add_fusion.where_ref, s32[1,32]{1,0:T(1,128)S(1)} %bitcast.4, bf16[16,2176]{1,0:T(8,128)(2,1)S(1)} %collective-permute-done.refs_0_.refs_4_, bf16[16,2176]{1,0:T(8,128)(2,1)S(1)} %collective-permute-done.1.refs_1_.refs_5_, ...), custom_call_target="tpu_custom_call" | custom-call | flops 142606336 | bytes 557056 | tf_op jit(solution)/shard_map/pallas_call | solution.py:214
  65.6 3.1 %collective-permute-start.5 = (bf16[32,2176]{1,0:T(8,128)(2,1)S(1)}, bf16[32,2176]{1,0:T(8,128)(2,1)S(1)}, u32[]{:S(2)}, u32[]{:S(2)}) collective-permute-start(bf16[32,2176]{1,0:T(8,128)(2,1)S(1)} %get-tuple-element.17.refs_8_), channel_id=1, source_target_pairs={{0,8},{2,10},{4,12},{6,14},{8,0},{10,2},{12,4},{14,6},{1,9},{3,11}... | collective-permute-start | bytes 417800 | tf_op jit(solution)/shard_map/ppermute | solution.py:427
  68.7 1.3 collective-permute-start.6
  70.0 34.3 %shard_map.85.refs_8_ = bf16[32,2176]{1,0:T(8,128)(2,1)S(1)} custom-call(s32[3]{0:T(128)S(1)} %pad_add_fusion.where_ref, s32[1,32]{1,0:T(1,128)S(1)} %bitcast.5, bf16[16,2176]{1,0:T(8,128)(2,1)S(1)} %collective-permute-done.7.refs_0_.refs_2_, bf16[16,2176]{1,0:T(8,128)(2,1)S(1)} %collective-permute-done.8.refs_1_.refs_3_, ...), custom_call_target="tpu_custom_call" | custom-call | flops 71303168 | bytes 278528 | tf_op jit(solution)/shard_map/pallas_call | solution.py:214
  104.3 0.3 collective-permute-start.10
  104.6 34.1 %shard_map.86.refs_3_ = bf16[32,2176]{1,0:T(8,128)(2,1)S(1)} custom-call(s32[3]{0:T(128)S(1)} %pad_add_fusion.where_ref, s32[1,32]{1,0:T(1,128)S(1)} %bitcast.6, bf16[16,2176]{1,0:T(8,128)(2,1)S(1)} %get-tuple-element.13.refs_0_.refs_2_, bf16[16,2176]{1,0:T(8,128)(2,1)S(1)} %collective-permute-done.9.refs_9_.refs_1_.refs_3_, ...), custom_call_target="tpu_custom_call" | custom-call | flops 71303168 | bytes 278528 | tf_op jit(solution)/shard_map/pallas_call | solution.py:214
  138.7 0.3 shard_map.87
  139.1 1.5 %shard_map.88.refs_3_ = bf16[4,4,4096]{2,1,0:T(4,128)(2,1)} custom-call(s32[3]{0:T(128)S(1)} %pad_add_fusion.where_ref, bf16[32,2176]{1,0:T(8,128)(2,1)S(1)} %collective-permute-done.5.refs_0_, bf16[32,2176]{1,0:T(8,128)(2,1)S(1)} %collective-permute-done.6.refs_1_, bf16[32,2176]{1,0:T(8,128)(2,1)S(1)} %collective-permute-done.10.refs_2_, ...), custom_call_target="tpu_custom_call" | custom-call | tf_op jit(solution)/shard_map/pallas_call | solution.py:399
  140.7 1.4 shard_map.89
  (31 shorter events, 0.3 us)
Async XLA Ops:
  0.0 2.2 %copy-start = (bf16[4,1024,512]{2,1,0:T(8,128)(2,1)S(1)}, bf16[4,1024,512]{2,1,0:T(8,128)(2,1)}, u32[]{:S(2)}) copy-start(bf16[4,1024,512]{2,1,0:T(8,128)(2,1)} %refs_4_.3) | copy-start | bytes 12582916
  2.2 2.2 %copy-start.2 = (bf16[4,1024,512]{2,1,0:T(8,128)(2,1)S(1)}, bf16[4,1024,512]{2,1,0:T(8,128)(2,1)}, u32[]{:S(2)}) copy-start(bf16[4,1024,512]{2,1,0:T(8,128)(2,1)} %refs_5_.3) | copy-start | bytes 12582916
  4.4 0.9 copy-start.4
  5.3 0.7 copy-start.6
  6.0 8.3 %copy-start.5 = (bf16[4,4,4096]{2,1,0:T(4,128)(2,1)S(1)}, bf16[4,4,4096]{2,1,0:T(4,128)(2,1)}, u32[]{:S(2)}) copy-start(bf16[4,4,4096]{2,1,0:T(4,128)(2,1)} %q_ref.3) | copy-start | bytes 393220
  6.0 8.3 %copy-start.8 = (bf16[4,128,512]{2,1,0:T(8,128)(2,1)S(1)}, bf16[4,128,512]{2,1,0:T(8,128)(2,1)}, u32[]{:S(2)}) copy-start(bf16[4,128,512]{2,1,0:T(8,128)(2,1)} %k_ref.3) | copy-start | bytes 1572868
  6.0 8.3 %copy-start.9 = (bf16[4,128,512]{2,1,0:T(8,128)(2,1)S(1)}, bf16[4,128,512]{2,1,0:T(8,128)(2,1)}, u32[]{:S(2)}) copy-start(bf16[4,128,512]{2,1,0:T(8,128)(2,1)} %v_ref.3) | copy-start | bytes 1572868
  6.0 8.3 %copy-start.10 = (s32[4]{0:T(128)S(1)}, s32[4]{0:T(128)}, u32[]{:S(2)}) copy-start(s32[4]{0:T(128)} %lengths_ref.1) | copy-start | bytes 52
  6.0 15.8 %copy-start.7 = (s32[32]{0:T(128)S(1)}, s32[32]{0:T(128)}, u32[]{:S(2)}) copy-start(s32[32]{0:T(128)} %param.10) | copy-start | bytes 388
  8.4 13.4 %collective-permute-start.4 = (bf16[8,1024,256]{2,1,0:T(8,128)(2,1)}, bf16[8,1024,256]{2,1,0:T(8,128)(2,1)}, u32[]{:S(2)}, u32[]{:S(2)}) collective-permute-start(bf16[8,1024,256]{2,1,0:T(8,128)(2,1)} %get-tuple-element.15), channel_id=1, source_target_pairs={{0,2},{2,0},{4,6},{6,4},{8,10},{10,8},{12,14},{14,12},{1,3},{3,1},... | collective-permute-start | bytes 12582920 | tf_op jit(solution)/shard_map/ppermute | solution.py:427
  8.9 8.3 %collective-permute-start = (bf16[16,2176]{1,0:T(8,128)(2,1)S(1)}, bf16[16,2176]{1,0:T(8,128)(2,1)S(1)}, u32[]{:S(2)}, u32[]{:S(2)}) collective-permute-start(bf16[16,2176]{1,0:T(8,128)(2,1)S(1)} %get-tuple-element.13.refs_0_.refs_2_), channel_id=1, source_target_pairs={{0,8},{2,10},{4,12},{6,14},{8,0},{10,2},{12,4},{14,6},{1,9},{3,11}... | collective-permute-start | bytes 208904 | tf_op jit(solution)/shard_map/ppermute | solution.py:427
  12.6 7.1 %collective-permute-start.1 = (bf16[16,2176]{1,0:T(8,128)(2,1)S(1)}, bf16[16,2176]{1,0:T(8,128)(2,1)S(1)}, u32[]{:S(2)}, u32[]{:S(2)}) collective-permute-start(bf16[16,2176]{1,0:T(8,128)(2,1)S(1)} %get-tuple-element.14.pass_ref), channel_id=1, source_target_pairs={{0,10},{2,8},{4,14},{6,12},{8,2},{10,0},{12,6},{14,4},{1,11},{3,9}... | collective-permute-start | bytes 208904 | tf_op jit(solution)/shard_map/ppermute | solution.py:427
  12.7 8.0 %collective-permute-start.2 = (bf16[16,2176]{1,0:T(8,128)(2,1)S(1)}, bf16[16,2176]{1,0:T(8,128)(2,1)S(1)}, u32[]{:S(2)}, u32[]{:S(2)}) collective-permute-start(bf16[16,2176]{1,0:T(8,128)(2,1)S(1)} %get-tuple-element.13.refs_0_.refs_2_), channel_id=1, source_target_pairs={{0,4},{2,6},{4,0},{6,2},{8,12},{10,14},{12,8},{14,10},{1,5},{3,7},... | collective-permute-start | bytes 208904 | tf_op jit(solution)/shard_map/ppermute | solution.py:427
  14.3 7.5 %collective-permute-start.3 = (bf16[16,2176]{1,0:T(8,128)(2,1)S(1)}, bf16[16,2176]{1,0:T(8,128)(2,1)S(1)}, u32[]{:S(2)}, u32[]{:S(2)}) collective-permute-start(bf16[16,2176]{1,0:T(8,128)(2,1)S(1)} %get-tuple-element.14.pass_ref), channel_id=1, source_target_pairs={{0,6},{2,4},{4,2},{6,0},{8,14},{10,12},{12,10},{14,8},{1,7},{3,5},... | collective-permute-start | bytes 208904 | tf_op jit(solution)/shard_map/ppermute | solution.py:427
  17.2 52.8 %collective-permute-start.9 = (bf16[16,2176]{1,0:T(8,128)(2,1)S(1)}, bf16[16,2176]{1,0:T(8,128)(2,1)S(1)}, u32[]{:S(2)}, u32[]{:S(2)}) collective-permute-start(bf16[16,2176]{1,0:T(8,128)(2,1)S(1)} %get-tuple-element.19), channel_id=1, source_target_pairs={{0,2},{2,0},{4,6},{6,4},{8,10},{10,8},{12,14},{14,12},{1,3},{3,1},... | collective-permute-start | bytes 208904 | tf_op jit(solution)/shard_map/ppermute | solution.py:427
  19.7 50.3 %collective-permute-start.7 = (bf16[16,2176]{1,0:T(8,128)(2,1)S(1)}, bf16[16,2176]{1,0:T(8,128)(2,1)S(1)}, u32[]{:S(2)}, u32[]{:S(2)}) collective-permute-start(bf16[16,2176]{1,0:T(8,128)(2,1)S(1)} %collective-permute-done.refs_0_.refs_4_), channel_id=1, source_target_pairs={{0,4},{2,6},{4,0},{6,2},{8,12},{10,14},{12,8},{14,10},{1,5},{3,7},... | collective-permute-start | bytes 208904 | tf_op jit(solution)/shard_map/ppermute | solution.py:427
  20.7 49.4 %collective-permute-start.8 = (bf16[16,2176]{1,0:T(8,128)(2,1)S(1)}, bf16[16,2176]{1,0:T(8,128)(2,1)S(1)}, u32[]{:S(2)}, u32[]{:S(2)}) collective-permute-start(bf16[16,2176]{1,0:T(8,128)(2,1)S(1)} %collective-permute-done.1.refs_1_.refs_5_), channel_id=1, source_target_pairs={{0,4},{2,6},{4,0},{6,2},{8,12},{10,14},{12,8},{14,10},{1,5},{3,7},... | collective-permute-start | bytes 208904 | tf_op jit(solution)/shard_map/ppermute | solution.py:427
  21.8 2.2 %copy-start.1 = (bf16[4,1024,512]{2,1,0:T(8,128)(2,1)S(1)}, bf16[4,1024,512]{2,1,0:T(8,128)(2,1)}, u32[]{:S(2)}) copy-start(bf16[4,1024,512]{2,1,0:T(8,128)(2,1)} %refs_4_.3) | copy-start | bytes 12582916
  24.0 2.2 %copy-start.3 = (bf16[4,1024,512]{2,1,0:T(8,128)(2,1)S(1)}, bf16[4,1024,512]{2,1,0:T(8,128)(2,1)}, u32[]{:S(2)}) copy-start(bf16[4,1024,512]{2,1,0:T(8,128)(2,1)} %refs_5_.3) | copy-start | bytes 12582916
  65.6 73.1 %collective-permute-start.5 = (bf16[32,2176]{1,0:T(8,128)(2,1)S(1)}, bf16[32,2176]{1,0:T(8,128)(2,1)S(1)}, u32[]{:S(2)}, u32[]{:S(2)}) collective-permute-start(bf16[32,2176]{1,0:T(8,128)(2,1)S(1)} %get-tuple-element.17.refs_8_), channel_id=1, source_target_pairs={{0,8},{2,10},{4,12},{6,14},{8,0},{10,2},{12,4},{14,6},{1,9},{3,11}... | collective-permute-start | bytes 417800 | tf_op jit(solution)/shard_map/ppermute | solution.py:427
  68.7 70.0 %collective-permute-start.6 = (bf16[32,2176]{1,0:T(8,128)(2,1)S(1)}, bf16[32,2176]{1,0:T(8,128)(2,1)S(1)}, u32[]{:S(2)}, u32[]{:S(2)}) collective-permute-start(bf16[32,2176]{1,0:T(8,128)(2,1)S(1)} %get-tuple-element.18), channel_id=1, source_target_pairs={{0,4},{2,6},{4,0},{6,2},{8,12},{10,14},{12,8},{14,10},{1,5},{3,7},... | collective-permute-start | bytes 417800 | tf_op jit(solution)/shard_map/ppermute | solution.py:427
  104.3 34.4 %collective-permute-start.10 = (bf16[32,2176]{1,0:T(8,128)(2,1)S(1)}, bf16[32,2176]{1,0:T(8,128)(2,1)S(1)}, u32[]{:S(2)}, u32[]{:S(2)}) collective-permute-start(bf16[32,2176]{1,0:T(8,128)(2,1)S(1)} %shard_map.85.refs_8_), channel_id=1, source_target_pairs={{0,12},{2,14},{4,8},{6,10},{8,4},{10,6},{12,0},{14,2},{1,13},{3,15... | collective-permute-start | bytes 417800 | tf_op jit(solution)/shard_map/ppermute | solution.py:427
  139.1 1.6 %collective-permute-start.11 = (f32[16,2176]{1,0:T(8,128)S(1)}, f32[16,2176]{1,0:T(8,128)S(1)}, u32[]{:S(2)}, u32[]{:S(2)}) collective-permute-start(f32[16,2176]{1,0:T(8,128)S(1)} %shard_map.87), channel_id=1, source_target_pairs={{0,2},{2,0},{4,6},{6,4},{8,10},{10,8},{12,14},{14,12},{1,3},{3,1},... | collective-permute-start | bytes 417800 | tf_op jit(solution)/shard_map/ppermute | solution.py:427

commit v7 on v6

--- a/solution.py
+++ b/solution.py
@@ -14,7 +14,8 @@
 LOG2E = math.log2(math.e)
 NONE = -1e30
 LOW, HIGH = 2.0**-80, 2.0**100
-VMEM = 36 * 1024 * 1024
+VMEM = 121 * 1024 * 1024 // 2
+SMALL = 16 * 1024 * 1024
 ROWS_STEP = 512
 
 
@@ -38,8 +39,8 @@
     return arrays[0] if len(arrays) == 1 else jnp.concatenate(arrays, axis=0)
 
 
-def params():
-    return pltpu.CompilerParams(vmem_limit_bytes=VMEM)
+def params(limit=VMEM):
+    return pltpu.CompilerParams(vmem_limit_bytes=limit)
 
 
 def flat(x):
@@ -49,21 +50,9 @@
 ANY = pl.BlockSpec(memory_space=pl.ANY)
 
 
-def pack_kernel(q_ref, selected_ref, k_ref, v_ref, mine_ref, other_ref, out_ref, held, in_sems, out_sems):
-    blocks, _, kv_columns = k_ref.shape
-    kv_half = kv_columns // 2
+def pack_kernel(q_ref, selected_ref, mine_ref, other_ref):
     half = q_ref.shape[2] // 2
     core = lax.axis_index("ctx") % 2
-    kv_start = pl.multiple_of((1 - core) * kv_half, LANES)
-    reads, writes = [], []
-    for n, ref in enumerate((k_ref, v_ref)):
-        for b in range(blocks):
-            m = n * blocks + b
-            source = ref.at[b, :, pl.ds(kv_start, kv_half)]
-            reads.append(pltpu.make_async_copy(source, held.at[m], in_sems.at[m]))
-            writes.append(pltpu.make_async_copy(held.at[m], out_ref.at[m], out_sems.at[m]))
-    for read in reads:
-        read.start()
     ids = flat(selected_ref[...])
     pad = jnp.full((ids.shape[0], LANES - ids.shape[1]), -1.0, jnp.float32)
     ids = jnp.concatenate([ids, pad], axis=1).astype(jnp.bfloat16)
@@ -71,38 +60,20 @@
         start = pl.multiple_of(which * half, LANES)
         ref[:, :half] = flat(q_ref[:, :, pl.ds(start, half)]).astype(jnp.bfloat16)
         ref[:, half:] = ids
-    for read, write in zip(reads, writes):
-        read.wait()
-        write.start()
-    for write in writes:
-        write.wait()
-
-
-def pack(queries, selected, cache_k, cache_v):
+
+
+def pack(queries, selected):
     rows, steps, width = queries.shape
-    blocks, tokens, columns = cache_k.shape
     shape = jax.ShapeDtypeStruct((rows * steps, width // 2 + LANES), jnp.bfloat16)
-    kv_shape = (2 * blocks, tokens, columns // 2)
-    whole = pl.BlockSpec(memory_space=pltpu.VMEM)
-    return pl.pallas_call(
-        pack_kernel,
-        in_specs=[whole, whole, ANY, ANY],
-        out_specs=[whole, whole, ANY],
-        out_shape=[shape, shape, jax.ShapeDtypeStruct(kv_shape, jnp.bfloat16)],
-        scratch_shapes=[
-            pltpu.VMEM(kv_shape, jnp.bfloat16),
-            pltpu.SemaphoreType.DMA((2 * blocks,)),
-            pltpu.SemaphoreType.DMA((2 * blocks,)),
-        ],
-        compiler_params=params(),
-    )(queries, selected, cache_k, cache_v)
-
-
-def block_kernel(pieces, group_size, step, where_ref, place_ref, *refs):
+    return pl.pallas_call(pack_kernel, out_shape=[shape, shape], compiler_params=params())(
+        queries, selected
+    )
+
+
+def block_kernel(pieces, outs, group_size, step, where_ref, place_ref, *refs):
     q_refs = refs[:pieces]
     id_refs = refs[pieces : 2 * pieces]
     own_k, own_v, next_k, next_v = refs[2 * pieces : 2 * pieces + 4]
-    outs = max(1, pieces // 2)
     out_refs = refs[-2 - outs : -2]
     logs_ref, s_ref = refs[-2:]
     kv = pl.program_id(1)
@@ -200,30 +171,25 @@
             ref[:, heads * HD :] = parts[n * kept : (n + 1) * kept]
 
 
-def attend_blocks(where, place, queries, cache_k, cache_v, halves, group_size, after):
+def attend_blocks(where, place, caches, group_size, queries, outs, after):
     pieces = len(queries)
     rows, columns = queries[0].shape
-    blocks, tokens, kv_width = cache_k.shape
+    blocks, tokens, kv_width = caches[0].shape
     kv_half = kv_width // HD // 2
     share = min(rows, 64)
     items = share * pieces
-    outs = max(1, pieces // 2)
-    own = pl.BlockSpec((blocks, tokens, HD), lambda i, g, w: (0, 0, w[2] * kv_half + g))
+    cache_block = pl.BlockSpec((blocks, tokens, HD), lambda i, g, w: (0, 0, w[2] * kv_half + g))
     queries_block = pl.BlockSpec((share, group_size * HD), lambda i, g, w: (i, g))
     ids_block = pl.BlockSpec((share, LANES), lambda i, g, w: (i, columns // LANES - 1))
     return pl.pallas_call(
-        functools.partial(block_kernel, pieces, group_size, min(group_size, max(1, ROWS_STEP // items))),
+        functools.partial(block_kernel, pieces, outs, group_size, min(group_size, max(1, ROWS_STEP // items))),
         grid_spec=pltpu.PrefetchScalarGridSpec(
             num_scalar_prefetch=1,
             grid=(rows // share, kv_half),
             in_specs=[pl.BlockSpec(place.shape, lambda i, g, w: (0, 0))]
             + [queries_block] * pieces
             + [ids_block] * pieces
-            + [own, own]
-            + [
-                pl.BlockSpec((blocks, tokens, HD), lambda i, g, w: (0, 0, g)),
-                pl.BlockSpec((blocks, tokens, HD), lambda i, g, w: (1, 0, g)),
-            ]
+            + [cache_block] * 4
             + [pl.BlockSpec(memory_space=pl.ANY)] * len(after),
             out_specs=[pl.BlockSpec((items // outs, columns), lambda i, g, w: (i, 0))] * outs,
             scratch_shapes=[
@@ -238,11 +204,10 @@
             bytes_accessed=4 * rows * pieces * columns,
             transcendentals=rows * pieces * columns,
         ),
-    )(where, place, *queries, *queries, cache_k, cache_v, halves, halves, *after)
-
-
-def suffix_kernel(group_size, lengths_ref, q_ref, k_ref, v_ref, pass_ref, out_ref, log_ref, passed_ref):
-    passed_ref[...] = pass_ref[...]
+    )(where, place, *queries, *queries, *caches, *after)
+
+
+def suffix_kernel(group_size, lengths_ref, q_ref, k_ref, v_ref, out_ref, log_ref):
     rows_here, steps, width = q_ref.shape
     tokens = k_ref.shape[1]
     kv_here = k_ref.shape[2] // HD
@@ -281,7 +246,7 @@
         log_ref[side] = logs[side]
 
 
-def attend_suffix(lengths, queries, suffix_k, suffix_v, passing):
+def attend_suffix(lengths, queries, suffix_k, suffix_v):
     rows, steps, width = queries.shape
     _, tokens, kv_width = suffix_k.shape
     items = rows * steps
@@ -291,18 +256,15 @@
         grid_spec=pltpu.PrefetchScalarGridSpec(
             num_scalar_prefetch=1,
             grid=(1,),
-            in_specs=[pl.BlockSpec(x.shape, whole) for x in (queries, suffix_k, suffix_v)]
-            + [pl.BlockSpec(passing.shape, lambda i, n: (0, 0))],
+            in_specs=[pl.BlockSpec(x.shape, whole) for x in (queries, suffix_k, suffix_v)],
             out_specs=[
                 pl.BlockSpec((items, width), lambda i, n: (0, 0)),
                 pl.BlockSpec((2, items, LANES), whole),
-                pl.BlockSpec(passing.shape, lambda i, n: (0, 0)),
             ],
         ),
         out_shape=(
             jax.ShapeDtypeStruct((items, width), jnp.float32),
             jax.ShapeDtypeStruct((2, items, LANES), jnp.float32),
-            jax.ShapeDtypeStruct(passing.shape, passing.dtype),
         ),
         compiler_params=params(),
         cost_estimate=pl.CostEstimate(
@@ -310,7 +272,7 @@
             bytes_accessed=4 * suffix_k.size + 6 * items * width,
             transcendentals=items * rows * tokens * width // HD,
         ),
-    )(lengths, queries, suffix_k, suffix_v, passing)
+    )(lengths, queries, suffix_k, suffix_v)
 
 
 def weigh(parts, items, heads):
@@ -334,85 +296,70 @@
     return [factor * inverse for factor in factors], top + jnp.log(total)
 
 
-def parts_of(refs, items, side):
-    return [(ref, start + side * items) for ref in refs for start in range(0, ref.shape[0], 2 * items)]
-
-
-def other_kernel(*refs):
-    out_ref = refs[-1]
-    items = out_ref.shape[0]
-    columns = out_ref.shape[1] - LANES
+def merge_kernel(sides, *refs):
+    out_refs = refs[-len(sides) :]
+    items, columns = out_refs[0].shape
+    columns -= LANES
     heads = columns // HD
-    parts = parts_of(refs[:-1], items, 1)
-    factors, log = shares(weigh(parts, items, heads))
-    for h in range(heads):
-        span = slice(h * HD, (h + 1) * HD)
-        acc = jnp.zeros((items, HD), jnp.float32)
-        for factor, (ref, start) in zip(factors, parts):
-            acc += factor[:, h : h + 1] * ref[start : start + items, span].astype(jnp.float32)
-        out_ref[:, span] = acc
     pad = jnp.zeros((items, LANES - heads), jnp.float32)
-    out_ref[:, columns:] = jnp.concatenate([log, pad], axis=1)
-
-
-def merge_other(back, items):
+    taken = 0
+    for count, out_ref in zip(sides, out_refs):
+        back_refs = refs[taken : taken + count]
+        taken += count
+        parts = [(ref, start) for ref in back_refs for start in range(0, ref.shape[0], items)]
+        factors, log = shares(weigh(parts, items, heads))
+        for h in range(heads):
+            span = slice(h * HD, (h + 1) * HD)
+            acc = jnp.zeros((items, HD), jnp.float32)
+            for factor, (ref, start) in zip(factors, parts):
+                acc += factor[:, h : h + 1] * ref[start : start + items, span].astype(jnp.float32)
+            out_ref[:, span] = acc
+        out_ref[:, columns:] = jnp.concatenate([log, pad], axis=1)
+
+
+def merge(sides, items, after):
+    arrays = [x for side in sides for x in side]
+    shape = jax.ShapeDtypeStruct((items, arrays[0].shape[1]), jnp.float32)
     return pl.pallas_call(
-        other_kernel,
-        out_shape=jax.ShapeDtypeStruct((items, back[0].shape[1]), jnp.float32),
-        compiler_params=params(),
-    )(*back)
-
-
-def finish_kernel(arrays, own, where_ref, *refs):
-    back_refs = refs[:arrays]
-    out_s_ref, log_s_ref = refs[arrays : arrays + 2]
-    out_ref = refs[-1]
-    rows, steps, columns = out_ref.shape
+        functools.partial(merge_kernel, [len(side) for side in sides]),
+        in_specs=[pl.BlockSpec(memory_space=pltpu.VMEM)] * len(arrays) + [ANY] * len(after),
+        out_shape=[shape, shape],
+        compiler_params=params(SMALL),
+        cost_estimate=pl.CostEstimate(
+            flops=1 << 30, bytes_accessed=8 * shape.size, transcendentals=items
+        ),
+    )(*arrays, *after)
+
+
+def finish_kernel(late, *refs):
+    out_s_ref, log_s_ref, out_ref = refs[-3:]
+    rows, steps, width = out_ref.shape
     items = rows * steps
+    columns = width // 2
     heads = columns // HD
-    log_s = log_s_ref[0][:, :heads]
-    if own:
-        parts = parts_of(back_refs, items, 0)
-        logs = weigh(parts, items, heads)
-    else:
-        parts = [(back_refs[0], 0)]
-        logs = [back_refs[0][:, columns : columns + heads]]
-    factors, _ = shares([log_s] + logs)
-    for h in range(heads):
-        span = slice(h * HD, (h + 1) * HD)
-        acc = factors[0][:, h : h + 1] * out_s_ref[:, span]
-        for factor, (ref, start) in zip(factors[1:], parts):
-            acc += factor[:, h : h + 1] * ref[start : start + items, span].astype(jnp.float32)
-        for row in range(rows):
-            out_ref[row, :, span] = acc[row * steps : (row + 1) * steps].astype(jnp.bfloat16)
-
-
-def finish(where, back, out_s, log_s, shape, so_far):
-    rows, steps, width = shape
-    items = rows * steps
-    own = so_far is None
-    others = [] if own else [so_far]
-
-    def side(w):
-        return w[2] if own else 1 - w[2]
-
+    core = lax.axis_index("ctx") % 2
+    for side, which in ((0, core), (1, 1 - core)):
+        merged_ref, *late_refs = refs[side * (late + 1) : (side + 1) * (late + 1)]
+        parts = [(ref, 0) for ref in late_refs]
+        logs = [log_s_ref[which][:, :heads], merged_ref[:, columns : columns + heads]]
+        factors, _ = shares(logs + weigh(parts, items, heads))
+        for h in range(heads):
+            here = slice(h * HD, (h + 1) * HD)
+            span = pl.ds(pl.multiple_of(which * columns + h * HD, HD), HD)
+            acc = factors[0][:, h : h + 1] * out_s_ref[:, span]
+            acc += factors[1][:, h : h + 1] * merged_ref[:, here]
+            for factor, (ref, _) in zip(factors[2:], parts):
+                acc += factor[:, h : h + 1] * ref[:, here].astype(jnp.float32)
+            for row in range(rows):
+                out_ref[row, :, span] = acc[row * steps : (row + 1) * steps].astype(jnp.bfloat16)
+
+
+def finish(own, other, out_s, log_s, shape):
     return pl.pallas_call(
-        functools.partial(finish_kernel, len(back), own),
-        grid_spec=pltpu.PrefetchScalarGridSpec(
-            num_scalar_prefetch=1,
-            grid=(1,),
-            in_specs=[pl.BlockSpec(x.shape, lambda i, w: (0, 0)) for x in back]
-            + [
-                pl.BlockSpec((items, width // 2), lambda i, w: (0, side(w))),
-                pl.BlockSpec((1,) + log_s.shape[1:], lambda i, w: (side(w), 0, 0)),
-            ]
-            + [ANY] * len(others),
-            out_specs=pl.BlockSpec((rows, steps, width // 2), lambda i, w: (0, 0, side(w))),
-        ),
+        functools.partial(finish_kernel, len(own) - 1),
         out_shape=jax.ShapeDtypeStruct(shape, jnp.bfloat16),
-        input_output_aliases={} if own else {len(back) + 3: 0},
-        compiler_params=params(),
-    )(where, *back, out_s, log_s, *others)
+        compiler_params=params(SMALL),
+    )(*own, *other, out_s, log_s)
 
 
 def local(queries, selected, placement, lengths, cache_k, cache_v, suffix_k, suffix_v):
@@ -429,38 +376,31 @@
     own = lax.axis_index("ctx")
     where = jnp.stack([own * blocks_here, (own ^ 1) * blocks_here, own & 1]).astype(jnp.int32)
     place = placement.reshape(1, -1)
-    *packed, halves = pack(queries, selected, cache_k, cache_v)
-    halves = swap(halves, 1)
-    out_s, log_s, passed = attend_suffix(lengths, queries, suffix_k, suffix_v, packed[1])
-    attend = functools.partial(attend_blocks, where, place)
-    if chips <= 4:
-        calls = [[2, 1], [3], [0]] if chips == 4 else [[k] for k in range(chips - 1, -1, -1)]
-        arrived = {0: [packed[0], swap(passed, 1)]}
-        for k in range(1, chips):
-            if k == 3:
-                arrived[k] = [swap(x, 2) for x in arrived[2]]
-            else:
-                arrived[k] = [swap(packed[0], 2 * k), swap(packed[1], 2 * k + 1)]
-        back = []
-        after = [log_s]
-        for call in calls:
-            pieces = [piece for k in call for piece in arrived[k]]
-            partial = attend(pieces, cache_k, cache_v, halves, group_size, after)
-            after = [partial[0], arrived[0][1]]
-            back += [swap(x, 2 * k) for k, x in zip(call, partial)]
+    caches = [cache_k, cache_v, swap(cache_k, 1), swap(cache_v, 1)]
+    packed = pack(queries, selected)
+    chip = jnp.concatenate([packed[0], swap(packed[1], 1)], axis=0)
+    out_s, log_s = attend_suffix(lengths, queries, suffix_k, suffix_v)
+    attend = functools.partial(attend_blocks, where, place, caches, group_size)
+    if chips == 4:
+        far, near = swap(chip, 4), swap(chip, 2)
+        farthest = swap(far, 2)
+        first = attend([far, near], 4, [log_s])
+        sides = [[swap(first[n], 4 + n), swap(first[2 + n], 2 + n)] for n in range(2)]
+        last = attend([farthest, chip], 4, [first[0]])
+        late = [[swap(last[n], 6 + n), swap(last[2 + n], n)] for n in range(2)]
+        after = [last[2]]
     else:
         same = [[2 * z + core for z in range(chips)] for core in range(2)]
-        chip = jnp.concatenate([packed[0], swap(passed, 1)], axis=0)
         every = lax.all_gather(chip, "ctx", axis=0, tiled=True, axis_index_groups=same)
-        (partial,) = attend([every], cache_k, cache_v, halves, group_size, [log_s])
-        back = [
-            lax.all_to_all(
-                partial, "ctx", split_axis=0, concat_axis=0, tiled=True, axis_index_groups=same
-            )
-        ]
-    other = swap(merge_other(back, items), 1)
-    half = finish(where, back, out_s, log_s, queries.shape, None)
-    return finish(where, [other], out_s, log_s, queries.shape, half)
+        (partial,) = attend([every], 1, [log_s])
+        back = lax.all_to_all(
+            partial, "ctx", split_axis=0, concat_axis=0, tiled=True, axis_index_groups=same
+        ).reshape(chips, 2, items, -1)
+        sides = [[swap(back[:, n].reshape(chips * items, -1), n)] for n in range(2)]
+        late, after = [[], []], []
+    merged = merge(sides, items, after)
+    own, other = ([x] + y for x, y in zip(merged, late))
+    return finish(own, other, out_s, log_s, queries.shape)
 
 
 def solution(mesh):

time: 142 us -> 122 us (0.86)
  Pallas kernels: 115 us -> 88.1 us
  waiting for transfers between devices: 3.64 us -> 13.4 us
  local copies, waits for them, and re-layouts: 10.4 us -> 3.09 us
  starting transfers between devices: 12.7 us -> 16.3 us
    pallas_call x7 -> x5, Pallas kernels: 113 us -> 84.3 us  [the longest x2 81 us: attend_blocks(): pl.pallas_call(functools.partial(block_kernel, pieces, outs, group_size,...]
    ppermute x12 -> x13, waiting for transfers between devices: 3.64 us -> 13.4 us  [swap(): lax.ppermute(x, 'ctx', [(i, i ^ bits) for i in range(size)])]
    unnamed x22 -> x15, local copies, waits for them, and re-layouts: 10.4 us -> 3.08 us
    ppermute x12 -> x13, starting transfers between devices: 12.7 us -> 16.3 us  [swap(): lax.ppermute(x, 'ctx', [(i, i ^ bits) for i in range(size)])]
    pallas_call x1, Pallas kernels: 1.74 us -> 3.81 us  [attend_suffix(): pl.pallas_call(functools.partial(suffix_kernel, width // kv_width), grid_...]
  transfers between devices with their start and end apart: 12 -> 13, of which waited for: 2 -> 4; matrix products, arithmetic and copies ran while one was open for 0% -> 1% of each run, Pallas kernels for 78% -> 71%
where the time goes in v7:
time: 122 us
  Pallas kernels  88.1 us (72%)
  starting transfers between devices  16.3 us (13%)
  waiting for transfers between devices  13.4 us (11%)
  local copies, waits for them, and re-layouts  3.09 us (3%)
    pallas_call x2, Pallas kernels, attend_blocks(): pl.pallas_call(functools.partial(block_kernel, pieces, outs, group_size,...  81 us
    ppermute x13, starting transfers between devices, swap(): lax.ppermute(x, 'ctx', [(i, i ^ bits) for i in range(size)])  16.3 us
    ppermute x13, waiting for transfers between devices, swap(): lax.ppermute(x, 'ctx', [(i, i ^ bits) for i in range(size)])  13.4 us
    pallas_call x1, Pallas kernels, attend_suffix(): pl.pallas_call(functools.partial(suffix_kernel, width // kv_width), grid_...  3.81 us
    unnamed x15, local copies, waits for them, and re-layouts  3.08 us
  transfers between devices with their start and end apart: 13, of which 4 were waited for; matrix products, arithmetic and copies ran while one was open for 1% of the time, Pallas kernels for 71%

profile of v7, /device:TPU:0, one launch (start us, length us, event | category | flops | bytes accessed | tf_op | source)
XLA Modules:
  0.0 121.6 jit_solution(5531609019435069417)
XLA Ops:
  0.0 0.5 collective-permute-start.3
  0.5 1.6 %shard_map.82 = (bf16[16,2176]{1,0:T(8,128)(2,1)}, bf16[16,2176]{1,0:T(8,128)(2,1)}) custom-call(bf16[4,4,4096]{2,1,0:T(4,128)(2,1)} %q_ref.3, s32[4,4,16]{2,1,0:T(4,128)} %selected_ref.1), custom_call_target="tpu_custom_call" | custom-call | tf_op jit(solution)/shard_map/pallas_call | solution.py:68
  2.5 0.9 constant_dynamic-update-slice_fusion.1
  3.4 4.2 %collective-permute-done = bf16[16,2176]{1,0:T(8,128)(2,1)S(1)} collective-permute-done((bf16[16,2176]{1,0:T(8,128)(2,1)}, bf16[16,2176]{1,0:T(8,128)(2,1)S(1)}, u32[]{:S(2)}, u32[]{:S(2)}) %collective-permute-start) | collective-permute-done | bytes 69664 | tf_op jit(solution)/shard_map/ppermute | solution.py:374
  7.7 4.0 %collective-permute-start.1 = (bf16[32,2176]{1,0:T(8,128)(2,1)S(1)}, bf16[32,2176]{1,0:T(8,128)(2,1)S(1)}, u32[]{:S(2)}, u32[]{:S(2)}) collective-permute-start(bf16[32,2176]{1,0:T(8,128)(2,1)S(1)} %constant_dynamic-update-slice_fusion.refs_1_.refs_3_), channel_id=1, source_target_pairs={{0,8},{2,10},{4,12},{6,14},{8,0},{10,2},{12,4},{14,6},{1,9},{3,11}... | collective-permute-start | bytes 417800 | tf_op jit(solution)/shard_map/ppermute | solution.py:374
  11.7 1.6 %collective-permute-start.2 = (bf16[32,2176]{1,0:T(8,128)(2,1)S(1)}, bf16[32,2176]{1,0:T(8,128)(2,1)S(1)}, u32[]{:S(2)}, u32[]{:S(2)}) collective-permute-start(bf16[32,2176]{1,0:T(8,128)(2,1)S(1)} %constant_dynamic-update-slice_fusion.refs_1_.refs_3_), channel_id=1, source_target_pairs={{0,4},{2,6},{4,0},{6,2},{8,12},{10,14},{12,8},{14,10},{1,5},{3,7},... | collective-permute-start | bytes 417800 | tf_op jit(solution)/shard_map/ppermute | solution.py:374
  13.3 5.5 %collective-permute-done.1.refs_0_.refs_2_ = bf16[32,2176]{1,0:T(8,128)(2,1)S(1)} collective-permute-done((bf16[32,2176]{1,0:T(8,128)(2,1)S(1)}, bf16[32,2176]{1,0:T(8,128)(2,1)S(1)}, u32[]{:S(2)}, u32[]{:S(2)}) %collective-permute-start.1) | collective-permute-done | bytes 139296 | tf_op jit(solution)/shard_map/ppermute | solution.py:374
  18.8 0.6 collective-permute-start.9
  19.4 0.6 pad_add_fusion.where_ref
  20.0 3.8 %shard_map.83 = (f32[16,4096]{1,0:T(8,128)}, f32[2,16,128]{2,1,0:T(8,128)}) custom-call(s32[4]{0:T(128)} %lengths_ref.1, bf16[4,4,4096]{2,1,0:T(4,128)(2,1)} %q_ref.3, bf16[4,128,512]{2,1,0:T(8,128)(2,1)} %k_ref.1, bf16[4,128,512]{2,1,0:T(8,128)(2,1)} %v_ref.1), custom_call_target="tpu_custom_call" | custom-call | flops 536870912 | bytes 1441792 | tf_op jit(solution)/shard_map/pallas_call | solution.py:254
  23.8 0.6 copy-done.6
  24.4 40.5 %shard_map.84 = (bf16[16,2176]{1,0:T(8,128)(2,1)}, bf16[16,2176]{1,0:T(8,128)(2,1)}, bf16[16,2176]{1,0:T(8,128)(2,1)}, bf16[16,2176]{1,0:T(8,128)(2,1)}) custom-call(s32[3]{0:T(128)} %pad_add_fusion.where_ref, s32[1,32]{1,0:T(1,128)} %bitcast.4, bf16[32,2176]{1,0:T(8,128)(2,1)} %copy-done.4, bf16[32,2176]{1,0:T(8,128)(2,1)} %copy-done.6, ...), custom_call_target="tpu_custom_call" | custom-call | flops 142606336 | bytes 557056 | tf_op jit(solution)/shard_map/pallas_call | solution.py:184
  64.9 1.5 %collective-permute-start.6 = (bf16[16,2176]{1,0:T(8,128)(2,1)}, bf16[16,2176]{1,0:T(8,128)(2,1)S(1)}, u32[]{:S(2)}, u32[]{:S(2)}) collective-permute-start(bf16[16,2176]{1,0:T(8,128)(2,1)} %get-tuple-element.23), channel_id=1, source_target_pairs={{0,4},{2,6},{4,0},{6,2},{8,12},{10,14},{12,8},{14,10},{1,5},{3,7},... | collective-permute-start | bytes 208904 | tf_op jit(solution)/shard_map/ppermute | solution.py:374
  66.4 1.4 %collective-permute-start.7 = (bf16[16,2176]{1,0:T(8,128)(2,1)}, bf16[16,2176]{1,0:T(8,128)(2,1)S(1)}, u32[]{:S(2)}, u32[]{:S(2)}) collective-permute-start(bf16[16,2176]{1,0:T(8,128)(2,1)} %get-tuple-element.24), channel_id=1, source_target_pairs={{0,10},{2,8},{4,14},{6,12},{8,2},{10,0},{12,6},{14,4},{1,11},{3,9}... | collective-permute-start | bytes 208904 | tf_op jit(solution)/shard_map/ppermute | solution.py:374
  67.8 2.3 %collective-permute-start.8 = (bf16[16,2176]{1,0:T(8,128)(2,1)}, bf16[16,2176]{1,0:T(8,128)(2,1)S(1)}, u32[]{:S(2)}, u32[]{:S(2)}) collective-permute-start(bf16[16,2176]{1,0:T(8,128)(2,1)} %get-tuple-element.25), channel_id=1, source_target_pairs={{0,6},{2,4},{4,2},{6,0},{8,14},{10,12},{12,10},{14,8},{1,7},{3,5},... | collective-permute-start | bytes 208904 | tf_op jit(solution)/shard_map/ppermute | solution.py:374
  70.1 0.7 copy-done.5
  70.8 40.5 %shard_map.85 = (bf16[16,2176]{1,0:T(8,128)(2,1)}, bf16[16,2176]{1,0:T(8,128)(2,1)}, bf16[16,2176]{1,0:T(8,128)(2,1)}, bf16[16,2176]{1,0:T(8,128)(2,1)}) custom-call(s32[3]{0:T(128)} %pad_add_fusion.where_ref, s32[1,32]{1,0:T(1,128)} %bitcast.5, bf16[32,2176]{1,0:T(8,128)(2,1)} %copy-done.5, bf16[32,2176]{1,0:T(8,128)(2,1)} %copy-done.3, ...), custom_call_target="tpu_custom_call" | custom-call | flops 142606336 | bytes 557056 | tf_op jit(solution)/shard_map/pallas_call | solution.py:184
  111.3 2.5 %collective-permute-start.10 = (bf16[16,2176]{1,0:T(8,128)(2,1)}, bf16[16,2176]{1,0:T(8,128)(2,1)S(1)}, u32[]{:S(2)}, u32[]{:S(2)}) collective-permute-start(bf16[16,2176]{1,0:T(8,128)(2,1)} %get-tuple-element.28), channel_id=1, source_target_pairs={{0,12},{2,14},{4,8},{6,10},{8,4},{10,6},{12,0},{14,2},{1,13},{3,15... | collective-permute-start | bytes 208904 | tf_op jit(solution)/shard_map/ppermute | solution.py:374
  113.8 0.8 collective-permute-start.11
  114.6 0.7 collective-permute-start.12
  115.3 0.9 copy-done.1
  116.6 1.1 collective-permute-done.10.refs_1_
  117.7 2.6 %collective-permute-done.11.refs_4_ = bf16[16,2176]{1,0:T(8,128)(2,1)S(1)} collective-permute-done((bf16[16,2176]{1,0:T(8,128)(2,1)}, bf16[16,2176]{1,0:T(8,128)(2,1)S(1)}, u32[]{:S(2)}, u32[]{:S(2)}) %collective-permute-start.11) | collective-permute-done | bytes 69664 | tf_op jit(solution)/shard_map/ppermute | solution.py:374
  120.3 1.3 %shard_map.87 = bf16[4,4,4096]{2,1,0:T(4,128)(2,1)} custom-call(f32[16,2176]{1,0:T(8,128)S(1)} %get-tuple-element.27.refs_0_, bf16[16,2176]{1,0:T(8,128)(2,1)S(1)} %collective-permute-done.10.refs_1_, bf16[16,2176]{1,0:T(8,128)(2,1)S(1)} %copy-done.1, f32[16,2176]{1,0:T(8,128)S(1)} %get-tuple-element.29.refs_3_, ...), custom_call_target="tpu_custom_call" | custom-call | tf_op jit(solution)/shard_map/pallas_call | solution.py:358
  (25 shorter events, 1.0 us)
Async XLA Ops:
  0.0 23.8 %collective-permute-start.3 = (bf16[4,1024,512]{2,1,0:T(8,128)(2,1)}, bf16[4,1024,512]{2,1,0:T(8,128)(2,1)}, u32[]{:S(2)}, u32[]{:S(2)}) collective-permute-start(bf16[4,1024,512]{2,1,0:T(8,128)(2,1)} %refs_4_.3), channel_id=1, source_target_pairs={{0,2},{2,0},{4,6},{6,4},{8,10},{10,8},{12,14},{14,12},{1,3},{3,1},... | collective-permute-start | bytes 12582920 | tf_op jit(solution)/shard_map/ppermute | solution.py:374
  0.5 23.3 %collective-permute-start.4 = (bf16[4,1024,512]{2,1,0:T(8,128)(2,1)}, bf16[4,1024,512]{2,1,0:T(8,128)(2,1)}, u32[]{:S(2)}, u32[]{:S(2)}) collective-permute-start(bf16[4,1024,512]{2,1,0:T(8,128)(2,1)} %refs_5_.3), channel_id=1, source_target_pairs={{0,2},{2,0},{4,6},{6,4},{8,10},{10,8},{12,14},{14,12},{1,3},{3,1},... | collective-permute-start | bytes 12582920 | tf_op jit(solution)/shard_map/ppermute | solution.py:374
  2.1 5.6 %collective-permute-start = (bf16[16,2176]{1,0:T(8,128)(2,1)}, bf16[16,2176]{1,0:T(8,128)(2,1)S(1)}, u32[]{:S(2)}, u32[]{:S(2)}) collective-permute-start(bf16[16,2176]{1,0:T(8,128)(2,1)} %get-tuple-element.20), channel_id=1, source_target_pairs={{0,2},{2,0},{4,6},{6,4},{8,10},{10,8},{12,14},{14,12},{1,3},{3,1},... | collective-permute-start | bytes 208904 | tf_op jit(solution)/shard_map/ppermute | solution.py:374
  7.7 57.3 %copy-start.3 = (bf16[32,2176]{1,0:T(8,128)(2,1)}, bf16[32,2176]{1,0:T(8,128)(2,1)S(1)}, u32[]{:S(2)}) copy-start(bf16[32,2176]{1,0:T(8,128)(2,1)S(1)} %constant_dynamic-update-slice_fusion.refs_1_.refs_3_) | copy-start | bytes 417796
  7.7 11.1 %collective-permute-start.1 = (bf16[32,2176]{1,0:T(8,128)(2,1)S(1)}, bf16[32,2176]{1,0:T(8,128)(2,1)S(1)}, u32[]{:S(2)}, u32[]{:S(2)}) collective-permute-start(bf16[32,2176]{1,0:T(8,128)(2,1)S(1)} %constant_dynamic-update-slice_fusion.refs_1_.refs_3_), channel_id=1, source_target_pairs={{0,8},{2,10},{4,12},{6,14},{8,0},{10,2},{12,4},{14,6},{1,9},{3,11}... | collective-permute-start | bytes 417800 | tf_op jit(solution)/shard_map/ppermute | solution.py:374
  11.7 12.1 %collective-permute-start.2 = (bf16[32,2176]{1,0:T(8,128)(2,1)S(1)}, bf16[32,2176]{1,0:T(8,128)(2,1)S(1)}, u32[]{:S(2)}, u32[]{:S(2)}) collective-permute-start(bf16[32,2176]{1,0:T(8,128)(2,1)S(1)} %constant_dynamic-update-slice_fusion.refs_1_.refs_3_), channel_id=1, source_target_pairs={{0,4},{2,6},{4,0},{6,2},{8,12},{10,14},{12,8},{14,10},{1,5},{3,7},... | collective-permute-start | bytes 417800 | tf_op jit(solution)/shard_map/ppermute | solution.py:374
  18.7 5.0 %copy-start.4 = (bf16[32,2176]{1,0:T(8,128)(2,1)}, bf16[32,2176]{1,0:T(8,128)(2,1)S(1)}, u32[]{:S(2)}) copy-start(bf16[32,2176]{1,0:T(8,128)(2,1)S(1)} %collective-permute-done.1.refs_0_.refs_2_) | copy-start | bytes 417796
  18.8 51.4 %collective-permute-start.9 = (bf16[32,2176]{1,0:T(8,128)(2,1)S(1)}, bf16[32,2176]{1,0:T(8,128)(2,1)S(1)}, u32[]{:S(2)}, u32[]{:S(2)}) collective-permute-start(bf16[32,2176]{1,0:T(8,128)(2,1)S(1)} %collective-permute-done.1.refs_0_.refs_2_), channel_id=1, source_target_pairs={{0,4},{2,6},{4,0},{6,2},{8,12},{10,14},{12,8},{14,10},{1,5},{3,7},... | collective-permute-start | bytes 417800 | tf_op jit(solution)/shard_map/ppermute | solution.py:374
  23.8 0.7 copy-start.6
  64.9 48.9 %collective-permute-start.6 = (bf16[16,2176]{1,0:T(8,128)(2,1)}, bf16[16,2176]{1,0:T(8,128)(2,1)S(1)}, u32[]{:S(2)}, u32[]{:S(2)}) collective-permute-start(bf16[16,2176]{1,0:T(8,128)(2,1)} %get-tuple-element.23), channel_id=1, source_target_pairs={{0,4},{2,6},{4,0},{6,2},{8,12},{10,14},{12,8},{14,10},{1,5},{3,7},... | collective-permute-start | bytes 208904 | tf_op jit(solution)/shard_map/ppermute | solution.py:374
  66.4 48.2 %collective-permute-start.7 = (bf16[16,2176]{1,0:T(8,128)(2,1)}, bf16[16,2176]{1,0:T(8,128)(2,1)S(1)}, u32[]{:S(2)}, u32[]{:S(2)}) collective-permute-start(bf16[16,2176]{1,0:T(8,128)(2,1)} %get-tuple-element.24), channel_id=1, source_target_pairs={{0,10},{2,8},{4,14},{6,12},{8,2},{10,0},{12,6},{14,4},{1,11},{3,9}... | collective-permute-start | bytes 208904 | tf_op jit(solution)/shard_map/ppermute | solution.py:374
  67.8 47.5 %collective-permute-start.8 = (bf16[16,2176]{1,0:T(8,128)(2,1)}, bf16[16,2176]{1,0:T(8,128)(2,1)S(1)}, u32[]{:S(2)}, u32[]{:S(2)}) collective-permute-start(bf16[16,2176]{1,0:T(8,128)(2,1)} %get-tuple-element.25), channel_id=1, source_target_pairs={{0,6},{2,4},{4,2},{6,0},{8,14},{10,12},{12,10},{14,8},{1,7},{3,5},... | collective-permute-start | bytes 208904 | tf_op jit(solution)/shard_map/ppermute | solution.py:374
  70.1 50.2 %copy-start = (f32[16,4096]{1,0:T(8,128)S(1)}, f32[16,4096]{1,0:T(8,128)}, u32[]{:S(2)}) copy-start(f32[16,4096]{1,0:T(8,128)} %get-tuple-element.32.refs_6_) | copy-start | bytes 786436
  70.1 50.2 %copy-start.2 = (f32[2,16,128]{2,1,0:T(8,128)S(1)}, f32[2,16,128]{2,1,0:T(8,128)}, u32[]{:S(2)}) copy-start(f32[2,16,128]{2,1,0:T(8,128)} %get-tuple-element.21.refs_8_.refs_7_) | copy-start | bytes 49156
  70.1 45.2 %collective-permute-start.5 = (bf16[16,2176]{1,0:T(8,128)(2,1)}, bf16[16,2176]{1,0:T(8,128)(2,1)S(1)}, u32[]{:S(2)}, u32[]{:S(2)}) collective-permute-start(bf16[16,2176]{1,0:T(8,128)(2,1)} %get-tuple-element.22.refs_8_), channel_id=1, source_target_pairs={{0,8},{2,10},{4,12},{6,14},{8,0},{10,2},{12,4},{14,6},{1,9},{3,11}... | collective-permute-start | bytes 208904 | tf_op jit(solution)/shard_map/ppermute | solution.py:374
  70.1 0.7 copy-start.5
  111.3 6.4 %collective-permute-start.10 = (bf16[16,2176]{1,0:T(8,128)(2,1)}, bf16[16,2176]{1,0:T(8,128)(2,1)S(1)}, u32[]{:S(2)}, u32[]{:S(2)}) collective-permute-start(bf16[16,2176]{1,0:T(8,128)(2,1)} %get-tuple-element.28), channel_id=1, source_target_pairs={{0,12},{2,14},{4,8},{6,10},{8,4},{10,6},{12,0},{14,2},{1,13},{3,15... | collective-permute-start | bytes 208904 | tf_op jit(solution)/shard_map/ppermute | solution.py:374
  113.8 6.6 %collective-permute-start.11 = (bf16[16,2176]{1,0:T(8,128)(2,1)}, bf16[16,2176]{1,0:T(8,128)(2,1)S(1)}, u32[]{:S(2)}, u32[]{:S(2)}) collective-permute-start(bf16[16,2176]{1,0:T(8,128)(2,1)} %get-tuple-element.30), channel_id=1, source_target_pairs={{0,14},{2,12},{4,10},{6,8},{8,6},{10,4},{12,2},{14,0},{1,15},{3,13... | collective-permute-start | bytes 208904 | tf_op jit(solution)/shard_map/ppermute | solution.py:374
  114.6 5.7 %collective-permute-start.12 = (bf16[16,2176]{1,0:T(8,128)(2,1)}, bf16[16,2176]{1,0:T(8,128)(2,1)S(1)}, u32[]{:S(2)}, u32[]{:S(2)}) collective-permute-start(bf16[16,2176]{1,0:T(8,128)(2,1)} %get-tuple-element.31), channel_id=1, source_target_pairs={{0,2},{2,0},{4,6},{6,4},{8,10},{10,8},{12,14},{14,12},{1,3},{3,1},... | collective-permute-start | bytes 208904 | tf_op jit(solution)/shard_map/ppermute | solution.py:374
  115.3 0.9 copy-start.1

commit v8 on v7

--- a/solution.py
+++ b/solution.py
@@ -16,7 +16,7 @@
 LOW, HIGH = 2.0**-80, 2.0**100
 VMEM = 121 * 1024 * 1024 // 2
 SMALL = 16 * 1024 * 1024
-ROWS_STEP = 512
+ROWS_STEP = 1024
 
 
 def split3(x):
@@ -296,70 +296,51 @@
     return [factor * inverse for factor in factors], top + jnp.log(total)
 
 
-def merge_kernel(sides, *refs):
-    out_refs = refs[-len(sides) :]
-    items, columns = out_refs[0].shape
-    columns -= LANES
-    heads = columns // HD
-    pad = jnp.zeros((items, LANES - heads), jnp.float32)
-    taken = 0
-    for count, out_ref in zip(sides, out_refs):
-        back_refs = refs[taken : taken + count]
-        taken += count
-        parts = [(ref, start) for ref in back_refs for start in range(0, ref.shape[0], items)]
-        factors, log = shares(weigh(parts, items, heads))
-        for h in range(heads):
-            span = slice(h * HD, (h + 1) * HD)
-            acc = jnp.zeros((items, HD), jnp.float32)
-            for factor, (ref, start) in zip(factors, parts):
-                acc += factor[:, h : h + 1] * ref[start : start + items, span].astype(jnp.float32)
-            out_ref[:, span] = acc
-        out_ref[:, columns:] = jnp.concatenate([log, pad], axis=1)
-
-
-def merge(sides, items, after):
-    arrays = [x for side in sides for x in side]
-    shape = jax.ShapeDtypeStruct((items, arrays[0].shape[1]), jnp.float32)
-    return pl.pallas_call(
-        functools.partial(merge_kernel, [len(side) for side in sides]),
-        in_specs=[pl.BlockSpec(memory_space=pltpu.VMEM)] * len(arrays) + [ANY] * len(after),
-        out_shape=[shape, shape],
-        compiler_params=params(SMALL),
-        cost_estimate=pl.CostEstimate(
-            flops=1 << 30, bytes_accessed=8 * shape.size, transcendentals=items
-        ),
-    )(*arrays, *after)
-
-
-def finish_kernel(late, *refs):
+def finish_kernel(sides, *refs):
     out_s_ref, log_s_ref, out_ref = refs[-3:]
     rows, steps, width = out_ref.shape
     items = rows * steps
     columns = width // 2
     heads = columns // HD
     core = lax.axis_index("ctx") % 2
-    for side, which in ((0, core), (1, 1 - core)):
-        merged_ref, *late_refs = refs[side * (late + 1) : (side + 1) * (late + 1)]
-        parts = [(ref, 0) for ref in late_refs]
-        logs = [log_s_ref[which][:, :heads], merged_ref[:, columns : columns + heads]]
-        factors, _ = shares(logs + weigh(parts, items, heads))
+    taken = 0
+    for count, which in zip(sides, (core, 1 - core)):
+        back_refs = refs[taken : taken + count]
+        taken += count
+        parts = [(ref, start) for ref in back_refs for start in range(0, ref.shape[0], items)]
+        factors, _ = shares([log_s_ref[which][:, :heads]] + weigh(parts, items, heads))
         for h in range(heads):
             here = slice(h * HD, (h + 1) * HD)
             span = pl.ds(pl.multiple_of(which * columns + h * HD, HD), HD)
             acc = factors[0][:, h : h + 1] * out_s_ref[:, span]
-            acc += factors[1][:, h : h + 1] * merged_ref[:, here]
-            for factor, (ref, _) in zip(factors[2:], parts):
-                acc += factor[:, h : h + 1] * ref[:, here].astype(jnp.float32)
+            for factor, (ref, start) in zip(factors[1:], parts):
+                acc += factor[:, h : h + 1] * ref[start : start + items, here].astype(jnp.float32)
             for row in range(rows):
                 out_ref[row, :, span] = acc[row * steps : (row + 1) * steps].astype(jnp.bfloat16)
 
 
-def finish(own, other, out_s, log_s, shape):
+def finish(sides, out_s, log_s, shape):
     return pl.pallas_call(
-        functools.partial(finish_kernel, len(own) - 1),
+        functools.partial(finish_kernel, [len(side) for side in sides]),
         out_shape=jax.ShapeDtypeStruct(shape, jnp.bfloat16),
         compiler_params=params(SMALL),
-    )(*own, *other, out_s, log_s)
+    )(*sides[0], *sides[1], out_s, log_s)
+
+
+def join_kernel(a_ref, b_ref, after_ref, out_ref):
+    rows = a_ref.shape[0]
+    out_ref[:rows] = a_ref[...]
+    out_ref[rows:] = b_ref[...]
+
+
+def join(a, b, after):
+    whole = pl.BlockSpec(memory_space=pltpu.VMEM)
+    return pl.pallas_call(
+        join_kernel,
+        in_specs=[whole, whole, ANY],
+        out_shape=jax.ShapeDtypeStruct((2 * a.shape[0], a.shape[1]), a.dtype),
+        compiler_params=params(),
+    )(a, b, after)
 
 
 def local(queries, selected, placement, lengths, cache_k, cache_v, suffix_k, suffix_v):
@@ -378,29 +359,24 @@
     place = placement.reshape(1, -1)
     caches = [cache_k, cache_v, swap(cache_k, 1), swap(cache_v, 1)]
     packed = pack(queries, selected)
-    chip = jnp.concatenate([packed[0], swap(packed[1], 1)], axis=0)
     out_s, log_s = attend_suffix(lengths, queries, suffix_k, suffix_v)
+    chip = join(packed[0], swap(packed[1], 1), log_s)
     attend = functools.partial(attend_blocks, where, place, caches, group_size)
     if chips == 4:
         far, near = swap(chip, 4), swap(chip, 2)
         farthest = swap(far, 2)
-        first = attend([far, near], 4, [log_s])
-        sides = [[swap(first[n], 4 + n), swap(first[2 + n], 2 + n)] for n in range(2)]
-        last = attend([farthest, chip], 4, [first[0]])
-        late = [[swap(last[n], 6 + n), swap(last[2 + n], n)] for n in range(2)]
-        after = [last[2]]
+        partial = attend([chip, near, far, farthest], size, [])
+        back = {n: swap(partial[n], n) for n in (3, 4, 5, 6, 7, 2, 1, 0)}
+        sides = [[back[n] for n in range(side, size, 2)] for side in range(2)]
     else:
         same = [[2 * z + core for z in range(chips)] for core in range(2)]
         every = lax.all_gather(chip, "ctx", axis=0, tiled=True, axis_index_groups=same)
-        (partial,) = attend([every], 1, [log_s])
+        (partial,) = attend([every], 1, [])
         back = lax.all_to_all(
             partial, "ctx", split_axis=0, concat_axis=0, tiled=True, axis_index_groups=same
         ).reshape(chips, 2, items, -1)
         sides = [[swap(back[:, n].reshape(chips * items, -1), n)] for n in range(2)]
-        late, after = [[], []], []
-    merged = merge(sides, items, after)
-    own, other = ([x] + y for x, y in zip(merged, late))
-    return finish(own, other, out_s, log_s, queries.shape)
+    return finish(sides, out_s, log_s, queries.shape)
 
 
 def solution(mesh):

time: 122 us -> 102 us (0.84)
  Pallas kernels: 88.1 us -> 65.3 us
  waiting for transfers between devices: 13.4 us -> 17.3 us
    pallas_call x2 -> x1, Pallas kernels: 81 us -> 57 us  [attend_blocks(): pl.pallas_call(functools.partial(block_kernel, pieces, outs, group_size,...]
    ppermute x13, waiting for transfers between devices: 13.4 us -> 17.3 us  [swap(): lax.ppermute(x, 'ctx', [(i, i ^ bits) for i in range(size)])]
    pallas_call x2, Pallas kernels: 1.71 us -> 2.99 us  [the longest x1 1.59 us: join(): pl.pallas_call(join_kernel, in_specs=[whole, whole, ANY], out_shape=jax.S...]
    unnamed x15 -> x14, local copies, waits for them, and re-layouts: 3.08 us -> 2.15 us
  transfers between devices with their start and end apart: 13 -> 13, of which waited for: 4 -> 7; matrix products, arithmetic and copies ran while one was open for 1% -> 1% of each run, Pallas kernels for 71% -> 7%
where the time goes in v8:
time: 102 us; the launch traced here: 101 us
  Pallas kernels  65.3 us (64%)
  waiting for transfers between devices  17.3 us (17%)
  starting transfers between devices  15.9 us (16%)
  local copies, waits for them, and re-layouts  2.15 us (2%)
    pallas_call x1, Pallas kernels, attend_blocks(): pl.pallas_call(functools.partial(block_kernel, pieces, outs, group_size,...  57 us
    ppermute x13, waiting for transfers between devices, swap(): lax.ppermute(x, 'ctx', [(i, i ^ bits) for i in range(size)])  17.3 us
    ppermute x13, starting transfers between devices, swap(): lax.ppermute(x, 'ctx', [(i, i ^ bits) for i in range(size)])  15.9 us
    pallas_call x1, Pallas kernels, attend_suffix(): pl.pallas_call(functools.partial(suffix_kernel, width // kv_width), grid_...  3.81 us
    unnamed x14, local copies, waits for them, and re-layouts  2.15 us
  transfers between devices with their start and end apart: 13, of which 7 were waited for; matrix products, arithmetic and copies ran while one was open for 1% of the time, Pallas kernels for 7%

profile of v8, /device:TPU:0, one launch (start us, length us, event | category | flops | bytes accessed | tf_op | source)
XLA Modules:
  0.0 101.4 jit_solution(923794479846814353)
XLA Ops:
  0.0 0.5 collective-permute-start.4
  0.5 1.6 %shard_map.82 = (bf16[16,2176]{1,0:T(8,128)(2,1)}, bf16[16,2176]{1,0:T(8,128)(2,1)}) custom-call(bf16[4,4,4096]{2,1,0:T(4,128)(2,1)} %q_ref.3, s32[4,4,16]{2,1,0:T(4,128)} %selected_ref.1), custom_call_target="tpu_custom_call" | custom-call | tf_op jit(solution)/shard_map/pallas_call | solution.py:68
  2.1 0.5 collective-permute-start
  2.5 3.8 %shard_map.83 = (f32[16,4096]{1,0:T(8,128)}, f32[2,16,128]{2,1,0:T(8,128)}) custom-call(s32[4]{0:T(128)} %lengths_ref.1, bf16[4,4,4096]{2,1,0:T(4,128)(2,1)} %q_ref.3, bf16[4,128,512]{2,1,0:T(8,128)(2,1)} %k_ref.1, bf16[4,128,512]{2,1,0:T(8,128)(2,1)} %v_ref.1), custom_call_target="tpu_custom_call" | custom-call | flops 536870912 | bytes 1441792 | tf_op jit(solution)/shard_map/pallas_call | solution.py:254
  6.4 1.3 %collective-permute-done.b_ref = bf16[16,2176]{1,0:T(8,128)(2,1)S(1)} collective-permute-done((bf16[16,2176]{1,0:T(8,128)(2,1)}, bf16[16,2176]{1,0:T(8,128)(2,1)S(1)}, u32[]{:S(2)}, u32[]{:S(2)}) %collective-permute-start) | collective-permute-done | bytes 69664 | tf_op jit(solution)/shard_map/ppermute | solution.py:355
  7.7 0.6 copy-done.6
  8.3 1.6 %shard_map.84.refs_0_.refs_4_ = bf16[32,2176]{1,0:T(8,128)(2,1)} custom-call(bf16[16,2176]{1,0:T(8,128)(2,1)} %get-tuple-element.17.a_ref, bf16[16,2176]{1,0:T(8,128)(2,1)} %copy-done.6, f32[2,16,128]{2,1,0:T(8,128)} %get-tuple-element.19.after_ref.refs_9_), custom_call_target="tpu_custom_call" | custom-call | tf_op jit(solution)/shard_map/pallas_call | solution.py:338
  9.9 4.0 %collective-permute-start.2 = (bf16[32,2176]{1,0:T(8,128)(2,1)}, bf16[32,2176]{1,0:T(8,128)(2,1)S(1)}, u32[]{:S(2)}, u32[]{:S(2)}) collective-permute-start(bf16[32,2176]{1,0:T(8,128)(2,1)} %shard_map.84.refs_0_.refs_4_), channel_id=1, source_target_pairs={{0,8},{2,10},{4,12},{6,14},{8,0},{10,2},{12,4},{14,6},{1,9},{3,11}... | collective-permute-start | bytes 417800 | tf_op jit(solution)/shard_map/ppermute | solution.py:355
  13.8 1.6 %collective-permute-start.1 = (bf16[32,2176]{1,0:T(8,128)(2,1)}, bf16[32,2176]{1,0:T(8,128)(2,1)S(1)}, u32[]{:S(2)}, u32[]{:S(2)}) collective-permute-start(bf16[32,2176]{1,0:T(8,128)(2,1)} %shard_map.84.refs_0_.refs_4_), channel_id=1, source_target_pairs={{0,4},{2,6},{4,0},{6,2},{8,12},{10,14},{12,8},{14,10},{1,5},{3,7},... | collective-permute-start | bytes 417800 | tf_op jit(solution)/shard_map/ppermute | solution.py:355
  15.4 5.7 %collective-permute-done.2.refs_2_.refs_6_ = bf16[32,2176]{1,0:T(8,128)(2,1)S(1)} collective-permute-done((bf16[32,2176]{1,0:T(8,128)(2,1)}, bf16[32,2176]{1,0:T(8,128)(2,1)S(1)}, u32[]{:S(2)}, u32[]{:S(2)}) %collective-permute-start.2) | collective-permute-done | bytes 139296 | tf_op jit(solution)/shard_map/ppermute | solution.py:355
  21.1 0.7 collective-permute-start.3
  21.8 0.7 pad_add_fusion.where_ref
  22.5 3.7 %collective-permute-done.3.refs_3_.refs_7_ = bf16[32,2176]{1,0:T(8,128)(2,1)S(1)} collective-permute-done((bf16[32,2176]{1,0:T(8,128)(2,1)S(1)}, bf16[32,2176]{1,0:T(8,128)(2,1)S(1)}, u32[]{:S(2)}, u32[]{:S(2)}) %collective-permute-start.3) | collective-permute-done | bytes 139296 | tf_op jit(solution)/shard_map/ppermute | solution.py:355
  26.2 0.6 copy-done.5
  26.9 57.0 %shard_map.85 = (bf16[16,2176]{1,0:T(8,128)(2,1)}, bf16[16,2176]{1,0:T(8,128)(2,1)}, bf16[16,2176]{1,0:T(8,128)(2,1)}, bf16[16,2176]{1,0:T(8,128)(2,1)}, bf16[16...) custom-call(s32[3]{0:T(128)} %pad_add_fusion.where_ref, ...), custom_call_target="tpu_custom_call" | custom-call | flops 285212672 | bytes 1114112 | tf_op jit(solution)/shard_map/pallas_call | solution.py:184
  83.8 1.3 %collective-permute-start.6 = (bf16[16,2176]{1,0:T(8,128)(2,1)}, bf16[16,2176]{1,0:T(8,128)(2,1)S(1)}, u32[]{:S(2)}, u32[]{:S(2)}) collective-permute-start(bf16[16,2176]{1,0:T(8,128)(2,1)} %get-tuple-element.21), channel_id=1, source_target_pairs={{0,4},{2,6},{4,0},{6,2},{8,12},{10,14},{12,8},{14,10},{1,5},{3,7},... | collective-permute-start | bytes 208904 | tf_op jit(solution)/shard_map/ppermute | solution.py:355
  85.1 3.3 %collective-permute-start.7 = (bf16[16,2176]{1,0:T(8,128)(2,1)}, bf16[16,2176]{1,0:T(8,128)(2,1)S(1)}, u32[]{:S(2)}, u32[]{:S(2)}) collective-permute-start(bf16[16,2176]{1,0:T(8,128)(2,1)} %get-tuple-element.22), channel_id=1, source_target_pairs={{0,8},{2,10},{4,12},{6,14},{8,0},{10,2},{12,4},{14,6},{1,9},{3,11}... | collective-permute-start | bytes 208904 | tf_op jit(solution)/shard_map/ppermute | solution.py:355
  88.4 0.7 collective-permute-start.10
  89.1 3.4 %collective-permute-start.11 = (bf16[16,2176]{1,0:T(8,128)(2,1)}, bf16[16,2176]{1,0:T(8,128)(2,1)S(1)}, u32[]{:S(2)}, u32[]{:S(2)}) collective-permute-start(bf16[16,2176]{1,0:T(8,128)(2,1)} %get-tuple-element.26), channel_id=1, source_target_pairs={{0,10},{2,8},{4,14},{6,12},{8,2},{10,0},{12,6},{14,4},{1,11},{3,9}... | collective-permute-start | bytes 208904 | tf_op jit(solution)/shard_map/ppermute | solution.py:355
  92.9 2.6 %collective-permute-done.8.refs_3_ = bf16[16,2176]{1,0:T(8,128)(2,1)S(1)} collective-permute-done((bf16[16,2176]{1,0:T(8,128)(2,1)}, bf16[16,2176]{1,0:T(8,128)(2,1)S(1)}, u32[]{:S(2)}, u32[]{:S(2)}) %collective-permute-start.8) | collective-permute-done | bytes 69664 | tf_op jit(solution)/shard_map/ppermute | solution.py:355
  95.5 1.1 %collective-permute-done.11.refs_6_ = bf16[16,2176]{1,0:T(8,128)(2,1)S(1)} collective-permute-done((bf16[16,2176]{1,0:T(8,128)(2,1)}, bf16[16,2176]{1,0:T(8,128)(2,1)S(1)}, u32[]{:S(2)}, u32[]{:S(2)}) %collective-permute-start.11) | collective-permute-done | bytes 69664 | tf_op jit(solution)/shard_map/ppermute | solution.py:355
  96.7 2.4 %collective-permute-done.12.refs_7_ = bf16[16,2176]{1,0:T(8,128)(2,1)S(1)} collective-permute-done((bf16[16,2176]{1,0:T(8,128)(2,1)}, bf16[16,2176]{1,0:T(8,128)(2,1)S(1)}, u32[]{:S(2)}, u32[]{:S(2)}) %collective-permute-start.12) | collective-permute-done | bytes 69664 | tf_op jit(solution)/shard_map/ppermute | solution.py:355
  99.1 0.9 copy-done.1
  100.0 1.4 %shard_map.86 = bf16[4,4,4096]{2,1,0:T(4,128)(2,1)} custom-call(bf16[16,2176]{1,0:T(8,128)(2,1)S(1)} %copy-done.1, bf16[16,2176]{1,0:T(8,128)(2,1)S(1)} %collective-permute-done.6.refs_1_, bf16[16,2176]{1,0:T(8,128)(2,1)S(1)} %collective-permute-done.7.refs_2_, bf16[16,2176]{1,0:T(8,128)(2,1)S(1)} %collective-permute-done.8.refs_3_, ...), custom_call_target="tpu_custom_call" | custom-call | tf_op jit(solution)/shard_map/pallas_call | solution.py:323
  (22 shorter events, 0.5 us)
Async XLA Ops:
  0.0 26.2 %collective-permute-start.4 = (bf16[4,1024,512]{2,1,0:T(8,128)(2,1)}, bf16[4,1024,512]{2,1,0:T(8,128)(2,1)}, u32[]{:S(2)}, u32[]{:S(2)}) collective-permute-start(bf16[4,1024,512]{2,1,0:T(8,128)(2,1)} %refs_8_.1), channel_id=1, source_target_pairs={{0,2},{2,0},{4,6},{6,4},{8,10},{10,8},{12,14},{14,12},{1,3},{3,1},... | collective-permute-start | bytes 12582920 | tf_op jit(solution)/shard_map/ppermute | solution.py:355
  0.5 25.7 %collective-permute-start.5 = (bf16[4,1024,512]{2,1,0:T(8,128)(2,1)}, bf16[4,1024,512]{2,1,0:T(8,128)(2,1)}, u32[]{:S(2)}, u32[]{:S(2)}) collective-permute-start(bf16[4,1024,512]{2,1,0:T(8,128)(2,1)} %refs_9_.1), channel_id=1, source_target_pairs={{0,2},{2,0},{4,6},{6,4},{8,10},{10,8},{12,14},{14,12},{1,3},{3,1},... | collective-permute-start | bytes 12582920 | tf_op jit(solution)/shard_map/ppermute | solution.py:355
  2.1 5.6 %collective-permute-start = (bf16[16,2176]{1,0:T(8,128)(2,1)}, bf16[16,2176]{1,0:T(8,128)(2,1)S(1)}, u32[]{:S(2)}, u32[]{:S(2)}) collective-permute-start(bf16[16,2176]{1,0:T(8,128)(2,1)} %get-tuple-element.18), channel_id=1, source_target_pairs={{0,2},{2,0},{4,6},{6,4},{8,10},{10,8},{12,14},{14,12},{1,3},{3,1},... | collective-permute-start | bytes 208904 | tf_op jit(solution)/shard_map/ppermute | solution.py:355
  7.6 0.6 copy-start.6
  9.9 11.2 %collective-permute-start.2 = (bf16[32,2176]{1,0:T(8,128)(2,1)}, bf16[32,2176]{1,0:T(8,128)(2,1)S(1)}, u32[]{:S(2)}, u32[]{:S(2)}) collective-permute-start(bf16[32,2176]{1,0:T(8,128)(2,1)} %shard_map.84.refs_0_.refs_4_), channel_id=1, source_target_pairs={{0,8},{2,10},{4,12},{6,14},{8,0},{10,2},{12,4},{14,6},{1,9},{3,11}... | collective-permute-start | bytes 417800 | tf_op jit(solution)/shard_map/ppermute | solution.py:355
  13.8 8.7 %collective-permute-start.1 = (bf16[32,2176]{1,0:T(8,128)(2,1)}, bf16[32,2176]{1,0:T(8,128)(2,1)S(1)}, u32[]{:S(2)}, u32[]{:S(2)}) collective-permute-start(bf16[32,2176]{1,0:T(8,128)(2,1)} %shard_map.84.refs_0_.refs_4_), channel_id=1, source_target_pairs={{0,4},{2,6},{4,0},{6,2},{8,12},{10,14},{12,8},{14,10},{1,5},{3,7},... | collective-permute-start | bytes 417800 | tf_op jit(solution)/shard_map/ppermute | solution.py:355
  21.1 5.1 %copy-start.3 = (bf16[32,2176]{1,0:T(8,128)(2,1)}, bf16[32,2176]{1,0:T(8,128)(2,1)S(1)}, u32[]{:S(2)}) copy-start(bf16[32,2176]{1,0:T(8,128)(2,1)S(1)} %collective-permute-done.2.refs_2_.refs_6_) | copy-start | bytes 417796
  21.1 5.1 %collective-permute-start.3 = (bf16[32,2176]{1,0:T(8,128)(2,1)S(1)}, bf16[32,2176]{1,0:T(8,128)(2,1)S(1)}, u32[]{:S(2)}, u32[]{:S(2)}) collective-permute-start(bf16[32,2176]{1,0:T(8,128)(2,1)S(1)} %collective-permute-done.2.refs_2_.refs_6_), channel_id=1, source_target_pairs={{0,4},{2,6},{4,0},{6,2},{8,12},{10,14},{12,8},{14,10},{1,5},{3,7},... | collective-permute-start | bytes 417800 | tf_op jit(solution)/shard_map/ppermute | solution.py:355
  22.5 3.7 %copy-start.4 = (bf16[32,2176]{1,0:T(8,128)(2,1)}, bf16[32,2176]{1,0:T(8,128)(2,1)S(1)}, u32[]{:S(2)}) copy-start(bf16[32,2176]{1,0:T(8,128)(2,1)S(1)} %collective-permute-done.1.refs_1_.refs_5_) | copy-start | bytes 417796
  26.2 0.7 copy-start.5
  26.8 72.3 %copy-start = (f32[16,4096]{1,0:T(8,128)S(1)}, f32[16,4096]{1,0:T(8,128)}, u32[]{:S(2)}) copy-start(f32[16,4096]{1,0:T(8,128)} %get-tuple-element.28.refs_8_) | copy-start | bytes 786436
  26.9 72.3 %copy-start.2 = (f32[2,16,128]{2,1,0:T(8,128)S(1)}, f32[2,16,128]{2,1,0:T(8,128)}, u32[]{:S(2)}) copy-start(f32[2,16,128]{2,1,0:T(8,128)} %get-tuple-element.19.after_ref.refs_9_) | copy-start | bytes 49156
  83.8 5.3 %collective-permute-start.6 = (bf16[16,2176]{1,0:T(8,128)(2,1)}, bf16[16,2176]{1,0:T(8,128)(2,1)S(1)}, u32[]{:S(2)}, u32[]{:S(2)}) collective-permute-start(bf16[16,2176]{1,0:T(8,128)(2,1)} %get-tuple-element.21), channel_id=1, source_target_pairs={{0,4},{2,6},{4,0},{6,2},{8,12},{10,14},{12,8},{14,10},{1,5},{3,7},... | collective-permute-start | bytes 208904 | tf_op jit(solution)/shard_map/ppermute | solution.py:355
  85.1 7.8 %collective-permute-start.7 = (bf16[16,2176]{1,0:T(8,128)(2,1)}, bf16[16,2176]{1,0:T(8,128)(2,1)S(1)}, u32[]{:S(2)}, u32[]{:S(2)}) collective-permute-start(bf16[16,2176]{1,0:T(8,128)(2,1)} %get-tuple-element.22), channel_id=1, source_target_pairs={{0,8},{2,10},{4,12},{6,14},{8,0},{10,2},{12,4},{14,6},{1,9},{3,11}... | collective-permute-start | bytes 208904 | tf_op jit(solution)/shard_map/ppermute | solution.py:355
  88.4 7.1 %collective-permute-start.8 = (bf16[16,2176]{1,0:T(8,128)(2,1)}, bf16[16,2176]{1,0:T(8,128)(2,1)S(1)}, u32[]{:S(2)}, u32[]{:S(2)}) collective-permute-start(bf16[16,2176]{1,0:T(8,128)(2,1)} %get-tuple-element.23), channel_id=1, source_target_pairs={{0,12},{2,14},{4,8},{6,10},{8,4},{10,6},{12,0},{14,2},{1,13},{3,15... | collective-permute-start | bytes 208904 | tf_op jit(solution)/shard_map/ppermute | solution.py:355
  88.4 7.1 %collective-permute-start.9 = (bf16[16,2176]{1,0:T(8,128)(2,1)}, bf16[16,2176]{1,0:T(8,128)(2,1)S(1)}, u32[]{:S(2)}, u32[]{:S(2)}) collective-permute-start(bf16[16,2176]{1,0:T(8,128)(2,1)} %get-tuple-element.24), channel_id=1, source_target_pairs={{0,2},{2,0},{4,6},{6,4},{8,10},{10,8},{12,14},{14,12},{1,3},{3,1},... | collective-permute-start | bytes 208904 | tf_op jit(solution)/shard_map/ppermute | solution.py:355
  88.4 7.1 %collective-permute-start.10 = (bf16[16,2176]{1,0:T(8,128)(2,1)}, bf16[16,2176]{1,0:T(8,128)(2,1)S(1)}, u32[]{:S(2)}, u32[]{:S(2)}) collective-permute-start(bf16[16,2176]{1,0:T(8,128)(2,1)} %get-tuple-element.25), channel_id=1, source_target_pairs={{0,6},{2,4},{4,2},{6,0},{8,14},{10,12},{12,10},{14,8},{1,7},{3,5},... | collective-permute-start | bytes 208904 | tf_op jit(solution)/shard_map/ppermute | solution.py:355
  89.1 7.6 %collective-permute-start.11 = (bf16[16,2176]{1,0:T(8,128)(2,1)}, bf16[16,2176]{1,0:T(8,128)(2,1)S(1)}, u32[]{:S(2)}, u32[]{:S(2)}) collective-permute-start(bf16[16,2176]{1,0:T(8,128)(2,1)} %get-tuple-element.26), channel_id=1, source_target_pairs={{0,10},{2,8},{4,14},{6,12},{8,2},{10,0},{12,6},{14,4},{1,11},{3,9}... | collective-permute-start | bytes 208904 | tf_op jit(solution)/shard_map/ppermute | solution.py:355
  92.9 6.2 %collective-permute-start.12 = (bf16[16,2176]{1,0:T(8,128)(2,1)}, bf16[16,2176]{1,0:T(8,128)(2,1)S(1)}, u32[]{:S(2)}, u32[]{:S(2)}) collective-permute-start(bf16[16,2176]{1,0:T(8,128)(2,1)} %get-tuple-element.27), channel_id=1, source_target_pairs={{0,14},{2,12},{4,10},{6,8},{8,6},{10,4},{12,2},{14,0},{1,15},{3,13... | collective-permute-start | bytes 208904 | tf_op jit(solution)/shard_map/ppermute | solution.py:355
  99.1 0.9 copy-start.1

commit v9 on v8

--- a/solution.py
+++ b/solution.py
@@ -327,22 +327,6 @@
     )(*sides[0], *sides[1], out_s, log_s)
 
 
-def join_kernel(a_ref, b_ref, after_ref, out_ref):
-    rows = a_ref.shape[0]
-    out_ref[:rows] = a_ref[...]
-    out_ref[rows:] = b_ref[...]
-
-
-def join(a, b, after):
-    whole = pl.BlockSpec(memory_space=pltpu.VMEM)
-    return pl.pallas_call(
-        join_kernel,
-        in_specs=[whole, whole, ANY],
-        out_shape=jax.ShapeDtypeStruct((2 * a.shape[0], a.shape[1]), a.dtype),
-        compiler_params=params(),
-    )(a, b, after)
-
-
 def local(queries, selected, placement, lengths, cache_k, cache_v, suffix_k, suffix_v):
     rows_here, steps, width = queries.shape
     size = lax.axis_size("ctx")
@@ -360,18 +344,18 @@
     caches = [cache_k, cache_v, swap(cache_k, 1), swap(cache_v, 1)]
     packed = pack(queries, selected)
     out_s, log_s = attend_suffix(lengths, queries, suffix_k, suffix_v)
-    chip = join(packed[0], swap(packed[1], 1), log_s)
     attend = functools.partial(attend_blocks, where, place, caches, group_size)
     if chips == 4:
-        far, near = swap(chip, 4), swap(chip, 2)
-        farthest = swap(far, 2)
-        partial = attend([chip, near, far, farthest], size, [])
+        arrived = {n: swap(packed[n % 2], n) for n in (4, 5, 2, 3, 0, 1)}
+        arrived.update({n: swap(arrived[n - 2], 2) for n in (6, 7)})
+        partial = attend([arrived[n] for n in range(size)], size, [log_s])
         back = {n: swap(partial[n], n) for n in (3, 4, 5, 6, 7, 2, 1, 0)}
         sides = [[back[n] for n in range(side, size, 2)] for side in range(2)]
     else:
         same = [[2 * z + core for z in range(chips)] for core in range(2)]
+        chip = jnp.concatenate([packed[0], swap(packed[1], 1)], axis=0)
         every = lax.all_gather(chip, "ctx", axis=0, tiled=True, axis_index_groups=same)
-        (partial,) = attend([every], 1, [])
+        (partial,) = attend([every], 1, [log_s])
         back = lax.all_to_all(
             partial, "ctx", split_axis=0, concat_axis=0, tiled=True, axis_index_groups=same
         ).reshape(chips, 2, items, -1)

time: 102 us -> 96.8 us (0.949)
  waiting for transfers between devices: 17.3 us -> 13.7 us
  Pallas kernels: 65.3 us -> 63.8 us
    ppermute x13 -> x16, waiting for transfers between devices: 17.3 us -> 13.7 us  [swap(): lax.ppermute(x, 'ctx', [(i, i ^ bits) for i in range(size)])]
    pallas_call x1 -> x0, Pallas kernels: 1.59 us -> none  [join(): pl.pallas_call(join_kernel, in_specs=[whole, whole, ANY], out_shape=jax.S...]
    ppermute x13 -> x16, starting transfers between devices: 15.9 us -> 16.8 us  [swap(): lax.ppermute(x, 'ctx', [(i, i ^ bits) for i in range(size)])]
    unnamed x14 -> x20, local copies, waits for them, and re-layouts: 2.15 us -> 1.49 us
  transfers between devices with their start and end apart: 13 -> 16, of which waited for: 7 -> 8; matrix products, arithmetic and copies ran while one was open for 1% -> 1% of each run, Pallas kernels for 7% -> 6%
where the time goes in v9:
time: 96.8 us; the launch traced here: 96.5 us
  Pallas kernels  63.8 us (66%)
  starting transfers between devices  16.8 us (17%)
  waiting for transfers between devices  13.7 us (14%)
  local copies, waits for them, and re-layouts  1.49 us (2%)
    pallas_call x1, Pallas kernels, attend_blocks(): pl.pallas_call(functools.partial(block_kernel, pieces, outs, group_size,...  57 us
    ppermute x16, starting transfers between devices, swap(): lax.ppermute(x, 'ctx', [(i, i ^ bits) for i in range(size)])  16.8 us
    ppermute x16, waiting for transfers between devices, swap(): lax.ppermute(x, 'ctx', [(i, i ^ bits) for i in range(size)])  13.7 us
    pallas_call x1, Pallas kernels, attend_suffix(): pl.pallas_call(functools.partial(suffix_kernel, width // kv_width), grid_...  3.83 us
  transfers between devices with their start and end apart: 16, of which 8 were waited for; matrix products, arithmetic and copies ran while one was open for 1% of the time, Pallas kernels for 6%

profile of v9, /device:TPU:0, one launch (start us, length us, event | category | flops | bytes accessed | tf_op | source)
XLA Modules:
  0.0 96.5 jit_solution(100391399843595705)
XLA Ops:
  0.5 1.6 %shard_map.82 = (bf16[16,2176]{1,0:T(8,128)(2,1)}, bf16[16,2176]{1,0:T(8,128)(2,1)}) custom-call(bf16[4,4,4096]{2,1,0:T(4,128)(2,1)} %q_ref.3, s32[4,4,16]{2,1,0:T(4,128)} %selected_ref.1), custom_call_target="tpu_custom_call" | custom-call | tf_op jit(solution)/shard_map/pallas_call | solution.py:68
  2.1 4.0 %collective-permute-start.3 = (bf16[16,2176]{1,0:T(8,128)(2,1)}, bf16[16,2176]{1,0:T(8,128)(2,1)S(1)}, u32[]{:S(2)}, u32[]{:S(2)}) collective-permute-start(bf16[16,2176]{1,0:T(8,128)(2,1)} %get-tuple-element.17.refs_0_.refs_8_), channel_id=1, source_target_pairs={{0,8},{2,10},{4,12},{6,14},{8,0},{10,2},{12,4},{14,6},{1,9},{3,11}... | collective-permute-start | bytes 208904 | tf_op jit(solution)/shard_map/ppermute | solution.py:339
  6.1 1.6 %collective-permute-start.1 = (bf16[16,2176]{1,0:T(8,128)(2,1)}, bf16[16,2176]{1,0:T(8,128)(2,1)S(1)}, u32[]{:S(2)}, u32[]{:S(2)}) collective-permute-start(bf16[16,2176]{1,0:T(8,128)(2,1)} %get-tuple-element.17.refs_0_.refs_8_), channel_id=1, source_target_pairs={{0,4},{2,6},{4,0},{6,2},{8,12},{10,14},{12,8},{14,10},{1,5},{3,7},... | collective-permute-start | bytes 208904 | tf_op jit(solution)/shard_map/ppermute | solution.py:339
  7.7 1.9 %collective-permute-done.3.refs_4_.refs_12_ = bf16[16,2176]{1,0:T(8,128)(2,1)S(1)} collective-permute-done((bf16[16,2176]{1,0:T(8,128)(2,1)}, bf16[16,2176]{1,0:T(8,128)(2,1)S(1)}, u32[]{:S(2)}, u32[]{:S(2)}) %collective-permute-start.3) | collective-permute-done | bytes 69664 | tf_op jit(solution)/shard_map/ppermute | solution.py:339
  9.6 0.7 collective-permute-start.2
  10.6 1.1 %collective-permute-start = (bf16[16,2176]{1,0:T(8,128)(2,1)}, bf16[16,2176]{1,0:T(8,128)(2,1)S(1)}, u32[]{:S(2)}, u32[]{:S(2)}) collective-permute-start(bf16[16,2176]{1,0:T(8,128)(2,1)} %get-tuple-element.18), channel_id=1, source_target_pairs={{0,2},{2,0},{4,6},{6,4},{8,10},{10,8},{12,14},{14,12},{1,3},{3,1},... | collective-permute-start | bytes 208904 | tf_op jit(solution)/shard_map/ppermute | solution.py:339
  11.7 2.7 %collective-permute-done.4.refs_5_.refs_13_ = bf16[16,2176]{1,0:T(8,128)(2,1)S(1)} collective-permute-done((bf16[16,2176]{1,0:T(8,128)(2,1)}, bf16[16,2176]{1,0:T(8,128)(2,1)S(1)}, u32[]{:S(2)}, u32[]{:S(2)}) %collective-permute-start.4) | collective-permute-done | bytes 69664 | tf_op jit(solution)/shard_map/ppermute | solution.py:339
  14.4 1.2 %collective-permute-done.2.refs_3_.refs_11_ = bf16[16,2176]{1,0:T(8,128)(2,1)S(1)} collective-permute-done((bf16[16,2176]{1,0:T(8,128)(2,1)}, bf16[16,2176]{1,0:T(8,128)(2,1)S(1)}, u32[]{:S(2)}, u32[]{:S(2)}) %collective-permute-start.2) | collective-permute-done | bytes 69664 | tf_op jit(solution)/shard_map/ppermute | solution.py:339
  15.6 0.9 collective-permute-start.6
  16.4 0.6 pad_add_fusion.where_ref
  17.0 3.8 %shard_map.83 = (f32[16,4096]{1,0:T(8,128)}, f32[2,16,128]{2,1,0:T(8,128)}) custom-call(s32[4]{0:T(128)} %lengths_ref.1, bf16[4,4,4096]{2,1,0:T(4,128)(2,1)} %q_ref.3, bf16[4,128,512]{2,1,0:T(8,128)(2,1)} %k_ref.1, bf16[4,128,512]{2,1,0:T(8,128)(2,1)} %v_ref.1), custom_call_target="tpu_custom_call" | custom-call | flops 536870912 | bytes 1441792 | tf_op jit(solution)/shard_map/pallas_call | solution.py:254
  20.9 0.5 copy-done.7
  21.5 57.0 %shard_map.84 = (bf16[16,2176]{1,0:T(8,128)(2,1)}, bf16[16,2176]{1,0:T(8,128)(2,1)}, bf16[16,2176]{1,0:T(8,128)(2,1)}, bf16[16,2176]{1,0:T(8,128)(2,1)}, bf16[16...) custom-call(s32[3]{0:T(128)} %pad_add_fusion.where_ref, ...), custom_call_target="tpu_custom_call" | custom-call | flops 285212672 | bytes 1114112 | tf_op jit(solution)/shard_map/pallas_call | solution.py:184
  78.6 1.2 %collective-permute-start.9 = (bf16[16,2176]{1,0:T(8,128)(2,1)}, bf16[16,2176]{1,0:T(8,128)(2,1)S(1)}, u32[]{:S(2)}, u32[]{:S(2)}) collective-permute-start(bf16[16,2176]{1,0:T(8,128)(2,1)} %get-tuple-element.21), channel_id=1, source_target_pairs={{0,4},{2,6},{4,0},{6,2},{8,12},{10,14},{12,8},{14,10},{1,5},{3,7},... | collective-permute-start | bytes 208904 | tf_op jit(solution)/shard_map/ppermute | solution.py:339
  79.8 1.9 %collective-permute-start.10 = (bf16[16,2176]{1,0:T(8,128)(2,1)}, bf16[16,2176]{1,0:T(8,128)(2,1)S(1)}, u32[]{:S(2)}, u32[]{:S(2)}) collective-permute-start(bf16[16,2176]{1,0:T(8,128)(2,1)} %get-tuple-element.22), channel_id=1, source_target_pairs={{0,8},{2,10},{4,12},{6,14},{8,0},{10,2},{12,4},{14,6},{1,9},{3,11}... | collective-permute-start | bytes 208904 | tf_op jit(solution)/shard_map/ppermute | solution.py:339
  81.7 1.4 %collective-permute-start.11 = (bf16[16,2176]{1,0:T(8,128)(2,1)}, bf16[16,2176]{1,0:T(8,128)(2,1)S(1)}, u32[]{:S(2)}, u32[]{:S(2)}) collective-permute-start(bf16[16,2176]{1,0:T(8,128)(2,1)} %get-tuple-element.23), channel_id=1, source_target_pairs={{0,12},{2,14},{4,8},{6,10},{8,4},{10,6},{12,0},{14,2},{1,13},{3,15... | collective-permute-start | bytes 208904 | tf_op jit(solution)/shard_map/ppermute | solution.py:339
  83.1 0.7 collective-permute-start.13
  83.9 1.9 %collective-permute-start.14 = (bf16[16,2176]{1,0:T(8,128)(2,1)}, bf16[16,2176]{1,0:T(8,128)(2,1)S(1)}, u32[]{:S(2)}, u32[]{:S(2)}) collective-permute-start(bf16[16,2176]{1,0:T(8,128)(2,1)} %get-tuple-element.26), channel_id=1, source_target_pairs={{0,10},{2,8},{4,14},{6,12},{8,2},{10,0},{12,6},{14,4},{1,11},{3,9}... | collective-permute-start | bytes 208904 | tf_op jit(solution)/shard_map/ppermute | solution.py:339
  85.8 2.7 %collective-permute-done.10.refs_2_ = bf16[16,2176]{1,0:T(8,128)(2,1)S(1)} collective-permute-done((bf16[16,2176]{1,0:T(8,128)(2,1)}, bf16[16,2176]{1,0:T(8,128)(2,1)S(1)}, u32[]{:S(2)}, u32[]{:S(2)}) %collective-permute-start.10) | collective-permute-done | bytes 69664 | tf_op jit(solution)/shard_map/ppermute | solution.py:339
  88.5 0.8 collective-permute-start.15
  89.4 2.2 %collective-permute-done.14.refs_6_ = bf16[16,2176]{1,0:T(8,128)(2,1)S(1)} collective-permute-done((bf16[16,2176]{1,0:T(8,128)(2,1)}, bf16[16,2176]{1,0:T(8,128)(2,1)S(1)}, u32[]{:S(2)}, u32[]{:S(2)}) %collective-permute-start.14) | collective-permute-done | bytes 69664 | tf_op jit(solution)/shard_map/ppermute | solution.py:339
  91.5 2.7 %collective-permute-done.15.refs_7_ = bf16[16,2176]{1,0:T(8,128)(2,1)S(1)} collective-permute-done((bf16[16,2176]{1,0:T(8,128)(2,1)}, bf16[16,2176]{1,0:T(8,128)(2,1)S(1)}, u32[]{:S(2)}, u32[]{:S(2)}) %collective-permute-start.15) | collective-permute-done | bytes 69664 | tf_op jit(solution)/shard_map/ppermute | solution.py:339
  94.3 0.9 copy-done.1
  95.1 1.4 %shard_map.85 = bf16[4,4,4096]{2,1,0:T(4,128)(2,1)} custom-call(bf16[16,2176]{1,0:T(8,128)(2,1)S(1)} %copy-done.1, bf16[16,2176]{1,0:T(8,128)(2,1)S(1)} %collective-permute-done.9.refs_1_, bf16[16,2176]{1,0:T(8,128)(2,1)S(1)} %collective-permute-done.10.refs_2_, bf16[16,2176]{1,0:T(8,128)(2,1)S(1)} %collective-permute-done.11.refs_3_, ...), custom_call_target="tpu_custom_call" | custom-call | tf_op jit(solution)/shard_map/pallas_call | solution.py:323
  (33 shorter events, 1.0 us)
Async XLA Ops:
  0.0 20.9 %collective-permute-start.7 = (bf16[4,1024,512]{2,1,0:T(8,128)(2,1)}, bf16[4,1024,512]{2,1,0:T(8,128)(2,1)}, u32[]{:S(2)}, u32[]{:S(2)}) collective-permute-start(bf16[4,1024,512]{2,1,0:T(8,128)(2,1)} %refs_16_.1), channel_id=1, source_target_pairs={{0,2},{2,0},{4,6},{6,4},{8,10},{10,8},{12,14},{14,12},{1,3},{3,1},... | collective-permute-start | bytes 12582920 | tf_op jit(solution)/shard_map/ppermute | solution.py:339
  0.5 20.4 %collective-permute-start.8 = (bf16[4,1024,512]{2,1,0:T(8,128)(2,1)}, bf16[4,1024,512]{2,1,0:T(8,128)(2,1)}, u32[]{:S(2)}, u32[]{:S(2)}) collective-permute-start(bf16[4,1024,512]{2,1,0:T(8,128)(2,1)} %refs_17_.1), channel_id=1, source_target_pairs={{0,2},{2,0},{4,6},{6,4},{8,10},{10,8},{12,14},{14,12},{1,3},{3,1},... | collective-permute-start | bytes 12582920 | tf_op jit(solution)/shard_map/ppermute | solution.py:339
  2.1 7.5 %collective-permute-start.3 = (bf16[16,2176]{1,0:T(8,128)(2,1)}, bf16[16,2176]{1,0:T(8,128)(2,1)S(1)}, u32[]{:S(2)}, u32[]{:S(2)}) collective-permute-start(bf16[16,2176]{1,0:T(8,128)(2,1)} %get-tuple-element.17.refs_0_.refs_8_), channel_id=1, source_target_pairs={{0,8},{2,10},{4,12},{6,14},{8,0},{10,2},{12,4},{14,6},{1,9},{3,11}... | collective-permute-start | bytes 208904 | tf_op jit(solution)/shard_map/ppermute | solution.py:339
  6.1 4.5 %collective-permute-start.1 = (bf16[16,2176]{1,0:T(8,128)(2,1)}, bf16[16,2176]{1,0:T(8,128)(2,1)S(1)}, u32[]{:S(2)}, u32[]{:S(2)}) collective-permute-start(bf16[16,2176]{1,0:T(8,128)(2,1)} %get-tuple-element.17.refs_0_.refs_8_), channel_id=1, source_target_pairs={{0,4},{2,6},{4,0},{6,2},{8,12},{10,14},{12,8},{14,10},{1,5},{3,7},... | collective-permute-start | bytes 208904 | tf_op jit(solution)/shard_map/ppermute | solution.py:339
  7.7 6.7 %collective-permute-start.4 = (bf16[16,2176]{1,0:T(8,128)(2,1)}, bf16[16,2176]{1,0:T(8,128)(2,1)S(1)}, u32[]{:S(2)}, u32[]{:S(2)}) collective-permute-start(bf16[16,2176]{1,0:T(8,128)(2,1)} %get-tuple-element.18), channel_id=1, source_target_pairs={{0,10},{2,8},{4,14},{6,12},{8,2},{10,0},{12,6},{14,4},{1,11},{3,9}... | collective-permute-start | bytes 208904 | tf_op jit(solution)/shard_map/ppermute | solution.py:339
  9.6 11.3 %copy-start.3 = (bf16[16,2176]{1,0:T(8,128)(2,1)}, bf16[16,2176]{1,0:T(8,128)(2,1)S(1)}, u32[]{:S(2)}) copy-start(bf16[16,2176]{1,0:T(8,128)(2,1)S(1)} %collective-permute-done.3.refs_4_.refs_12_) | copy-start | bytes 208900
  9.6 5.9 %collective-permute-start.2 = (bf16[16,2176]{1,0:T(8,128)(2,1)}, bf16[16,2176]{1,0:T(8,128)(2,1)S(1)}, u32[]{:S(2)}, u32[]{:S(2)}) collective-permute-start(bf16[16,2176]{1,0:T(8,128)(2,1)} %get-tuple-element.18), channel_id=1, source_target_pairs={{0,6},{2,4},{4,2},{6,0},{8,14},{10,12},{12,10},{14,8},{1,7},{3,5},... | collective-permute-start | bytes 208904 | tf_op jit(solution)/shard_map/ppermute | solution.py:339
  10.6 10.3 %copy-start.4 = (bf16[16,2176]{1,0:T(8,128)(2,1)}, bf16[16,2176]{1,0:T(8,128)(2,1)S(1)}, u32[]{:S(2)}) copy-start(bf16[16,2176]{1,0:T(8,128)(2,1)S(1)} %collective-permute-done.1.refs_2_.refs_10_) | copy-start | bytes 208900
  10.6 10.2 %collective-permute-start = (bf16[16,2176]{1,0:T(8,128)(2,1)}, bf16[16,2176]{1,0:T(8,128)(2,1)S(1)}, u32[]{:S(2)}, u32[]{:S(2)}) collective-permute-start(bf16[16,2176]{1,0:T(8,128)(2,1)} %get-tuple-element.18), channel_id=1, source_target_pairs={{0,2},{2,0},{4,6},{6,4},{8,10},{10,8},{12,14},{14,12},{1,3},{3,1},... | collective-permute-start | bytes 208904 | tf_op jit(solution)/shard_map/ppermute | solution.py:339
  14.4 6.5 %copy-start.5 = (bf16[16,2176]{1,0:T(8,128)(2,1)}, bf16[16,2176]{1,0:T(8,128)(2,1)S(1)}, u32[]{:S(2)}) copy-start(bf16[16,2176]{1,0:T(8,128)(2,1)S(1)} %collective-permute-done.4.refs_5_.refs_13_) | copy-start | bytes 208900
  14.4 6.4 %collective-permute-start.5 = (bf16[16,2176]{1,0:T(8,128)(2,1)S(1)}, bf16[16,2176]{1,0:T(8,128)(2,1)S(1)}, u32[]{:S(2)}, u32[]{:S(2)}) collective-permute-start(bf16[16,2176]{1,0:T(8,128)(2,1)S(1)} %collective-permute-done.3.refs_4_.refs_12_), channel_id=1, source_target_pairs={{0,4},{2,6},{4,0},{6,2},{8,12},{10,14},{12,8},{14,10},{1,5},{3,7},... | collective-permute-start | bytes 208904 | tf_op jit(solution)/shard_map/ppermute | solution.py:339
  15.5 5.4 %copy-start.6 = (bf16[16,2176]{1,0:T(8,128)(2,1)}, bf16[16,2176]{1,0:T(8,128)(2,1)S(1)}, u32[]{:S(2)}) copy-start(bf16[16,2176]{1,0:T(8,128)(2,1)S(1)} %collective-permute-done.2.refs_3_.refs_11_) | copy-start | bytes 208900
  15.6 5.3 %collective-permute-start.6 = (bf16[16,2176]{1,0:T(8,128)(2,1)S(1)}, bf16[16,2176]{1,0:T(8,128)(2,1)S(1)}, u32[]{:S(2)}, u32[]{:S(2)}) collective-permute-start(bf16[16,2176]{1,0:T(8,128)(2,1)S(1)} %collective-permute-done.4.refs_5_.refs_13_), channel_id=1, source_target_pairs={{0,4},{2,6},{4,0},{6,2},{8,12},{10,14},{12,8},{14,10},{1,5},{3,7},... | collective-permute-start | bytes 208904 | tf_op jit(solution)/shard_map/ppermute | solution.py:339
  20.8 0.7 copy-start.8
  21.5 72.8 %copy-start = (f32[16,4096]{1,0:T(8,128)S(1)}, f32[16,4096]{1,0:T(8,128)}, u32[]{:S(2)}) copy-start(f32[16,4096]{1,0:T(8,128)} %get-tuple-element.28.refs_8_) | copy-start | bytes 786436
  21.5 72.8 %copy-start.2 = (f32[2,16,128]{2,1,0:T(8,128)S(1)}, f32[2,16,128]{2,1,0:T(8,128)}, u32[]{:S(2)}) copy-start(f32[2,16,128]{2,1,0:T(8,128)} %get-tuple-element.19.refs_20_.refs_9_) | copy-start | bytes 49156
  78.6 5.3 %collective-permute-start.9 = (bf16[16,2176]{1,0:T(8,128)(2,1)}, bf16[16,2176]{1,0:T(8,128)(2,1)S(1)}, u32[]{:S(2)}, u32[]{:S(2)}) collective-permute-start(bf16[16,2176]{1,0:T(8,128)(2,1)} %get-tuple-element.21), channel_id=1, source_target_pairs={{0,4},{2,6},{4,0},{6,2},{8,12},{10,14},{12,8},{14,10},{1,5},{3,7},... | collective-permute-start | bytes 208904 | tf_op jit(solution)/shard_map/ppermute | solution.py:339
  79.8 8.7 %collective-permute-start.10 = (bf16[16,2176]{1,0:T(8,128)(2,1)}, bf16[16,2176]{1,0:T(8,128)(2,1)S(1)}, u32[]{:S(2)}, u32[]{:S(2)}) collective-permute-start(bf16[16,2176]{1,0:T(8,128)(2,1)} %get-tuple-element.22), channel_id=1, source_target_pairs={{0,8},{2,10},{4,12},{6,14},{8,0},{10,2},{12,4},{14,6},{1,9},{3,11}... | collective-permute-start | bytes 208904 | tf_op jit(solution)/shard_map/ppermute | solution.py:339
  81.7 7.6 %collective-permute-start.11 = (bf16[16,2176]{1,0:T(8,128)(2,1)}, bf16[16,2176]{1,0:T(8,128)(2,1)S(1)}, u32[]{:S(2)}, u32[]{:S(2)}) collective-permute-start(bf16[16,2176]{1,0:T(8,128)(2,1)} %get-tuple-element.23), channel_id=1, source_target_pairs={{0,12},{2,14},{4,8},{6,10},{8,4},{10,6},{12,0},{14,2},{1,13},{3,15... | collective-permute-start | bytes 208904 | tf_op jit(solution)/shard_map/ppermute | solution.py:339
  83.1 6.3 %collective-permute-start.12 = (bf16[16,2176]{1,0:T(8,128)(2,1)}, bf16[16,2176]{1,0:T(8,128)(2,1)S(1)}, u32[]{:S(2)}, u32[]{:S(2)}) collective-permute-start(bf16[16,2176]{1,0:T(8,128)(2,1)} %get-tuple-element.24), channel_id=1, source_target_pairs={{0,2},{2,0},{4,6},{6,4},{8,10},{10,8},{12,14},{14,12},{1,3},{3,1},... | collective-permute-start | bytes 208904 | tf_op jit(solution)/shard_map/ppermute | solution.py:339
  83.1 6.3 %collective-permute-start.13 = (bf16[16,2176]{1,0:T(8,128)(2,1)}, bf16[16,2176]{1,0:T(8,128)(2,1)S(1)}, u32[]{:S(2)}, u32[]{:S(2)}) collective-permute-start(bf16[16,2176]{1,0:T(8,128)(2,1)} %get-tuple-element.25), channel_id=1, source_target_pairs={{0,6},{2,4},{4,2},{6,0},{8,14},{10,12},{12,10},{14,8},{1,7},{3,5},... | collective-permute-start | bytes 208904 | tf_op jit(solution)/shard_map/ppermute | solution.py:339
  83.9 7.6 %collective-permute-start.14 = (bf16[16,2176]{1,0:T(8,128)(2,1)}, bf16[16,2176]{1,0:T(8,128)(2,1)S(1)}, u32[]{:S(2)}, u32[]{:S(2)}) collective-permute-start(bf16[16,2176]{1,0:T(8,128)(2,1)} %get-tuple-element.26), channel_id=1, source_target_pairs={{0,10},{2,8},{4,14},{6,12},{8,2},{10,0},{12,6},{14,4},{1,11},{3,9}... | collective-permute-start | bytes 208904 | tf_op jit(solution)/shard_map/ppermute | solution.py:339
  88.5 5.7 %collective-permute-start.15 = (bf16[16,2176]{1,0:T(8,128)(2,1)}, bf16[16,2176]{1,0:T(8,128)(2,1)S(1)}, u32[]{:S(2)}, u32[]{:S(2)}) collective-permute-start(bf16[16,2176]{1,0:T(8,128)(2,1)} %get-tuple-element.27), channel_id=1, source_target_pairs={{0,14},{2,12},{4,10},{6,8},{8,6},{10,4},{12,2},{14,0},{1,15},{3,13... | collective-permute-start | bytes 208904 | tf_op jit(solution)/shard_map/ppermute | solution.py:339
  94.3 0.9 copy-start.1
  (2 other events, 1.3 us)

commit v10 on v9

--- a/solution.py
+++ b/solution.py
@@ -207,7 +207,8 @@
     )(where, place, *queries, *queries, *caches, *after)
 
 
-def suffix_kernel(group_size, lengths_ref, q_ref, k_ref, v_ref, out_ref, log_ref):
+def suffix_kernel(group_size, lengths_ref, q_ref, k_ref, v_ref, pass_ref, where_ref, out_ref, log_ref, passed_ref):
+    passed_ref[...] = pass_ref[...]
     rows_here, steps, width = q_ref.shape
     tokens = k_ref.shape[1]
     kv_here = k_ref.shape[2] // HD
@@ -246,7 +247,7 @@
         log_ref[side] = logs[side]
 
 
-def attend_suffix(lengths, queries, suffix_k, suffix_v):
+def attend_suffix(lengths, queries, suffix_k, suffix_v, passing, where):
     rows, steps, width = queries.shape
     _, tokens, kv_width = suffix_k.shape
     items = rows * steps
@@ -256,15 +257,18 @@
         grid_spec=pltpu.PrefetchScalarGridSpec(
             num_scalar_prefetch=1,
             grid=(1,),
-            in_specs=[pl.BlockSpec(x.shape, whole) for x in (queries, suffix_k, suffix_v)],
+            in_specs=[pl.BlockSpec(x.shape, whole) for x in (queries, suffix_k, suffix_v)]
+            + [pl.BlockSpec(passing.shape, lambda i, n: (0, 0)), ANY],
             out_specs=[
                 pl.BlockSpec((items, width), lambda i, n: (0, 0)),
                 pl.BlockSpec((2, items, LANES), whole),
+                pl.BlockSpec(passing.shape, lambda i, n: (0, 0)),
             ],
         ),
         out_shape=(
             jax.ShapeDtypeStruct((items, width), jnp.float32),
             jax.ShapeDtypeStruct((2, items, LANES), jnp.float32),
+            jax.ShapeDtypeStruct(passing.shape, passing.dtype),
         ),
         compiler_params=params(),
         cost_estimate=pl.CostEstimate(
@@ -272,7 +276,7 @@
             bytes_accessed=4 * suffix_k.size + 6 * items * width,
             transcendentals=items * rows * tokens * width // HD,
         ),
-    )(lengths, queries, suffix_k, suffix_v)
+    )(lengths, queries, suffix_k, suffix_v, passing, where)
 
 
 def weigh(parts, items, heads):
@@ -343,17 +347,20 @@
     place = placement.reshape(1, -1)
     caches = [cache_k, cache_v, swap(cache_k, 1), swap(cache_v, 1)]
     packed = pack(queries, selected)
-    out_s, log_s = attend_suffix(lengths, queries, suffix_k, suffix_v)
+    out_s, log_s, passed = attend_suffix(
+        lengths, queries, suffix_k, suffix_v, packed[1], where
+    )
     attend = functools.partial(attend_blocks, where, place, caches, group_size)
     if chips == 4:
-        arrived = {n: swap(packed[n % 2], n) for n in (4, 5, 2, 3, 0, 1)}
+        arrived = {n: swap(packed[n % 2], n) for n in (4, 5, 2, 0)}
+        arrived.update({n: swap(passed, n) for n in (3, 1)})
         arrived.update({n: swap(arrived[n - 2], 2) for n in (6, 7)})
         partial = attend([arrived[n] for n in range(size)], size, [log_s])
-        back = {n: swap(partial[n], n) for n in (3, 4, 5, 6, 7, 2, 1, 0)}
+        back = {n: swap(partial[n], n) for n in (1, 3, 4, 5, 6, 7, 2, 0)}
         sides = [[back[n] for n in range(side, size, 2)] for side in range(2)]
     else:
         same = [[2 * z + core for z in range(chips)] for core in range(2)]
-        chip = jnp.concatenate([packed[0], swap(packed[1], 1)], axis=0)
+        chip = jnp.concatenate([packed[0], swap(passed, 1)], axis=0)
         every = lax.all_gather(chip, "ctx", axis=0, tiled=True, axis_index_groups=same)
         (partial,) = attend([every], 1, [log_s])
         back = lax.all_to_all(

time: 96.8 us -> 97.6 us (level)
  waiting for transfers between devices: 13.7 us -> 16 us
  starting transfers between devices: 16.8 us -> 15.4 us
    ppermute x16, waiting for transfers between devices: 13.7 us -> 16 us  [swap(): lax.ppermute(x, 'ctx', [(i, i ^ bits) for i in range(size)])]
    ppermute x16, starting transfers between devices: 16.8 us -> 15.4 us  [swap(): lax.ppermute(x, 'ctx', [(i, i ^ bits) for i in range(size)])]
  transfers between devices with their start and end apart: 16 -> 16, of which waited for: 8 -> 10; matrix products, arithmetic and copies ran while one was open for 1% -> 1% of each run, Pallas kernels for 6% -> 6%
where the time goes in v10:
time: 97.6 us; the launch traced here: 97.4 us
  Pallas kernels  63.9 us (65%)
  waiting for transfers between devices  16 us (16%)
  starting transfers between devices  15.4 us (16%)
  local copies, waits for them, and re-layouts  1.47 us (2%)
    pallas_call x1, Pallas kernels, attend_blocks(): pl.pallas_call(functools.partial(block_kernel, pieces, outs, group_size,...  57.1 us
    ppermute x16, waiting for transfers between devices, swap(): lax.ppermute(x, 'ctx', [(i, i ^ bits) for i in range(size)])  16 us
    ppermute x16, starting transfers between devices, swap(): lax.ppermute(x, 'ctx', [(i, i ^ bits) for i in range(size)])  15.4 us
    pallas_call x1, Pallas kernels, attend_suffix(): pl.pallas_call(functools.partial(suffix_kernel, width // kv_width), grid_...  3.84 us
  transfers between devices with their start and end apart: 16, of which 10 were waited for; matrix products, arithmetic and copies ran while one was open for 1% of the time, Pallas kernels for 6%

profile of v10, /device:TPU:0, one launch (start us, length us, event | category | flops | bytes accessed | tf_op | source)
XLA Modules:
  0.0 97.4 jit_solution(16926816045915024748)
XLA Ops:
  0.0 0.5 collective-permute-start.7
  0.5 1.6 %shard_map.82 = (bf16[16,2176]{1,0:T(8,128)(2,1)}, bf16[16,2176]{1,0:T(8,128)(2,1)}) custom-call(bf16[4,4,4096]{2,1,0:T(4,128)(2,1)} %q_ref.3, s32[4,4,16]{2,1,0:T(4,128)} %selected_ref.1), custom_call_target="tpu_custom_call" | custom-call | tf_op jit(solution)/shard_map/pallas_call | solution.py:68
  2.1 4.0 %collective-permute-start.3 = (bf16[16,2176]{1,0:T(8,128)(2,1)}, bf16[16,2176]{1,0:T(8,128)(2,1)S(1)}, u32[]{:S(2)}, u32[]{:S(2)}) collective-permute-start(bf16[16,2176]{1,0:T(8,128)(2,1)} %get-tuple-element.18.refs_0_.refs_8_), channel_id=1, source_target_pairs={{0,8},{2,10},{4,12},{6,14},{8,0},{10,2},{12,4},{14,6},{1,9},{3,11}... | collective-permute-start | bytes 208904 | tf_op jit(solution)/shard_map/ppermute | solution.py:343
  6.1 1.6 %collective-permute-start.1 = (bf16[16,2176]{1,0:T(8,128)(2,1)}, bf16[16,2176]{1,0:T(8,128)(2,1)S(1)}, u32[]{:S(2)}, u32[]{:S(2)}) collective-permute-start(bf16[16,2176]{1,0:T(8,128)(2,1)} %get-tuple-element.18.refs_0_.refs_8_), channel_id=1, source_target_pairs={{0,4},{2,6},{4,0},{6,2},{8,12},{10,14},{12,8},{14,10},{1,5},{3,7},... | collective-permute-start | bytes 208904 | tf_op jit(solution)/shard_map/ppermute | solution.py:343
  7.7 0.6 pad_add_fusion.where_ref
  8.3 3.8 %shard_map.83 = (f32[16,4096]{1,0:T(8,128)}, f32[2,16,128]{2,1,0:T(8,128)}, bf16[16,2176]{1,0:T(8,128)(2,1)}) custom-call(s32[4]{0:T(128)} %lengths_ref.1, bf16[4,4,4096]{2,1,0:T(4,128)(2,1)} %q_ref.3, bf16[4,128,512]{2,1,0:T(8,128)(2,1)} %k_ref.1, bf16[4,128,512]{2,1,0:T(8,128)(2,1)} %v_ref.1, bf16[16,2176]{1,0:T(8,128)(2,1)} %get-tuple-element.19.pass_ref, ...), custom_call_target="tpu_custom_call" | custom-call | flops 536870912 | bytes 1441792 | tf_op jit(solution)/shard_map/pallas_call | solution.py:255
  12.1 2.2 %collective-permute-done.4.refs_5_.refs_13_ = bf16[16,2176]{1,0:T(8,128)(2,1)S(1)} collective-permute-done((bf16[16,2176]{1,0:T(8,128)(2,1)}, bf16[16,2176]{1,0:T(8,128)(2,1)S(1)}, u32[]{:S(2)}, u32[]{:S(2)}) %collective-permute-start.4) | collective-permute-done | bytes 69664 | tf_op jit(solution)/shard_map/ppermute | solution.py:343
  14.5 2.0 %collective-permute-start.6 = (bf16[16,2176]{1,0:T(8,128)(2,1)S(1)}, bf16[16,2176]{1,0:T(8,128)(2,1)S(1)}, u32[]{:S(2)}, u32[]{:S(2)}) collective-permute-start(bf16[16,2176]{1,0:T(8,128)(2,1)S(1)} %collective-permute-done.4.refs_5_.refs_13_), channel_id=1, source_target_pairs={{0,4},{2,6},{4,0},{6,2},{8,12},{10,14},{12,8},{14,10},{1,5},{3,7},... | collective-permute-start | bytes 208904 | tf_op jit(solution)/shard_map/ppermute | solution.py:343
  16.4 2.3 %collective-permute-done.2.refs_3_.refs_11_ = bf16[16,2176]{1,0:T(8,128)(2,1)S(1)} collective-permute-done((bf16[16,2176]{1,0:T(8,128)(2,1)}, bf16[16,2176]{1,0:T(8,128)(2,1)S(1)}, u32[]{:S(2)}, u32[]{:S(2)}) %collective-permute-start.2) | collective-permute-done | bytes 69664 | tf_op jit(solution)/shard_map/ppermute | solution.py:343
  18.9 1.6 %collective-permute-done.6.refs_7_.refs_15_ = bf16[16,2176]{1,0:T(8,128)(2,1)S(1)} collective-permute-done((bf16[16,2176]{1,0:T(8,128)(2,1)S(1)}, bf16[16,2176]{1,0:T(8,128)(2,1)S(1)}, u32[]{:S(2)}, u32[]{:S(2)}) %collective-permute-start.6) | collective-permute-done | bytes 69664 | tf_op jit(solution)/shard_map/ppermute | solution.py:343
  20.5 2.7 %collective-permute-done.5.refs_6_.refs_14_ = bf16[16,2176]{1,0:T(8,128)(2,1)S(1)} collective-permute-done((bf16[16,2176]{1,0:T(8,128)(2,1)S(1)}, bf16[16,2176]{1,0:T(8,128)(2,1)S(1)}, u32[]{:S(2)}, u32[]{:S(2)}) %collective-permute-start.5) | collective-permute-done | bytes 69664 | tf_op jit(solution)/shard_map/ppermute | solution.py:343
  23.2 0.6 copy-done.9
  23.8 57.1 %shard_map.84 = (bf16[16,2176]{1,0:T(8,128)(2,1)}, bf16[16,2176]{1,0:T(8,128)(2,1)}, bf16[16,2176]{1,0:T(8,128)(2,1)}, bf16[16,2176]{1,0:T(8,128)(2,1)}, bf16[16...) custom-call(s32[3]{0:T(128)} %pad_add_fusion.where_ref, ...), custom_call_target="tpu_custom_call" | custom-call | flops 285212672 | bytes 1114112 | tf_op jit(solution)/shard_map/pallas_call | solution.py:184
  81.2 2.5 %collective-permute-start.10 = (bf16[16,2176]{1,0:T(8,128)(2,1)}, bf16[16,2176]{1,0:T(8,128)(2,1)S(1)}, u32[]{:S(2)}, u32[]{:S(2)}) collective-permute-start(bf16[16,2176]{1,0:T(8,128)(2,1)} %get-tuple-element.24), channel_id=1, source_target_pairs={{0,8},{2,10},{4,12},{6,14},{8,0},{10,2},{12,4},{14,6},{1,9},{3,11}... | collective-permute-start | bytes 208904 | tf_op jit(solution)/shard_map/ppermute | solution.py:343
  83.7 1.6 %collective-permute-start.11 = (bf16[16,2176]{1,0:T(8,128)(2,1)}, bf16[16,2176]{1,0:T(8,128)(2,1)S(1)}, u32[]{:S(2)}, u32[]{:S(2)}) collective-permute-start(bf16[16,2176]{1,0:T(8,128)(2,1)} %get-tuple-element.25), channel_id=1, source_target_pairs={{0,12},{2,14},{4,8},{6,10},{8,4},{10,6},{12,0},{14,2},{1,13},{3,15... | collective-permute-start | bytes 208904 | tf_op jit(solution)/shard_map/ppermute | solution.py:343
  85.3 0.5 collective-permute-done.9.refs_1_
  85.8 2.1 %collective-permute-start.14 = (bf16[16,2176]{1,0:T(8,128)(2,1)}, bf16[16,2176]{1,0:T(8,128)(2,1)S(1)}, u32[]{:S(2)}, u32[]{:S(2)}) collective-permute-start(bf16[16,2176]{1,0:T(8,128)(2,1)} %get-tuple-element.28), channel_id=1, source_target_pairs={{0,10},{2,8},{4,14},{6,12},{8,2},{10,0},{12,6},{14,4},{1,11},{3,9}... | collective-permute-start | bytes 208904 | tf_op jit(solution)/shard_map/ppermute | solution.py:343
  87.8 1.3 %collective-permute-done.10.refs_2_ = bf16[16,2176]{1,0:T(8,128)(2,1)S(1)} collective-permute-done((bf16[16,2176]{1,0:T(8,128)(2,1)}, bf16[16,2176]{1,0:T(8,128)(2,1)S(1)}, u32[]{:S(2)}, u32[]{:S(2)}) %collective-permute-start.10) | collective-permute-done | bytes 69664 | tf_op jit(solution)/shard_map/ppermute | solution.py:343
  89.5 1.2 %collective-permute-done.11.refs_3_ = bf16[16,2176]{1,0:T(8,128)(2,1)S(1)} collective-permute-done((bf16[16,2176]{1,0:T(8,128)(2,1)}, bf16[16,2176]{1,0:T(8,128)(2,1)S(1)}, u32[]{:S(2)}, u32[]{:S(2)}) %collective-permute-start.11) | collective-permute-done | bytes 69664 | tf_op jit(solution)/shard_map/ppermute | solution.py:343
  90.7 1.0 collective-permute-done.13.refs_5_
  91.7 1.7 %collective-permute-done.14.refs_6_ = bf16[16,2176]{1,0:T(8,128)(2,1)S(1)} collective-permute-done((bf16[16,2176]{1,0:T(8,128)(2,1)}, bf16[16,2176]{1,0:T(8,128)(2,1)S(1)}, u32[]{:S(2)}, u32[]{:S(2)}) %collective-permute-start.14) | collective-permute-done | bytes 69664 | tf_op jit(solution)/shard_map/ppermute | solution.py:343
  93.4 1.7 %collective-permute-done.15.refs_7_ = bf16[16,2176]{1,0:T(8,128)(2,1)S(1)} collective-permute-done((bf16[16,2176]{1,0:T(8,128)(2,1)}, bf16[16,2176]{1,0:T(8,128)(2,1)S(1)}, u32[]{:S(2)}, u32[]{:S(2)}) %collective-permute-start.15) | collective-permute-done | bytes 69664 | tf_op jit(solution)/shard_map/ppermute | solution.py:343
  95.1 0.9 copy-done.1
  96.0 1.4 %shard_map.85 = bf16[4,4,4096]{2,1,0:T(4,128)(2,1)} custom-call(bf16[16,2176]{1,0:T(8,128)(2,1)S(1)} %copy-done.1, bf16[16,2176]{1,0:T(8,128)(2,1)S(1)} %collective-permute-done.9.refs_1_, bf16[16,2176]{1,0:T(8,128)(2,1)S(1)} %collective-permute-done.10.refs_2_, bf16[16,2176]{1,0:T(8,128)(2,1)S(1)} %collective-permute-done.11.refs_3_, ...), custom_call_target="tpu_custom_call" | custom-call | tf_op jit(solution)/shard_map/pallas_call | solution.py:327
  (33 shorter events, 1.2 us)
Async XLA Ops:
  0.0 23.2 %collective-permute-start.7 = (bf16[4,1024,512]{2,1,0:T(8,128)(2,1)}, bf16[4,1024,512]{2,1,0:T(8,128)(2,1)}, u32[]{:S(2)}, u32[]{:S(2)}) collective-permute-start(bf16[4,1024,512]{2,1,0:T(8,128)(2,1)} %refs_16_.1), channel_id=1, source_target_pairs={{0,2},{2,0},{4,6},{6,4},{8,10},{10,8},{12,14},{14,12},{1,3},{3,1},... | collective-permute-start | bytes 12582920 | tf_op jit(solution)/shard_map/ppermute | solution.py:343
  0.5 22.7 %collective-permute-start.8 = (bf16[4,1024,512]{2,1,0:T(8,128)(2,1)}, bf16[4,1024,512]{2,1,0:T(8,128)(2,1)}, u32[]{:S(2)}, u32[]{:S(2)}) collective-permute-start(bf16[4,1024,512]{2,1,0:T(8,128)(2,1)} %refs_17_.1), channel_id=1, source_target_pairs={{0,2},{2,0},{4,6},{6,4},{8,10},{10,8},{12,14},{14,12},{1,3},{3,1},... | collective-permute-start | bytes 12582920 | tf_op jit(solution)/shard_map/ppermute | solution.py:343
  2.1 12.2 %collective-permute-start.3 = (bf16[16,2176]{1,0:T(8,128)(2,1)}, bf16[16,2176]{1,0:T(8,128)(2,1)S(1)}, u32[]{:S(2)}, u32[]{:S(2)}) collective-permute-start(bf16[16,2176]{1,0:T(8,128)(2,1)} %get-tuple-element.18.refs_0_.refs_8_), channel_id=1, source_target_pairs={{0,8},{2,10},{4,12},{6,14},{8,0},{10,2},{12,4},{14,6},{1,9},{3,11}... | collective-permute-start | bytes 208904 | tf_op jit(solution)/shard_map/ppermute | solution.py:343
  6.1 8.3 %collective-permute-start.1 = (bf16[16,2176]{1,0:T(8,128)(2,1)}, bf16[16,2176]{1,0:T(8,128)(2,1)S(1)}, u32[]{:S(2)}, u32[]{:S(2)}) collective-permute-start(bf16[16,2176]{1,0:T(8,128)(2,1)} %get-tuple-element.18.refs_0_.refs_8_), channel_id=1, source_target_pairs={{0,4},{2,6},{4,0},{6,2},{8,12},{10,14},{12,8},{14,10},{1,5},{3,7},... | collective-permute-start | bytes 208904 | tf_op jit(solution)/shard_map/ppermute | solution.py:343
  7.7 6.6 %collective-permute-start.4 = (bf16[16,2176]{1,0:T(8,128)(2,1)}, bf16[16,2176]{1,0:T(8,128)(2,1)S(1)}, u32[]{:S(2)}, u32[]{:S(2)}) collective-permute-start(bf16[16,2176]{1,0:T(8,128)(2,1)} %get-tuple-element.19.pass_ref), channel_id=1, source_target_pairs={{0,10},{2,8},{4,14},{6,12},{8,2},{10,0},{12,6},{14,4},{1,11},{3,9}... | collective-permute-start | bytes 208904 | tf_op jit(solution)/shard_map/ppermute | solution.py:343
  14.3 8.9 %copy-start.5 = (bf16[16,2176]{1,0:T(8,128)(2,1)}, bf16[16,2176]{1,0:T(8,128)(2,1)S(1)}, u32[]{:S(2)}) copy-start(bf16[16,2176]{1,0:T(8,128)(2,1)S(1)} %collective-permute-done.4.refs_5_.refs_13_) | copy-start | bytes 208900
  14.3 4.4 %collective-permute-start.2 = (bf16[16,2176]{1,0:T(8,128)(2,1)}, bf16[16,2176]{1,0:T(8,128)(2,1)S(1)}, u32[]{:S(2)}, u32[]{:S(2)}) collective-permute-start(bf16[16,2176]{1,0:T(8,128)(2,1)} %get-tuple-element.20), channel_id=1, source_target_pairs={{0,6},{2,4},{4,2},{6,0},{8,14},{10,12},{12,10},{14,8},{1,7},{3,5},... | collective-permute-start | bytes 208904 | tf_op jit(solution)/shard_map/ppermute | solution.py:343
  14.3 8.9 %copy-start.3 = (bf16[16,2176]{1,0:T(8,128)(2,1)}, bf16[16,2176]{1,0:T(8,128)(2,1)S(1)}, u32[]{:S(2)}) copy-start(bf16[16,2176]{1,0:T(8,128)(2,1)S(1)} %collective-permute-done.3.refs_4_.refs_12_) | copy-start | bytes 208900
  14.3 4.6 %collective-permute-start = (bf16[16,2176]{1,0:T(8,128)(2,1)}, bf16[16,2176]{1,0:T(8,128)(2,1)S(1)}, u32[]{:S(2)}, u32[]{:S(2)}) collective-permute-start(bf16[16,2176]{1,0:T(8,128)(2,1)} %get-tuple-element.20), channel_id=1, source_target_pairs={{0,2},{2,0},{4,6},{6,4},{8,10},{10,8},{12,14},{14,12},{1,3},{3,1},... | collective-permute-start | bytes 208904 | tf_op jit(solution)/shard_map/ppermute | solution.py:343
  14.5 8.7 %copy-start.4 = (bf16[16,2176]{1,0:T(8,128)(2,1)}, bf16[16,2176]{1,0:T(8,128)(2,1)S(1)}, u32[]{:S(2)}) copy-start(bf16[16,2176]{1,0:T(8,128)(2,1)S(1)} %collective-permute-done.1.refs_2_.refs_10_) | copy-start | bytes 208900
  14.5 6.0 %collective-permute-start.6 = (bf16[16,2176]{1,0:T(8,128)(2,1)S(1)}, bf16[16,2176]{1,0:T(8,128)(2,1)S(1)}, u32[]{:S(2)}, u32[]{:S(2)}) collective-permute-start(bf16[16,2176]{1,0:T(8,128)(2,1)S(1)} %collective-permute-done.4.refs_5_.refs_13_), channel_id=1, source_target_pairs={{0,4},{2,6},{4,0},{6,2},{8,12},{10,14},{12,8},{14,10},{1,5},{3,7},... | collective-permute-start | bytes 208904 | tf_op jit(solution)/shard_map/ppermute | solution.py:343
  18.7 4.5 %copy-start.6 = (bf16[16,2176]{1,0:T(8,128)(2,1)}, bf16[16,2176]{1,0:T(8,128)(2,1)S(1)}, u32[]{:S(2)}) copy-start(bf16[16,2176]{1,0:T(8,128)(2,1)S(1)} %collective-permute-done.2.refs_3_.refs_11_) | copy-start | bytes 208900
  18.7 4.4 %collective-permute-start.5 = (bf16[16,2176]{1,0:T(8,128)(2,1)S(1)}, bf16[16,2176]{1,0:T(8,128)(2,1)S(1)}, u32[]{:S(2)}, u32[]{:S(2)}) collective-permute-start(bf16[16,2176]{1,0:T(8,128)(2,1)S(1)} %collective-permute-done.3.refs_4_.refs_12_), channel_id=1, source_target_pairs={{0,4},{2,6},{4,0},{6,2},{8,12},{10,14},{12,8},{14,10},{1,5},{3,7},... | collective-permute-start | bytes 208904 | tf_op jit(solution)/shard_map/ppermute | solution.py:343
  18.9 4.3 %copy-start.7 = (bf16[16,2176]{1,0:T(8,128)(2,1)}, bf16[16,2176]{1,0:T(8,128)(2,1)S(1)}, u32[]{:S(2)}) copy-start(bf16[16,2176]{1,0:T(8,128)(2,1)S(1)} %collective-permute-done.refs_1_.refs_9_) | copy-start | bytes 208900
  20.5 2.7 %copy-start.8 = (bf16[16,2176]{1,0:T(8,128)(2,1)}, bf16[16,2176]{1,0:T(8,128)(2,1)S(1)}, u32[]{:S(2)}) copy-start(bf16[16,2176]{1,0:T(8,128)(2,1)S(1)} %collective-permute-done.6.refs_7_.refs_15_) | copy-start | bytes 208900
  23.8 71.3 %copy-start = (f32[16,4096]{1,0:T(8,128)S(1)}, f32[16,4096]{1,0:T(8,128)}, u32[]{:S(2)}) copy-start(f32[16,4096]{1,0:T(8,128)} %get-tuple-element.30.refs_8_) | copy-start | bytes 786436
  23.8 71.3 %copy-start.2 = (f32[2,16,128]{2,1,0:T(8,128)S(1)}, f32[2,16,128]{2,1,0:T(8,128)}, u32[]{:S(2)}) copy-start(f32[2,16,128]{2,1,0:T(8,128)} %get-tuple-element.21.refs_20_.refs_9_) | copy-start | bytes 49156
  80.8 4.9 %collective-permute-start.9 = (bf16[16,2176]{1,0:T(8,128)(2,1)}, bf16[16,2176]{1,0:T(8,128)(2,1)S(1)}, u32[]{:S(2)}, u32[]{:S(2)}) collective-permute-start(bf16[16,2176]{1,0:T(8,128)(2,1)} %get-tuple-element.23), channel_id=1, source_target_pairs={{0,4},{2,6},{4,0},{6,2},{8,12},{10,14},{12,8},{14,10},{1,5},{3,7},... | collective-permute-start | bytes 208904 | tf_op jit(solution)/shard_map/ppermute | solution.py:343
  81.2 7.9 %collective-permute-start.10 = (bf16[16,2176]{1,0:T(8,128)(2,1)}, bf16[16,2176]{1,0:T(8,128)(2,1)S(1)}, u32[]{:S(2)}, u32[]{:S(2)}) collective-permute-start(bf16[16,2176]{1,0:T(8,128)(2,1)} %get-tuple-element.24), channel_id=1, source_target_pairs={{0,8},{2,10},{4,12},{6,14},{8,0},{10,2},{12,4},{14,6},{1,9},{3,11}... | collective-permute-start | bytes 208904 | tf_op jit(solution)/shard_map/ppermute | solution.py:343
  83.7 7.0 %collective-permute-start.11 = (bf16[16,2176]{1,0:T(8,128)(2,1)}, bf16[16,2176]{1,0:T(8,128)(2,1)S(1)}, u32[]{:S(2)}, u32[]{:S(2)}) collective-permute-start(bf16[16,2176]{1,0:T(8,128)(2,1)} %get-tuple-element.25), channel_id=1, source_target_pairs={{0,12},{2,14},{4,8},{6,10},{8,4},{10,6},{12,0},{14,2},{1,13},{3,15... | collective-permute-start | bytes 208904 | tf_op jit(solution)/shard_map/ppermute | solution.py:343
  85.3 5.4 %collective-permute-start.12 = (bf16[16,2176]{1,0:T(8,128)(2,1)}, bf16[16,2176]{1,0:T(8,128)(2,1)S(1)}, u32[]{:S(2)}, u32[]{:S(2)}) collective-permute-start(bf16[16,2176]{1,0:T(8,128)(2,1)} %get-tuple-element.26), channel_id=1, source_target_pairs={{0,2},{2,0},{4,6},{6,4},{8,10},{10,8},{12,14},{14,12},{1,3},{3,1},... | collective-permute-start | bytes 208904 | tf_op jit(solution)/shard_map/ppermute | solution.py:343
  85.3 6.4 %collective-permute-start.13 = (bf16[16,2176]{1,0:T(8,128)(2,1)}, bf16[16,2176]{1,0:T(8,128)(2,1)S(1)}, u32[]{:S(2)}, u32[]{:S(2)}) collective-permute-start(bf16[16,2176]{1,0:T(8,128)(2,1)} %get-tuple-element.27), channel_id=1, source_target_pairs={{0,6},{2,4},{4,2},{6,0},{8,14},{10,12},{12,10},{14,8},{1,7},{3,5},... | collective-permute-start | bytes 208904 | tf_op jit(solution)/shard_map/ppermute | solution.py:343
  85.8 7.6 %collective-permute-start.14 = (bf16[16,2176]{1,0:T(8,128)(2,1)}, bf16[16,2176]{1,0:T(8,128)(2,1)S(1)}, u32[]{:S(2)}, u32[]{:S(2)}) collective-permute-start(bf16[16,2176]{1,0:T(8,128)(2,1)} %get-tuple-element.28), channel_id=1, source_target_pairs={{0,10},{2,8},{4,14},{6,12},{8,2},{10,0},{12,6},{14,4},{1,11},{3,9}... | collective-permute-start | bytes 208904 | tf_op jit(solution)/shard_map/ppermute | solution.py:343
  89.1 6.0 %collective-permute-start.15 = (bf16[16,2176]{1,0:T(8,128)(2,1)}, bf16[16,2176]{1,0:T(8,128)(2,1)S(1)}, u32[]{:S(2)}, u32[]{:S(2)}) collective-permute-start(bf16[16,2176]{1,0:T(8,128)(2,1)} %get-tuple-element.29), channel_id=1, source_target_pairs={{0,14},{2,12},{4,10},{6,8},{8,6},{10,4},{12,2},{14,0},{1,15},{3,13... | collective-permute-start | bytes 208904 | tf_op jit(solution)/shard_map/ppermute | solution.py:343
  (2 other events, 1.5 us)

commit v11 on v10

--- a/solution.py
+++ b/solution.py
@@ -352,8 +352,8 @@
     )
     attend = functools.partial(attend_blocks, where, place, caches, group_size)
     if chips == 4:
-        arrived = {n: swap(packed[n % 2], n) for n in (4, 5, 2, 0)}
-        arrived.update({n: swap(passed, n) for n in (3, 1)})
+        arrived = {n: swap(packed[n % 2], n) for n in (4, 5, 2, 3, 0)}
+        arrived[1] = swap(passed, 1)
         arrived.update({n: swap(arrived[n - 2], 2) for n in (6, 7)})
         partial = attend([arrived[n] for n in range(size)], size, [log_s])
         back = {n: swap(partial[n], n) for n in (1, 3, 4, 5, 6, 7, 2, 0)}

time: 97.6 us -> 98.3 us (level)
  starting transfers between devices: 15.4 us -> 18.8 us
  waiting for transfers between devices: 16 us -> 13.3 us
    ppermute x16, starting transfers between devices: 15.4 us -> 18.8 us  [swap(): lax.ppermute(x, 'ctx', [(i, i ^ bits) for i in range(size)])]
    ppermute x16, waiting for transfers between devices: 16 us -> 13.3 us  [swap(): lax.ppermute(x, 'ctx', [(i, i ^ bits) for i in range(size)])]
  transfers between devices with their start and end apart: 16 -> 16, of which waited for: 10 -> 7; matrix products, arithmetic and copies ran while one was open for 1% -> 1% of each run, Pallas kernels for 6% -> 6%
where the time goes in v11:
time: 98.3 us; the launch traced here: 98.1 us
  Pallas kernels  63.9 us (65%)
  starting transfers between devices  18.8 us (19%)
  waiting for transfers between devices  13.3 us (14%)
  local copies, waits for them, and re-layouts  1.48 us (2%)
    pallas_call x1, Pallas kernels, attend_blocks(): pl.pallas_call(functools.partial(block_kernel, pieces, outs, group_size,...  57.1 us
    ppermute x16, starting transfers between devices, swap(): lax.ppermute(x, 'ctx', [(i, i ^ bits) for i in range(size)])  18.8 us
    ppermute x16, waiting for transfers between devices, swap(): lax.ppermute(x, 'ctx', [(i, i ^ bits) for i in range(size)])  13.3 us
    pallas_call x1, Pallas kernels, attend_suffix(): pl.pallas_call(functools.partial(suffix_kernel, width // kv_width), grid_...  3.84 us
  transfers between devices with their start and end apart: 16, of which 7 were waited for; matrix products, arithmetic and copies ran while one was open for 1% of the time, Pallas kernels for 6%

profile of v11, /device:TPU:0, one launch (start us, length us, event | category | flops | bytes accessed | tf_op | source)
XLA Modules:
  0.0 98.1 jit_solution(8294962074440511760)
XLA Ops:
  0.5 1.6 %shard_map.82 = (bf16[16,2176]{1,0:T(8,128)(2,1)}, bf16[16,2176]{1,0:T(8,128)(2,1)}) custom-call(bf16[4,4,4096]{2,1,0:T(4,128)(2,1)} %q_ref.3, s32[4,4,16]{2,1,0:T(4,128)} %selected_ref.1), custom_call_target="tpu_custom_call" | custom-call | tf_op jit(solution)/shard_map/pallas_call | solution.py:68
  2.1 4.0 %collective-permute-start.3 = (bf16[16,2176]{1,0:T(8,128)(2,1)}, bf16[16,2176]{1,0:T(8,128)(2,1)S(1)}, u32[]{:S(2)}, u32[]{:S(2)}) collective-permute-start(bf16[16,2176]{1,0:T(8,128)(2,1)} %get-tuple-element.18.refs_0_.refs_8_), channel_id=1, source_target_pairs={{0,8},{2,10},{4,12},{6,14},{8,0},{10,2},{12,4},{14,6},{1,9},{3,11}... | collective-permute-start | bytes 208904 | tf_op jit(solution)/shard_map/ppermute | solution.py:343
  6.1 1.6 %collective-permute-start.1 = (bf16[16,2176]{1,0:T(8,128)(2,1)}, bf16[16,2176]{1,0:T(8,128)(2,1)S(1)}, u32[]{:S(2)}, u32[]{:S(2)}) collective-permute-start(bf16[16,2176]{1,0:T(8,128)(2,1)} %get-tuple-element.18.refs_0_.refs_8_), channel_id=1, source_target_pairs={{0,4},{2,6},{4,0},{6,2},{8,12},{10,14},{12,8},{14,10},{1,5},{3,7},... | collective-permute-start | bytes 208904 | tf_op jit(solution)/shard_map/ppermute | solution.py:343
  7.7 1.9 %collective-permute-done.3.refs_4_.refs_12_ = bf16[16,2176]{1,0:T(8,128)(2,1)S(1)} collective-permute-done((bf16[16,2176]{1,0:T(8,128)(2,1)}, bf16[16,2176]{1,0:T(8,128)(2,1)S(1)}, u32[]{:S(2)}, u32[]{:S(2)}) %collective-permute-start.3) | collective-permute-done | bytes 69664 | tf_op jit(solution)/shard_map/ppermute | solution.py:343
  9.6 0.7 collective-permute-start.2
  10.3 0.6 pad_add_fusion.where_ref
  10.9 3.8 %shard_map.83 = (f32[16,4096]{1,0:T(8,128)}, f32[2,16,128]{2,1,0:T(8,128)}, bf16[16,2176]{1,0:T(8,128)(2,1)}) custom-call(s32[4]{0:T(128)} %lengths_ref.1, bf16[4,4,4096]{2,1,0:T(4,128)(2,1)} %q_ref.3, bf16[4,128,512]{2,1,0:T(8,128)(2,1)} %k_ref.1, bf16[4,128,512]{2,1,0:T(8,128)(2,1)} %v_ref.1, bf16[16,2176]{1,0:T(8,128)(2,1)} %get-tuple-element.19.pass_ref, ...), custom_call_target="tpu_custom_call" | custom-call | flops 536870912 | bytes 1441792 | tf_op jit(solution)/shard_map/pallas_call | solution.py:255
  14.8 1.4 %collective-permute-start = (bf16[16,2176]{1,0:T(8,128)(2,1)}, bf16[16,2176]{1,0:T(8,128)(2,1)S(1)}, u32[]{:S(2)}, u32[]{:S(2)}) collective-permute-start(bf16[16,2176]{1,0:T(8,128)(2,1)} %get-tuple-element.20), channel_id=1, source_target_pairs={{0,2},{2,0},{4,6},{6,4},{8,10},{10,8},{12,14},{14,12},{1,3},{3,1},... | collective-permute-start | bytes 208904 | tf_op jit(solution)/shard_map/ppermute | solution.py:343
  16.3 2.0 %collective-permute-start.6 = (bf16[16,2176]{1,0:T(8,128)(2,1)S(1)}, bf16[16,2176]{1,0:T(8,128)(2,1)S(1)}, u32[]{:S(2)}, u32[]{:S(2)}) collective-permute-start(bf16[16,2176]{1,0:T(8,128)(2,1)S(1)} %collective-permute-done.4.refs_5_.refs_13_), channel_id=1, source_target_pairs={{0,4},{2,6},{4,0},{6,2},{8,12},{10,14},{12,8},{14,10},{1,5},{3,7},... | collective-permute-start | bytes 208904 | tf_op jit(solution)/shard_map/ppermute | solution.py:343
  18.2 2.9 %collective-permute-done.5.refs_6_.refs_14_ = bf16[16,2176]{1,0:T(8,128)(2,1)S(1)} collective-permute-done((bf16[16,2176]{1,0:T(8,128)(2,1)S(1)}, bf16[16,2176]{1,0:T(8,128)(2,1)S(1)}, u32[]{:S(2)}, u32[]{:S(2)}) %collective-permute-start.5) | collective-permute-done | bytes 69664 | tf_op jit(solution)/shard_map/ppermute | solution.py:343
  21.1 0.7 collective-permute-done.6.refs_7_.refs_15_
  21.9 0.6 copy-done.9
  22.5 57.1 %shard_map.84 = (bf16[16,2176]{1,0:T(8,128)(2,1)}, bf16[16,2176]{1,0:T(8,128)(2,1)}, bf16[16,2176]{1,0:T(8,128)(2,1)}, bf16[16,2176]{1,0:T(8,128)(2,1)}, bf16[16...) custom-call(s32[3]{0:T(128)} %pad_add_fusion.where_ref, ...), custom_call_target="tpu_custom_call" | custom-call | flops 285212672 | bytes 1114112 | tf_op jit(solution)/shard_map/pallas_call | solution.py:184
  79.6 0.7 collective-permute-start.9
  80.3 3.7 %collective-permute-start.10 = (bf16[16,2176]{1,0:T(8,128)(2,1)}, bf16[16,2176]{1,0:T(8,128)(2,1)S(1)}, u32[]{:S(2)}, u32[]{:S(2)}) collective-permute-start(bf16[16,2176]{1,0:T(8,128)(2,1)} %get-tuple-element.24), channel_id=1, source_target_pairs={{0,8},{2,10},{4,12},{6,14},{8,0},{10,2},{12,4},{14,6},{1,9},{3,11}... | collective-permute-start | bytes 208904 | tf_op jit(solution)/shard_map/ppermute | solution.py:343
  84.0 0.8 collective-permute-start.11
  84.7 0.7 collective-permute-start.13
  85.4 2.6 %collective-permute-start.14 = (bf16[16,2176]{1,0:T(8,128)(2,1)}, bf16[16,2176]{1,0:T(8,128)(2,1)S(1)}, u32[]{:S(2)}, u32[]{:S(2)}) collective-permute-start(bf16[16,2176]{1,0:T(8,128)(2,1)} %get-tuple-element.28), channel_id=1, source_target_pairs={{0,10},{2,8},{4,14},{6,12},{8,2},{10,0},{12,6},{14,4},{1,11},{3,9}... | collective-permute-start | bytes 208904 | tf_op jit(solution)/shard_map/ppermute | solution.py:343
  88.1 1.1 %collective-permute-done.10.refs_2_ = bf16[16,2176]{1,0:T(8,128)(2,1)S(1)} collective-permute-done((bf16[16,2176]{1,0:T(8,128)(2,1)}, bf16[16,2176]{1,0:T(8,128)(2,1)S(1)}, u32[]{:S(2)}, u32[]{:S(2)}) %collective-permute-start.10) | collective-permute-done | bytes 69664 | tf_op jit(solution)/shard_map/ppermute | solution.py:343
  89.2 1.9 %collective-permute-done.11.refs_3_ = bf16[16,2176]{1,0:T(8,128)(2,1)S(1)} collective-permute-done((bf16[16,2176]{1,0:T(8,128)(2,1)}, bf16[16,2176]{1,0:T(8,128)(2,1)S(1)}, u32[]{:S(2)}, u32[]{:S(2)}) %collective-permute-start.11) | collective-permute-done | bytes 69664 | tf_op jit(solution)/shard_map/ppermute | solution.py:343
  91.1 2.2 %collective-permute-done.14.refs_6_ = bf16[16,2176]{1,0:T(8,128)(2,1)S(1)} collective-permute-done((bf16[16,2176]{1,0:T(8,128)(2,1)}, bf16[16,2176]{1,0:T(8,128)(2,1)S(1)}, u32[]{:S(2)}, u32[]{:S(2)}) %collective-permute-start.14) | collective-permute-done | bytes 69664 | tf_op jit(solution)/shard_map/ppermute | solution.py:343
  93.3 2.5 %collective-permute-done.15.refs_7_ = bf16[16,2176]{1,0:T(8,128)(2,1)S(1)} collective-permute-done((bf16[16,2176]{1,0:T(8,128)(2,1)}, bf16[16,2176]{1,0:T(8,128)(2,1)S(1)}, u32[]{:S(2)}, u32[]{:S(2)}) %collective-permute-start.15) | collective-permute-done | bytes 69664 | tf_op jit(solution)/shard_map/ppermute | solution.py:343
  95.8 0.9 copy-done.1
  96.7 1.4 %shard_map.85 = bf16[4,4,4096]{2,1,0:T(4,128)(2,1)} custom-call(bf16[16,2176]{1,0:T(8,128)(2,1)S(1)} %copy-done.1, bf16[16,2176]{1,0:T(8,128)(2,1)S(1)} %collective-permute-done.9.refs_1_, bf16[16,2176]{1,0:T(8,128)(2,1)S(1)} %collective-permute-done.10.refs_2_, bf16[16,2176]{1,0:T(8,128)(2,1)S(1)} %collective-permute-done.11.refs_3_, ...), custom_call_target="tpu_custom_call" | custom-call | tf_op jit(solution)/shard_map/pallas_call | solution.py:327
  (33 shorter events, 0.6 us)
Async XLA Ops:
  0.0 21.9 %collective-permute-start.7 = (bf16[4,1024,512]{2,1,0:T(8,128)(2,1)}, bf16[4,1024,512]{2,1,0:T(8,128)(2,1)}, u32[]{:S(2)}, u32[]{:S(2)}) collective-permute-start(bf16[4,1024,512]{2,1,0:T(8,128)(2,1)} %refs_16_.1), channel_id=1, source_target_pairs={{0,2},{2,0},{4,6},{6,4},{8,10},{10,8},{12,14},{14,12},{1,3},{3,1},... | collective-permute-start | bytes 12582920 | tf_op jit(solution)/shard_map/ppermute | solution.py:343
  0.5 21.4 %collective-permute-start.8 = (bf16[4,1024,512]{2,1,0:T(8,128)(2,1)}, bf16[4,1024,512]{2,1,0:T(8,128)(2,1)}, u32[]{:S(2)}, u32[]{:S(2)}) collective-permute-start(bf16[4,1024,512]{2,1,0:T(8,128)(2,1)} %refs_17_.1), channel_id=1, source_target_pairs={{0,2},{2,0},{4,6},{6,4},{8,10},{10,8},{12,14},{14,12},{1,3},{3,1},... | collective-permute-start | bytes 12582920 | tf_op jit(solution)/shard_map/ppermute | solution.py:343
  2.1 7.5 %collective-permute-start.3 = (bf16[16,2176]{1,0:T(8,128)(2,1)}, bf16[16,2176]{1,0:T(8,128)(2,1)S(1)}, u32[]{:S(2)}, u32[]{:S(2)}) collective-permute-start(bf16[16,2176]{1,0:T(8,128)(2,1)} %get-tuple-element.18.refs_0_.refs_8_), channel_id=1, source_target_pairs={{0,8},{2,10},{4,12},{6,14},{8,0},{10,2},{12,4},{14,6},{1,9},{3,11}... | collective-permute-start | bytes 208904 | tf_op jit(solution)/shard_map/ppermute | solution.py:343
  6.1 8.7 %collective-permute-start.1 = (bf16[16,2176]{1,0:T(8,128)(2,1)}, bf16[16,2176]{1,0:T(8,128)(2,1)S(1)}, u32[]{:S(2)}, u32[]{:S(2)}) collective-permute-start(bf16[16,2176]{1,0:T(8,128)(2,1)} %get-tuple-element.18.refs_0_.refs_8_), channel_id=1, source_target_pairs={{0,4},{2,6},{4,0},{6,2},{8,12},{10,14},{12,8},{14,10},{1,5},{3,7},... | collective-permute-start | bytes 208904 | tf_op jit(solution)/shard_map/ppermute | solution.py:343
  7.7 8.5 %collective-permute-start.4 = (bf16[16,2176]{1,0:T(8,128)(2,1)}, bf16[16,2176]{1,0:T(8,128)(2,1)S(1)}, u32[]{:S(2)}, u32[]{:S(2)}) collective-permute-start(bf16[16,2176]{1,0:T(8,128)(2,1)} %get-tuple-element.19.pass_ref), channel_id=1, source_target_pairs={{0,10},{2,8},{4,14},{6,12},{8,2},{10,0},{12,6},{14,4},{1,11},{3,9}... | collective-permute-start | bytes 208904 | tf_op jit(solution)/shard_map/ppermute | solution.py:343
  9.6 12.3 %copy-start.3 = (bf16[16,2176]{1,0:T(8,128)(2,1)}, bf16[16,2176]{1,0:T(8,128)(2,1)S(1)}, u32[]{:S(2)}) copy-start(bf16[16,2176]{1,0:T(8,128)(2,1)S(1)} %collective-permute-done.3.refs_4_.refs_12_) | copy-start | bytes 208900
  9.6 6.6 %collective-permute-start.2 = (bf16[16,2176]{1,0:T(8,128)(2,1)}, bf16[16,2176]{1,0:T(8,128)(2,1)S(1)}, u32[]{:S(2)}, u32[]{:S(2)}) collective-permute-start(bf16[16,2176]{1,0:T(8,128)(2,1)} %get-tuple-element.19.pass_ref), channel_id=1, source_target_pairs={{0,6},{2,4},{4,2},{6,0},{8,14},{10,12},{12,10},{14,8},{1,7},{3,5},... | collective-permute-start | bytes 208904 | tf_op jit(solution)/shard_map/ppermute | solution.py:343
  14.8 7.1 %copy-start.4 = (bf16[16,2176]{1,0:T(8,128)(2,1)}, bf16[16,2176]{1,0:T(8,128)(2,1)S(1)}, u32[]{:S(2)}) copy-start(bf16[16,2176]{1,0:T(8,128)(2,1)S(1)} %collective-permute-done.1.refs_2_.refs_10_) | copy-start | bytes 208900
  14.8 3.5 %collective-permute-start = (bf16[16,2176]{1,0:T(8,128)(2,1)}, bf16[16,2176]{1,0:T(8,128)(2,1)S(1)}, u32[]{:S(2)}, u32[]{:S(2)}) collective-permute-start(bf16[16,2176]{1,0:T(8,128)(2,1)} %get-tuple-element.20), channel_id=1, source_target_pairs={{0,2},{2,0},{4,6},{6,4},{8,10},{10,8},{12,14},{14,12},{1,3},{3,1},... | collective-permute-start | bytes 208904 | tf_op jit(solution)/shard_map/ppermute | solution.py:343
  16.2 5.7 %copy-start.5 = (bf16[16,2176]{1,0:T(8,128)(2,1)}, bf16[16,2176]{1,0:T(8,128)(2,1)S(1)}, u32[]{:S(2)}) copy-start(bf16[16,2176]{1,0:T(8,128)(2,1)S(1)} %collective-permute-done.4.refs_5_.refs_13_) | copy-start | bytes 208900
  16.2 4.9 %collective-permute-start.5 = (bf16[16,2176]{1,0:T(8,128)(2,1)S(1)}, bf16[16,2176]{1,0:T(8,128)(2,1)S(1)}, u32[]{:S(2)}, u32[]{:S(2)}) collective-permute-start(bf16[16,2176]{1,0:T(8,128)(2,1)S(1)} %collective-permute-done.3.refs_4_.refs_12_), channel_id=1, source_target_pairs={{0,4},{2,6},{4,0},{6,2},{8,12},{10,14},{12,8},{14,10},{1,5},{3,7},... | collective-permute-start | bytes 208904 | tf_op jit(solution)/shard_map/ppermute | solution.py:343
  16.3 5.6 %copy-start.6 = (bf16[16,2176]{1,0:T(8,128)(2,1)}, bf16[16,2176]{1,0:T(8,128)(2,1)S(1)}, u32[]{:S(2)}) copy-start(bf16[16,2176]{1,0:T(8,128)(2,1)S(1)} %collective-permute-done.2.refs_3_.refs_11_) | copy-start | bytes 208900
  16.3 5.6 %collective-permute-start.6 = (bf16[16,2176]{1,0:T(8,128)(2,1)S(1)}, bf16[16,2176]{1,0:T(8,128)(2,1)S(1)}, u32[]{:S(2)}, u32[]{:S(2)}) collective-permute-start(bf16[16,2176]{1,0:T(8,128)(2,1)S(1)} %collective-permute-done.4.refs_5_.refs_13_), channel_id=1, source_target_pairs={{0,4},{2,6},{4,0},{6,2},{8,12},{10,14},{12,8},{14,10},{1,5},{3,7},... | collective-permute-start | bytes 208904 | tf_op jit(solution)/shard_map/ppermute | solution.py:343
  18.2 3.7 %copy-start.7 = (bf16[16,2176]{1,0:T(8,128)(2,1)}, bf16[16,2176]{1,0:T(8,128)(2,1)S(1)}, u32[]{:S(2)}) copy-start(bf16[16,2176]{1,0:T(8,128)(2,1)S(1)} %collective-permute-done.refs_1_.refs_9_) | copy-start | bytes 208900
  22.5 73.3 %copy-start = (f32[16,4096]{1,0:T(8,128)S(1)}, f32[16,4096]{1,0:T(8,128)}, u32[]{:S(2)}) copy-start(f32[16,4096]{1,0:T(8,128)} %get-tuple-element.30.refs_8_) | copy-start | bytes 786436
  22.5 73.3 %copy-start.2 = (f32[2,16,128]{2,1,0:T(8,128)S(1)}, f32[2,16,128]{2,1,0:T(8,128)}, u32[]{:S(2)}) copy-start(f32[2,16,128]{2,1,0:T(8,128)} %get-tuple-element.21.refs_20_.refs_9_) | copy-start | bytes 49156
  79.6 5.9 %collective-permute-start.9 = (bf16[16,2176]{1,0:T(8,128)(2,1)}, bf16[16,2176]{1,0:T(8,128)(2,1)S(1)}, u32[]{:S(2)}, u32[]{:S(2)}) collective-permute-start(bf16[16,2176]{1,0:T(8,128)(2,1)} %get-tuple-element.23), channel_id=1, source_target_pairs={{0,4},{2,6},{4,0},{6,2},{8,12},{10,14},{12,8},{14,10},{1,5},{3,7},... | collective-permute-start | bytes 208904 | tf_op jit(solution)/shard_map/ppermute | solution.py:343
  80.3 8.9 %collective-permute-start.10 = (bf16[16,2176]{1,0:T(8,128)(2,1)}, bf16[16,2176]{1,0:T(8,128)(2,1)S(1)}, u32[]{:S(2)}, u32[]{:S(2)}) collective-permute-start(bf16[16,2176]{1,0:T(8,128)(2,1)} %get-tuple-element.24), channel_id=1, source_target_pairs={{0,8},{2,10},{4,12},{6,14},{8,0},{10,2},{12,4},{14,6},{1,9},{3,11}... | collective-permute-start | bytes 208904 | tf_op jit(solution)/shard_map/ppermute | solution.py:343
  84.0 7.2 %collective-permute-start.11 = (bf16[16,2176]{1,0:T(8,128)(2,1)}, bf16[16,2176]{1,0:T(8,128)(2,1)S(1)}, u32[]{:S(2)}, u32[]{:S(2)}) collective-permute-start(bf16[16,2176]{1,0:T(8,128)(2,1)} %get-tuple-element.25), channel_id=1, source_target_pairs={{0,12},{2,14},{4,8},{6,10},{8,4},{10,6},{12,0},{14,2},{1,13},{3,15... | collective-permute-start | bytes 208904 | tf_op jit(solution)/shard_map/ppermute | solution.py:343
  84.7 6.4 %collective-permute-start.12 = (bf16[16,2176]{1,0:T(8,128)(2,1)}, bf16[16,2176]{1,0:T(8,128)(2,1)S(1)}, u32[]{:S(2)}, u32[]{:S(2)}) collective-permute-start(bf16[16,2176]{1,0:T(8,128)(2,1)} %get-tuple-element.26), channel_id=1, source_target_pairs={{0,2},{2,0},{4,6},{6,4},{8,10},{10,8},{12,14},{14,12},{1,3},{3,1},... | collective-permute-start | bytes 208904 | tf_op jit(solution)/shard_map/ppermute | solution.py:343
  84.7 6.4 %collective-permute-start.13 = (bf16[16,2176]{1,0:T(8,128)(2,1)}, bf16[16,2176]{1,0:T(8,128)(2,1)S(1)}, u32[]{:S(2)}, u32[]{:S(2)}) collective-permute-start(bf16[16,2176]{1,0:T(8,128)(2,1)} %get-tuple-element.27), channel_id=1, source_target_pairs={{0,6},{2,4},{4,2},{6,0},{8,14},{10,12},{12,10},{14,8},{1,7},{3,5},... | collective-permute-start | bytes 208904 | tf_op jit(solution)/shard_map/ppermute | solution.py:343
  85.4 7.9 %collective-permute-start.14 = (bf16[16,2176]{1,0:T(8,128)(2,1)}, bf16[16,2176]{1,0:T(8,128)(2,1)S(1)}, u32[]{:S(2)}, u32[]{:S(2)}) collective-permute-start(bf16[16,2176]{1,0:T(8,128)(2,1)} %get-tuple-element.28), channel_id=1, source_target_pairs={{0,10},{2,8},{4,14},{6,12},{8,2},{10,0},{12,6},{14,4},{1,11},{3,9}... | collective-permute-start | bytes 208904 | tf_op jit(solution)/shard_map/ppermute | solution.py:343
  89.2 6.6 %collective-permute-start.15 = (bf16[16,2176]{1,0:T(8,128)(2,1)}, bf16[16,2176]{1,0:T(8,128)(2,1)S(1)}, u32[]{:S(2)}, u32[]{:S(2)}) collective-permute-start(bf16[16,2176]{1,0:T(8,128)(2,1)} %get-tuple-element.29), channel_id=1, source_target_pairs={{0,14},{2,12},{4,10},{6,8},{8,6},{10,4},{12,2},{14,0},{1,15},{3,13... | collective-permute-start | bytes 208904 | tf_op jit(solution)/shard_map/ppermute | solution.py:343
  95.8 0.9 copy-start.1
  (2 other events, 1.4 us)
